TPU v7x, 128 devices: a whole 4x4x4 slice. The times are simulated.
128 devices in a mesh: fsdp: 16 (over z_lo, y, core), ctx: 8 (over z_hi, x).
Axes of the slice: x: 4, y: 4, z: 4 (z_hi: 2, z_lo: 2; z = z_hi * 2 + z_lo), core: 2. Of those that a mesh axis runs over, the one named last changes fastest.
Arguments:
- inputs: bfloat16 [16, 1536, 1024], P('fsdp', 'ctx'), may hold values from -6 to 6
- doc_ids: int32 [16, 1536], P('fsdp', 'ctx'), may hold values from 0 to 2, never falling along the last dimension, each value on 1 to 1152 neighbouring positions
- query_proj: bfloat16 [1024, 2048], P('fsdp'), may hold values from -0.1875 to 0.1875
- key_projection: bfloat16 [1024, 1024], P('fsdp'), may hold values from -0.1875 to 0.1875
- value_projection: bfloat16 [1024, 1024], P('fsdp'), may hold values from -0.1875 to 0.1875
- output_proj: bfloat16 [2048, 1024], P('fsdp'), may hold values from -1 to 1
- gate_proj: bfloat16 [1024, 3072], P('fsdp'), may hold values from -0.1875 to 0.1875
- up_proj: bfloat16 [1024, 3072], P('fsdp'), may hold values from -0.1875 to 0.1875
- down_proj: bfloat16 [3072, 1024], P('fsdp'), may hold values from -0.109375 to 0.109375
- attn_gain: bfloat16 [1024], P('fsdp'), may hold values from 0.25 to 1.75
- mlp_gain: bfloat16 [1024], P('fsdp'), may hold values from 0.25 to 1.75
- query_norm_gain: bfloat16 [128], P('fsdp'), may hold values from 0.25 to 1.75
- key_gain: bfloat16 [128], P('fsdp'), may hold values from 0.25 to 1.75
- out_grad: bfloat16 [16, 1536, 1024], P('fsdp', 'ctx'), may hold values from -6 to 6
Outputs:
- outputs: bfloat16 [16, 1536, 1024], P('fsdp', 'ctx')
- input_grad: float32 [16, 1536, 1024], P('fsdp', 'ctx')
- query_proj_grad: float32 [1024, 2048], P('fsdp')
- key_proj_grad: float32 [1024, 1024], P('fsdp')
- value_proj_grad: float32 [1024, 1024], P('fsdp')
- output_proj_grad: float32 [2048, 1024], P('fsdp')
- gate_proj_grad: float32 [1024, 3072], P('fsdp')
- up_proj_grad: float32 [1024, 3072], P('fsdp')
- down_proj_grad: float32 [3072, 1024], P('fsdp')
- attn_gain_grad: float32 [1024], P('fsdp')
- mlp_gain_grad: float32 [1024], P('fsdp')
- query_gain_grad: float32 [128], P('fsdp')
- key_gain_grad: float32 [128], P('fsdp')
Inputs may be any that keep to these rules, and one draw needn't show every extreme that they name: Each row of doc_ids numbers its documents 0 to 2 in order, never falling; each document has 1 to 1152 tokens, and one has exactly 1152.
All inputs are finite; a program needn't handle non-finite values.
Results may differ from a plain program's by a relative error of at most 0.025.
Values may be sent and summed in bfloat16 or wider, within the bound.
A program may use at most 192 MiB of HBM per device.

v0:
```python
import math

import jax
import jax.numpy as jnp
from jax import lax
from jax.sharding import PartitionSpec as P

HEAD_SIZE = 128
DOCS = 3


EPSILON = 1e-06
THETA = 1000000.0
NEGATIVE = -1e30


def sent_together(arrays, axis, dim, along):
    ends, at = ([], 0)
    for a in arrays[:-1]:
        at += a.shape[along]
        ends.append(at)
    both = jnp.concatenate(arrays, axis=along)
    return tuple(jnp.split(lax.all_gather(both, axis, axis=dim, tiled=True), ends, axis=along))


def in_order(tiles, dim):
    tiles = jnp.moveaxis(tiles, 0, dim)
    lengths = tiles.shape
    return tiles.reshape(*lengths[:dim], lengths[dim] * lengths[dim + 1], *lengths[dim + 2 :])


def from_everyone(x, axis):
    length = lax.axis_size(axis)
    return lax.all_to_all(jnp.broadcast_to(x[None], (length, *x.shape)), axis, 0, 0, tiled=True)


def gather_directly(x, axis, dim):
    return in_order(from_everyone(x, axis), dim)


def side_by_side(arrays, axis, dim, along):
    widths = [a.shape[along] for a in arrays]
    both = jnp.concatenate(arrays, axis=along)
    result = lax.psum_scatter(both, axis, scatter_dimension=dim, tiled=True)
    return tuple(jnp.split(result, [sum(widths[:k]) for k in range(1, len(widths))], axis=along))


def as_sent(x):
    return jax.tree.map(lambda a: a.astype(jnp.bfloat16) if a.dtype == jnp.float32 else a, x)


def root_mean_norm(value_rows, scaling):
    return (
        value_rows
        * lax.rsqrt(jnp.mean(value_rows * value_rows, axis=-1, keepdims=True) + EPSILON)
        * scaling
    )


def rotate_halves(value_rows, cosine_table, sine_table):
    middle = value_rows.shape[-1] // 2
    former = value_rows[..., :middle]
    latter = value_rows[..., middle:]
    return jnp.concatenate(
        [former * cosine_table - latter * sine_table, latter * cosine_table + former * sine_table],
        axis=-1,
    )


def doc_positions(row_document_index):
    position_table = jnp.arange(row_document_index.shape[0], dtype=jnp.int32)
    numbers = jnp.arange(DOCS, dtype=jnp.int32)
    starts = jnp.sum((row_document_index[:, None] < numbers[None, :]).astype(jnp.int32), axis=0)
    own_start = jnp.sum(
        jnp.where(row_document_index[:, None] == numbers[None, :], starts[None, :], 0), axis=1
    )
    return position_table - own_start


def rope_tables(positions):
    freqs = THETA ** (-jnp.arange(HEAD_SIZE // 2, dtype=jnp.float32) * 2.0 / HEAD_SIZE)
    angles = positions.astype(jnp.float32)[:, None] * freqs[None, :]
    return (jnp.cos(angles)[:, None, :], jnp.sin(angles)[:, None, :])


def first_dot(left, right):
    return lax.dot_general(
        left, right, (((0,), (0,)), ((), ())), preferred_element_type=jnp.float32
    )


def second_dot(left, right):
    return lax.dot_general(
        left, right, (((1,), (1,)), ((), ())), preferred_element_type=jnp.float32
    )


def plain_dot(left, right):
    return jnp.dot(left, right, preferred_element_type=jnp.float32)


def silu_product(gate, upward):
    return jax.nn.silu(gate) * upward


def unchanged(current):
    return current


def body(
    inputs,
    doc_ids,
    query_proj,
    key_projection,
    value_projection,
    output_proj,
    gate_proj,
    up_proj,
    down_proj,
    attn_gain,
    mlp_gain,
    query_norm_gain,
    key_gain,
    out_grad,
):
    shards = (
        query_proj,
        key_projection,
        value_projection,
        output_proj,
        gate_proj,
        up_proj,
        down_proj,
        attn_gain,
        mlp_gain,
        query_norm_gain,
        key_gain,
    )
    gathered = (
        *sent_together((shards[0], shards[1], shards[2]), "fsdp", 0, 1),
        lax.all_gather(shards[3], "fsdp", axis=0, tiled=True),
        *sent_together((shards[4], shards[5]), "fsdp", 0, 1),
        lax.all_gather(shards[6], "fsdp", axis=0, tiled=True),
        lax.all_gather(shards[7], "fsdp", axis=0, tiled=True),
        lax.all_gather(shards[8], "fsdp", axis=0, tiled=True),
        lax.all_gather(shards[9], "fsdp", axis=0, tiled=True),
        lax.all_gather(shards[10], "fsdp", axis=0, tiled=True),
    )
    full_query, full_key, full_value, full_output, full_gate, full_up, full_down = gathered[:7]
    attn_scale, mlp_scale, query_scale, key_scale = tuple(
        (item.astype(jnp.float32) for item in gathered[7:])
    )
    row_document_index = gather_directly(doc_ids, "ctx", 1)[0]
    rows_own = inputs.shape[1]
    length_total = row_document_index.shape[0]
    offset = lax.axis_index("ctx") * rows_own
    positions = lax.dynamic_slice_in_dim(doc_positions(row_document_index), offset, rows_own)
    own_ids = lax.dynamic_slice_in_dim(row_document_index, offset, rows_own)
    own_places = offset + jnp.arange(rows_own, dtype=jnp.int32)
    cosine_table, sine_table = rope_tables(positions)
    heads_kv = full_key.shape[1] // HEAD_SIZE
    heads_q = full_query.shape[1] // HEAD_SIZE
    group = heads_q // heads_kv
    factor = 1.0 / math.sqrt(HEAD_SIZE)

    def allowed_at(begin_row, number):
        key_places = begin_row + jnp.arange(number, dtype=jnp.int32)
        key_ids = lax.dynamic_slice_in_dim(row_document_index, begin_row, number)
        return (own_ids[:, None] == key_ids[None, :]) & (key_places[None, :] <= own_places[:, None])

    residual = inputs[0].astype(jnp.float32)
    normed_f, norm_pull = jax.vjp(root_mean_norm, residual, attn_scale)
    normalized_rows = normed_f.astype(jnp.bfloat16)
    query_linear = plain_dot(normalized_rows, full_query)
    key_linear = plain_dot(normalized_rows, full_key)
    value_rows = (
        plain_dot(normalized_rows, full_value)
        .astype(jnp.bfloat16)
        .reshape(rows_own, heads_kv, HEAD_SIZE)
    )

    def prepare(query_in, key_in, query_weight, key_weight):
        query_out = rotate_halves(
            root_mean_norm(query_in.reshape(rows_own, heads_q, HEAD_SIZE), query_weight),
            cosine_table,
            sine_table,
        )
        key_out = rotate_halves(
            root_mean_norm(key_in.reshape(rows_own, heads_kv, HEAD_SIZE), key_weight),
            cosine_table,
            sine_table,
        )
        return (query_out, key_out)

    (query_rot, key_rot), prep_pull = jax.vjp(
        prepare, query_linear, key_linear, query_scale, key_scale
    )
    query_rows = query_rot.astype(jnp.bfloat16).reshape(rows_own, heads_kv, group, HEAD_SIZE)
    keys = key_rot.astype(jnp.bfloat16)
    start_state = (
        jnp.full((rows_own, heads_kv, group), NEGATIVE, jnp.float32),
        jnp.zeros((rows_own, heads_kv, group), jnp.float32),
        jnp.zeros((rows_own, heads_kv, group, HEAD_SIZE), jnp.float32),
    )
    key_block, value_block = sent_together((keys, value_rows), "ctx", 0, 1)
    number = key_block.shape[0]
    width = min(number, rows_own)

    def one_block(index, inner_state):
        local = index * width
        keys_here = lax.dynamic_slice_in_dim(key_block, local, width)
        values_here = lax.dynamic_slice_in_dim(value_block, local, width)
        allowed = allowed_at(local, width)

        def one_compute(current):
            running_max, weight_sum, accumulated = current
            scores = (
                jnp.einsum(
                    "tgrd,sgd->tgrs", query_rows, keys_here, preferred_element_type=jnp.float32
                )
                * factor
            )
            wide = allowed[:, None, None, :]
            scores = jnp.where(wide, scores, NEGATIVE)
            new_max = jnp.maximum(running_max, jnp.max(scores, axis=-1))
            weights = jnp.where(wide, jnp.exp(scores - new_max[..., None]), 0.0)
            fading = jnp.exp(running_max - new_max)
            weight_sum = weight_sum * fading + jnp.sum(weights, axis=-1)
            accumulated = accumulated * fading[..., None] + jnp.einsum(
                "tgrs,sgd->tgrd",
                weights.astype(jnp.bfloat16),
                values_here,
                preferred_element_type=jnp.float32,
            )
            return (new_max, weight_sum, accumulated)

        return lax.cond(jnp.any(allowed), one_compute, unchanged, inner_state)

    running_max, weight_sum, accumulated = lax.fori_loop(0, number // width, one_block, start_state)
    heads_f = accumulated / weight_sum[..., None]
    log_sum = running_max + jnp.log(weight_sum)
    heads = heads_f.reshape(rows_own, heads_q * HEAD_SIZE).astype(jnp.bfloat16)
    hidden = residual + plain_dot(heads, full_output)
    mixed_f, mix_pull = jax.vjp(root_mean_norm, hidden, mlp_scale)
    mixed = mixed_f.astype(jnp.bfloat16)
    gate = plain_dot(mixed, full_gate)
    upward = plain_dot(mixed, full_up)
    active_f, active_pull = jax.vjp(silu_product, gate, upward)
    active = active_f.astype(jnp.bfloat16)
    outputs = (hidden + plain_dot(active, full_down)).astype(jnp.bfloat16)[None]
    again = (
        *sent_together((query_proj, key_projection, value_projection), "fsdp", 0, 1),
        lax.all_gather(output_proj, "fsdp", axis=0, tiled=True),
        *sent_together((gate_proj, up_proj), "fsdp", 0, 1),
        lax.all_gather(down_proj, "fsdp", axis=0, tiled=True),
    )
    full_query, full_key, full_value, full_output, full_gate, full_up, full_down = again
    grad_rows = out_grad[0]
    d_down = first_dot(active, grad_rows)
    d_active = second_dot(grad_rows, full_down)
    d_gate, d_upward = active_pull(d_active)
    gate_low = d_gate.astype(jnp.bfloat16)
    up_low = d_upward.astype(jnp.bfloat16)
    d_gate_w = first_dot(mixed, gate_low)
    d_up_w = first_dot(mixed, up_low)
    d_mixed = second_dot(gate_low, full_gate) + second_dot(up_low, full_up)
    d_hidden_norm, d_mlp_scale = mix_pull(d_mixed)
    d_hidden = grad_rows.astype(jnp.float32) + d_hidden_norm
    mlp_terms = (d_gate_w, d_up_w, d_down, d_mlp_scale)
    mlp_part = (
        *tuple(
            (
                part.astype(jnp.float32)
                for part in side_by_side(
                    (mlp_terms[0].astype(jnp.bfloat16), mlp_terms[1].astype(jnp.bfloat16)),
                    "fsdp",
                    0,
                    1,
                )
            )
        ),
        lax.psum_scatter(
            mlp_terms[2].astype(jnp.bfloat16), "fsdp", scatter_dimension=0, tiled=True
        ).astype(jnp.float32),
        lax.psum_scatter(
            mlp_terms[3].astype(jnp.bfloat16), "fsdp", scatter_dimension=0, tiled=True
        ).astype(jnp.float32),
    )
    hidden_low = d_hidden.astype(jnp.bfloat16)
    d_output_w = first_dot(heads, hidden_low)
    d_heads = (
        second_dot(hidden_low, full_output)
        .astype(jnp.bfloat16)
        .reshape(rows_own, heads_kv, group, HEAD_SIZE)
    )
    delta = jnp.sum(d_heads.astype(jnp.float32) * heads_f, axis=-1)
    keys_all, values_all = sent_together((keys, value_rows), "ctx", 0, 1)

    def back_block(index, carry_state):
        begin_row = index * rows_own
        keys_here = lax.dynamic_slice_in_dim(keys_all, begin_row, rows_own)
        values_here = lax.dynamic_slice_in_dim(values_all, begin_row, rows_own)
        allowed = allowed_at(begin_row, rows_own)

        def back_compute(current):
            d_query, d_keys, d_values = current
            scores = (
                jnp.einsum(
                    "tgrd,sgd->tgrs", query_rows, keys_here, preferred_element_type=jnp.float32
                )
                * factor
            )
            wide = allowed[:, None, None, :]
            probs = jnp.where(wide, jnp.exp(scores - log_sum[..., None]), 0.0)
            d_probs = jnp.einsum(
                "tgrd,sgd->tgrs", d_heads, values_here, preferred_element_type=jnp.float32
            )
            d_scores = (probs * (d_probs - delta[..., None])).astype(jnp.bfloat16)
            d_query = (
                d_query
                + jnp.einsum(
                    "tgrs,sgd->tgrd", d_scores, keys_here, preferred_element_type=jnp.float32
                )
                * factor
            )
            key_part = (
                jnp.einsum(
                    "tgrs,tgrd->sgd", d_scores, query_rows, preferred_element_type=jnp.float32
                )
                * factor
            )
            value_part = jnp.einsum(
                "tgrs,tgrd->sgd",
                probs.astype(jnp.bfloat16),
                d_heads,
                preferred_element_type=jnp.float32,
            )
            d_keys = lax.dynamic_update_slice_in_dim(
                d_keys,
                lax.dynamic_slice_in_dim(d_keys, begin_row, rows_own) + key_part,
                begin_row,
                0,
            )
            d_values = lax.dynamic_update_slice_in_dim(
                d_values,
                lax.dynamic_slice_in_dim(d_values, begin_row, rows_own) + value_part,
                begin_row,
                0,
            )
            return (d_query, d_keys, d_values)

        return lax.cond(jnp.any(allowed), back_compute, unchanged, carry_state)

    zeros_kv = jnp.zeros((length_total, heads_kv, HEAD_SIZE), jnp.float32)
    zeros_query = jnp.zeros((rows_own, heads_kv, group, HEAD_SIZE), jnp.float32)
    d_query, d_keys, d_values = lax.fori_loop(
        0, length_total // rows_own, back_block, (zeros_query, zeros_kv, zeros_kv)
    )
    key_sum, value_sum = tuple(
        (
            part.astype(jnp.float32)
            for part in side_by_side(
                (d_keys.astype(jnp.bfloat16), d_values.astype(jnp.bfloat16)), "ctx", 0, 1
            )
        )
    )
    d_query_lin, d_key_lin, d_query_scale, d_key_scale = prep_pull(
        (d_query.reshape(rows_own, heads_q, HEAD_SIZE), key_sum)
    )
    query_low = d_query_lin.astype(jnp.bfloat16)
    key_low = d_key_lin.astype(jnp.bfloat16)
    value_low = value_sum.reshape(rows_own, heads_kv * HEAD_SIZE).astype(jnp.bfloat16)
    d_query_w = first_dot(normalized_rows, query_low)
    d_key_w = first_dot(normalized_rows, key_low)
    d_value_w = first_dot(normalized_rows, value_low)
    d_normed = (
        second_dot(query_low, full_query)
        + second_dot(key_low, full_key)
        + second_dot(value_low, full_value)
    )
    d_residual, d_attn_scale = norm_pull(d_normed)
    input_grad = (d_hidden + d_residual)[None]
    attn_terms = (
        d_query_w,
        d_key_w,
        d_value_w,
        d_output_w,
        d_attn_scale,
        d_query_scale,
        d_key_scale,
    )
    attn_part = (
        *tuple(
            (
                part.astype(jnp.float32)
                for part in side_by_side(
                    (
                        attn_terms[0].astype(jnp.bfloat16),
                        attn_terms[1].astype(jnp.bfloat16),
                        attn_terms[2].astype(jnp.bfloat16),
                    ),
                    "fsdp",
                    0,
                    1,
                )
            )
        ),
        lax.psum_scatter(
            attn_terms[3].astype(jnp.bfloat16), "fsdp", scatter_dimension=0, tiled=True
        ).astype(jnp.float32),
        lax.psum_scatter(
            attn_terms[4].astype(jnp.bfloat16), "fsdp", scatter_dimension=0, tiled=True
        ).astype(jnp.float32),
        lax.psum_scatter(
            attn_terms[5].astype(jnp.bfloat16), "fsdp", scatter_dimension=0, tiled=True
        ).astype(jnp.float32),
        lax.psum_scatter(
            attn_terms[6].astype(jnp.bfloat16), "fsdp", scatter_dimension=0, tiled=True
        ).astype(jnp.float32),
    )
    ordered = (
        tuple(attn_part[:4])
        + tuple(mlp_part[:3])
        + (attn_part[4], mlp_part[3], attn_part[5], attn_part[6])
    )
    summed = jax.tree.map(lambda part: part.astype(jnp.float32), lax.psum(as_sent(ordered), "ctx"))
    return (outputs, input_grad) + tuple(summed)


def solution(mesh):
    in_specs = (
        P("fsdp", "ctx", None),
        P("fsdp", "ctx"),
        P("fsdp", None),
        P("fsdp", None),
        P("fsdp", None),
        P("fsdp", None),
        P("fsdp", None),
        P("fsdp", None),
        P("fsdp", None),
        P("fsdp"),
        P("fsdp"),
        P("fsdp"),
        P("fsdp"),
        P("fsdp", "ctx", None),
    )
    out_specs = (
        P("fsdp", "ctx", None),
        P("fsdp", "ctx", None),
        P("fsdp", None),
        P("fsdp", None),
        P("fsdp", None),
        P("fsdp", None),
        P("fsdp", None),
        P("fsdp", None),
        P("fsdp", None),
        P("fsdp"),
        P("fsdp"),
        P("fsdp"),
        P("fsdp"),
    )
    return jax.shard_map(body, mesh=mesh, in_specs=in_specs, out_specs=out_specs, check_vma=False)
```

profile of v0, /device:TPU:1, one launch (start us, length us, event | category | flops | bytes accessed | tf_op | source)
XLA Modules:
  0.0 984.9 jit_solution(89749412626142603)
XLA Ops:
  11.3 8.2 all-to-all-start
  24.2 28.7 %all-reduce.13 = (bf16[1024]{0:T(1024)(128)(2,1)S(1)}, bf16[128]{0:T(256)(128)(2,1)S(1)}, bf16[128]{0:T(256)(128)(2,1)S(1)}, bf16[1024]{0:T(1024)(128)(2,1)S(1)}) all-reduce(bf16[1024]{0:T(1024)(128)(2,1)S(1)} %dynamic-update-slice, bf16[128]{0:T(256)(128)(2,1)S(1)} %dynamic-update-slice.1, ...), channel_id=1, replica_groups=mesh['fsdp'=16,'ctx'=8] {'fsdp'}, use_global_device_ids=true, to_apply=%add.4 | all-reduce | flops 2304 | bytes 9216
  53.7 13.2 %all-gather.6.cloned.1.call-done = bf16[1024,4096]{1,0:T(8,128)(2,1)} async-done(((bf16[64,4096]{1,0:T(8,128)(2,1)}), bf16[1024,4096]{1,0:T(8,128)(2,1)}) %all-gather.6.cloned.1.call-update) | async-done | bytes 8388624 | tf_op jit(solution)/shard_map/all_gather | solution.py:23
  81.4 30.4 %all-gather.14.cloned.1.call-done = bf16[3072,1024]{1,0:T(8,128)(2,1)} async-done(((bf16[192,1024]{1,0:T(8,128)(2,1)}), bf16[3072,1024]{1,0:T(8,128)(2,1)}) %all-gather.14.cloned.1.call-update) | async-done | bytes 6291472 | tf_op jit(solution)/shard_map/all_gather | solution.py:143
  111.8 6.4 fusion.129
  118.1 4.8 slice_bitcast_fusion
  122.9 6.5 copy.65
  129.4 3.9 multiply_reduce_fusion.3
  135.6 68.6 %all-gather.8.cloned.1.call-done = bf16[1536,16,128]{2,0,1:T(8,128)(2,1)} async-done(((bf16[192,16,128]{2,0,1:T(8,128)(2,1)}), bf16[1536,16,128]{2,0,1:T(8,128)(2,1)}) %all-gather.8.cloned.1.call-update) | async-done | bytes 6291472 | tf_op jit(solution)/shard_map/all_gather | solution.py:23
  204.2 6.1 fusion.158
  210.5 17.5 %while.36 = (s32[]{:T(128)}, f32[192,8,2]{0,2,1:T(2,128)S(1)}, f32[192,8,2]{0,2,1:T(2,128)S(1)}, f32[192,8,2,128]{3,0,2,1:T(8,128)S(1)}, s32[192]{0:T(256)S(1)},...) while((s32[]{:T(128)}, f32[192,8,2]{0,2,1:T(2,128)S(1)}, ...), condition=%wide.region_11.12_spmd.clone, body=%wide.region_5.11_spmd.clone.sunk | while | flops 310598016 | bytes 12148037 | solution.py:239
  212.0 5.1 conditional.6
  232.9 8.8 all-gather.10.cloned.1.call-done
  246.1 69.8 %all-gather.12.cloned.1.call-done = bf16[1024,6144]{1,0:T(8,128)(2,1)} async-done(((bf16[64,6144]{1,0:T(8,128)(2,1)}), bf16[1024,6144]{1,0:T(8,128)(2,1)}) %all-gather.12.cloned.1.call-update) | async-done | bytes 12582928 | tf_op jit(solution)/shard_map/all_gather | solution.py:23
  315.9 4.3 fusion.64
  320.3 6.6 fusion.74
  335.5 3.4 reshape.281
  352.3 37.2 %while.37 = (s32[]{:T(128)}, f32[192,8,2,128]{3,0,2,1:T(8,128)}, f32[1536,8,128]{2,0,1:T(8,128)}, f32[1536,8,128]{2,0,1:T(8,128)}, s32[192]{0:T(256)S(1)}, /*ind...) while((s32[]{:T(128)}, f32[192,8,2,128]{3,0,2,1:T(8,128)}, ...), condition=%wide.region_19.20_spmd.clone, body=%wide.region_15.19_spmd.clone.sunk | while | flops 762397056 | bytes 43851912 | solution.py:356
  355.3 13.4 %conditional.7 = ((f32[192,8,2,128]{3,0,2,1:T(8,128)}, f32[1536,8,128]{2,0,1:T(8,128)}, f32[1536,8,128]{2,0,1:T(8,128)})) conditional(s32[]{:T(128)} %convert_element_type.411, (f32[192,8,2,128]{3,0,2,1:T(8,128)}, f32[1536,8,128]{2,0,1:T(8,128)}, f32[1536,8,128]{2,0,1:T(8,128)}) %tuple.135, (pred[192,192]{0,1:T(8,128)(4,1)}, ...), branch_computations={%region_17.17_spmd, %region_18.18_spmd} | conditional | flops 762249216 | bytes 43808556 | solution.py:352
  403.8 9.3 pad_maximum_fusion
  424.5 153.1 %reduce-scatter.6.cloned.1.call-done = bf16[192,16,128]{2,0,1:T(8,128)(2,1)} async-done(((bf16[1536,16,128]{2,0,1:T(8,128)(2,1)}), bf16[192,16,128]{2,0,1:T(8,128)(2,1)}) %reduce-scatter.6.cloned.1.call-update) | async-done | bytes 786448 | tf_op jit(solution)/shard_map/reduce_scatter | solution.py:44
  584.2 3.9 pad_maximum_fusion.1
  594.1 4.5 convolution_convert_fusion
  600.2 58.2 %reduce-scatter.12.cloned.1.call-done = bf16[64,6144]{1,0:T(8,128)(2,1)} async-done(((bf16[1024,6144]{1,0:T(8,128)(2,1)}), bf16[64,6144]{1,0:T(8,128)(2,1)}) %reduce-scatter.12.cloned.1.call-update) | async-done | bytes 786448 | tf_op jit(solution)/shard_map/reduce_scatter | solution.py:44
  660.5 73.6 %reduce-scatter.8.cloned.1.call-done = bf16[64,4096]{1,0:T(8,128)(2,1)} async-done(((bf16[1024,4096]{1,0:T(8,128)(2,1)}), bf16[64,4096]{1,0:T(8,128)(2,1)}) %reduce-scatter.8.cloned.1.call-update) | async-done | bytes 524304 | tf_op jit(solution)/shard_map/reduce_scatter | solution.py:44
  737.5 64.4 %reduce-scatter.10.cloned.1.call-done = bf16[128,1024]{1,0:T(8,128)(2,1)} async-done(((bf16[2048,1024]{1,0:T(8,128)(2,1)}), bf16[128,1024]{1,0:T(8,128)(2,1)}) %reduce-scatter.10.cloned.1.call-update) | async-done | bytes 262160 | tf_op jit(solution)/shard_map/reduce_scatter | solution.py:408
  801.9 71.6 %reduce-scatter.14.cloned.1.call-done = bf16[192,1024]{1,0:T(8,128)(2,1)} async-done(((bf16[3072,1024]{1,0:T(8,128)(2,1)}), bf16[192,1024]{1,0:T(8,128)(2,1)}) %reduce-scatter.14.cloned.1.call-update) | async-done | bytes 393232 | tf_op jit(solution)/shard_map/reduce_scatter | solution.py:282
  873.6 3.9 fusion.70
  877.5 5.1 fusion.99
  884.8 32.7 %all-reduce.12 = (bf16[1024]{0:T(1024)(128)(2,1)S(1)}, bf16[1024]{0:T(1024)(128)(2,1)S(1)}, bf16[128]{0:T(256)(128)(2,1)S(1)}, bf16[128]{0:T(256)(128)(2,1)S(1)}) all-reduce(bf16[1024]{0:T(1024)(128)(2,1)S(1)} %get-tuple-element.710, bf16[1024]{0:T(1024)(128)(2,1)S(1)} %copy-done.76, ...), channel_id=7, replica_groups=mesh['fsdp'=16,'ctx'=8] {'fsdp'}, use_global_device_ids=true, to_apply=%region_36.37.clone | all-reduce | flops 2304 | bytes 9216
  917.8 20.3 %all-reduce.14 = (bf16[64]{0:T(256)(128)(2,1)S(1)}, bf16[64]{0:T(256)(128)(2,1)S(1)}, bf16[8]{0:T(256)(128)(2,1)S(1)}, bf16[8]{0:T(256)(128)(2,1)S(1)}) all-reduce(bf16[64]{0:T(256)(128)(2,1)S(1)} %dynamic-slice.5, bf16[64]{0:T(256)(128)(2,1)S(1)} %dynamic-slice.7, ...), channel_id=1, replica_groups=mesh['fsdp'=16,'ctx'=8] {'ctx'}, use_global_device_ids=true, to_apply=%region_37.38 | all-reduce | flops 144 | bytes 576 | tf_op jit(solution)/shard_map/psum | solution.py:426
  941.3 27.1 %all-reduce.18.cloned.1.call-done = (bf16[64,2048]{1,0:T(8,128)(2,1)}, bf16[64,1024]{1,0:T(8,128)(2,1)}, bf16[64,1024]{1,0:T(8,128)(2,1)}, bf16[128,1024]{1,0:T(...) async-done(((bf16[64,2048]{1,0:T(8,128)(2,1)}, bf16[64,1024]{1,0:T(8,128)(2,1)}, bf16[64,1024]{1,0:T(8,128)(2,1)}, ...) | async-done | bytes 1966096 | tf_op jit(solution)/shard_map/psum | solution.py:426
  (371 shorter events, 158.1 us)
Async XLA Ops:
  7.2 14.1 %copy-start.75 = (u32[128]{0:T(128)S(1)}, u32[128]{0:T(128)}, u32[]{:S(2)}) copy-start(u32[128]{0:T(128)} %constant.178) | copy-start | bytes 1540
  7.2 59.7 %copy-start.6 = (bf16[1,192,1024]{2,1,0:T(8,128)(2,1)S(1)}, bf16[1,192,1024]{2,1,0:T(8,128)(2,1)}, u32[]{:S(2)}) copy-start(bf16[1,192,1024]{2,1,0:T(8,128)(2,1)} %param.22) | copy-start | bytes 1179652
  7.2 16.0 %copy-start.78 = (bf16[8]{0:T(256)(128)(2,1)S(1)}, bf16[8]{0:T(256)(128)(2,1)}, u32[]{:S(2)}) copy-start(bf16[8]{0:T(256)(128)(2,1)} %param.34) | copy-start | bytes 52
  7.2 16.2 %copy-start.79 = (bf16[8]{0:T(256)(128)(2,1)S(1)}, bf16[8]{0:T(256)(128)(2,1)}, u32[]{:S(2)}) copy-start(bf16[8]{0:T(256)(128)(2,1)} %param.33) | copy-start | bytes 52
  7.2 16.5 %copy-start.80 = (bf16[64]{0:T(256)(128)(2,1)S(1)}, bf16[64]{0:T(256)(128)(2,1)}, u32[]{:S(2)}) copy-start(bf16[64]{0:T(256)(128)(2,1)} %param.31) | copy-start | bytes 388
  7.2 16.7 %copy-start.81 = (bf16[64]{0:T(256)(128)(2,1)S(1)}, bf16[64]{0:T(256)(128)(2,1)}, u32[]{:S(2)}) copy-start(bf16[64]{0:T(256)(128)(2,1)} %param.32) | copy-start | bytes 388
  7.2 59.7 %all-gather.6.cloned.1.call-start = ((), (), s32[]{:S(2)}) async-start(), calls=%async_computation.6 | async-start | bytes 8912896 | tf_op jit(solution)/shard_map/all_gather | solution.py:23
  9.3 102.5 %all-gather.14.cloned.1.call-start = ((), (), s32[]{:S(2)}) async-start(), calls=%async_computation.10 | async-start | bytes 6684672 | tf_op jit(solution)/shard_map/all_gather | solution.py:143
  11.3 41.6 %all-to-all-start = ((s32[8,1,192]{2,1,0:T(1,128)}), s32[8,1,192]{2,1,0:T(1,128)S(1)}, u32[]{:S(2)}, u32[]{:S(2)}) async-start(s32[8,1,192]{2,1,0:T(1,128)} %broadcast_in_dim.132), calls=%async_computation | async-start | bytes 16384 | tf_op jit(solution)/shard_map/all_to_all | solution.py:34
  19.5 184.7 %all-gather.8.cloned.1.call-start = ((), (), s32[]{:S(2)}) async-start(), calls=%async_computation.7 | async-start | bytes 7077888 | tf_op jit(solution)/shard_map/all_gather | solution.py:23
  21.2 108.1 %copy-start.56 = (f32[192]{0:T(256)}, f32[192]{0:T(256)S(1)}, u32[]{:S(2)}) copy-start(f32[192]{0:T(256)S(1)} %fusion.149) | copy-start | bytes 2308
  52.8 76.5 %copy-start.45 = (f32[1024]{0:T(1024)}, f32[1024]{0:T(1024)S(1)}, u32[]{:S(2)}) copy-start(f32[1024]{0:T(1024)S(1)} %convert_element_type.231) | copy-start | bytes 12292
  52.9 23.4 %copy-start.70 = (f32[128]{0:T(128)}, f32[128]{0:T(128)S(1)}, u32[]{:S(2)}) copy-start(f32[128]{0:T(128)S(1)} %convert_element_type.234) | copy-start | bytes 1540
  53.7 80.7 %copy-start.23 = (f32[192,64]{1,0:T(8,128)}, f32[192,64]{1,0:T(8,128)S(1)}, u32[]{:S(2)}) copy-start(f32[192,64]{1,0:T(8,128)S(1)} %get-tuple-element.808) | copy-start | bytes 147460
  53.7 80.7 %copy-start.25 = (f32[192,64]{1,0:T(8,128)}, f32[192,64]{1,0:T(8,128)S(1)}, u32[]{:S(2)}) copy-start(f32[192,64]{1,0:T(8,128)S(1)} %get-tuple-element.809) | copy-start | bytes 147460
  77.4 34.4 %copy-start.17 = (bf16[1,192,1024]{2,1,0:T(8,128)(2,1)S(1)}, bf16[1,192,1024]{2,1,0:T(8,128)(2,1)}, u32[]{:S(2)}) copy-start(bf16[1,192,1024]{2,1,0:T(8,128)(2,1)} %param.35) | copy-start | bytes 1179652
  78.5 163.2 %all-gather.10.cloned.1.call-start = ((), (), s32[]{:S(2)}) async-start(), calls=%async_computation.8 | async-start | bytes 4456448 | tf_op jit(solution)/shard_map/all_gather | solution.py:141
  79.1 236.8 %all-gather.12.cloned.1.call-start = ((), (), s32[]{:S(2)}) async-start(), calls=%async_computation.9 | async-start | bytes 13369344 | tf_op jit(solution)/shard_map/all_gather | solution.py:23
  80.1 497.4 %reduce-scatter.6.cloned.1.call-start = ((), (), s32[]{:S(2)}) async-start(), calls=%async_computation.11 | async-start | bytes 7077888 | tf_op jit(solution)/shard_map/reduce_scatter | solution.py:44
  80.7 52.6 %copy-start.72 = (f32[128]{0:T(128)}, f32[128]{0:T(128)S(1)}, u32[]{:S(2)}) copy-start(f32[128]{0:T(128)S(1)} %convert_element_type.239) | copy-start | bytes 1540
  133.3 77.0 %copy-start.50 = (f32[192,16]{0,1:T(8,128)}, f32[192,16]{0,1:T(8,128)S(1)}, u32[]{:S(2)}) copy-start(f32[192,16]{0,1:T(8,128)S(1)} %get-tuple-element.814) | copy-start | bytes 36868
  245.6 83.6 %copy-start.69 = (f32[192]{0:T(256)}, f32[192]{0:T(256)S(1)}, u32[]{:S(2)}) copy-start(f32[192]{0:T(256)S(1)} %fusion.150) | copy-start | bytes 2308
  246.1 74.2 %copy-start.15 = (bf16[192,1024]{1,0:T(8,128)(2,1)}, bf16[192,1024]{1,0:T(8,128)(2,1)S(1)}, u32[]{:S(2)}) copy-start(bf16[192,1024]{1,0:T(8,128)(2,1)S(1)} %multiply_convert_fusion.2) | copy-start | bytes 1179652
  397.9 260.5 %reduce-scatter.12.cloned.1.call-start = ((), (), s32[]{:S(2)}) async-start(), calls=%async_computation.14 | async-start | bytes 13369344 | tf_op jit(solution)/shard_map/reduce_scatter | solution.py:44
  413.1 321.0 %reduce-scatter.8.cloned.1.call-start = ((), (), s32[]{:S(2)}) async-start(), calls=%async_computation.12 | async-start | bytes 8912896 | tf_op jit(solution)/shard_map/reduce_scatter | solution.py:44
  424.5 155.7 %copy-start.14 = (f32[192,8,128]{2,0,1:T(8,128)S(1)}, f32[192,8,128]{2,0,1:T(8,128)}, u32[]{:S(2)}) copy-start(f32[192,8,128]{2,0,1:T(8,128)} %copy-done.13) | copy-start | bytes 2359300
  424.5 155.7 %copy-start.53 = (f32[192,8]{0,1:T(8,128)S(1)}, f32[192,8]{0,1:T(8,128)}, u32[]{:S(2)}) copy-start(f32[192,8]{0,1:T(8,128)} %copy-done.52) | copy-start | bytes 18436
  588.1 213.7 %reduce-scatter.10.cloned.1.call-start = ((), (), s32[]{:S(2)}) async-start(), calls=%async_computation.13 | async-start | bytes 4456448 | tf_op jit(solution)/shard_map/reduce_scatter | solution.py:408
  592.7 280.8 %reduce-scatter.14.cloned.1.call-start = ((), (), s32[]{:S(2)}) async-start(), calls=%async_computation.15 | async-start | bytes 6684672 | tf_op jit(solution)/shard_map/reduce_scatter | solution.py:282
  598.6 275.0 %copy-start.21 = (bf16[16,24,8,128]{3,2,1,0:T(8,128)(2,1)S(1)}, bf16[16,24,8,128]{3,2,1,0:T(8,128)(2,1)}, u32[]{:S(2)}) copy-start(bf16[16,24,8,128]{3,2,1,0:T(8,128)(2,1)} %copy-done.20) | copy-start | bytes 2359300
  598.6 369.8 %all-reduce.18.cloned.1.call-start = ((), (), s32[]{:S(2)}) async-start(), calls=%async_computation.16 | async-start | bytes 3932160 | tf_op jit(solution)/shard_map/psum | solution.py:426
  883.6 56.5 %copy-start.66 = (f32[192]{0:T(256)S(1)}, f32[192]{0:T(256)}, u32[]{:S(2)}) copy-start(f32[192]{0:T(256)} %copy-done.65) | copy-start | bytes 2308
  (67 other events, 196.2 us)
Sparse Core Ops, SparseCore 0:
  10.4 56.5 all-gather.5
  68.6 43.0 all-gather.13
  114.6 89.5 all-gather.7
  205.7 35.9 all-gather.9
  243.9 71.9 all-gather.11
  398.0 179.5 reduce-scatter.5
  580.1 78.2 reduce-scatter.11
  661.0 73.1 reduce-scatter.7
  736.7 65.1 reduce-scatter.9
  804.3 69.2 reduce-scatter.13
  877.5 90.8 all-reduce.17
where the time goes:
time: 997 us; the launch traced here: 985 us
  waiting for transfers between devices  640 us (64%)
  matrix products  83.1 us (8%)
  blocking collectives  81.7 us (8%)
  other arithmetic  75.9 us (8%)
  local copies, waits for them, and re-layouts  65 us (7%)
  between operations  17.8 us (2%)
  loops' own time  11.8 us (1%)
    reduce_scatter x3, waiting for transfers between devices, side_by_side(): result = lax.psum_scatter(both, axis, scatter_dimension=dim, tiled=True)  285 us
    all_gather x3, waiting for transfers between devices, sent_together(): lax.all_gather(both, axis, axis=dim, tiled=True)  152 us
    reduce_scatter x1, waiting for transfers between devices, body(): lax.psum_scatter(mlp_terms[2].astype(jnp.bfloat16), 'fsdp', scatter_dimen...  71.6 us
    reduce_scatter x1, waiting for transfers between devices, body(): lax.psum_scatter(attn_terms[3].astype(jnp.bfloat16), 'fsdp', scatter_dime...  64.4 us
    unnamed x2, blocking collectives  61.4 us
    all_gather x1, waiting for transfers between devices, body(): lax.all_gather(shards[6], 'fsdp', axis=0, tiled=True)  30.4 us
    dot_general x7, matrix products, plain_dot(): return jnp.dot(left, right, preferred_element_type=jnp.float32)  28.1 us
    psum x1, waiting for transfers between devices, body(): lax.psum(as_sent(ordered), 'ctx')  27.1 us
  transfers between devices with their start and end apart: 12, of which 11 were waited for; matrix products, arithmetic and copies ran while one was open for 13% of the time, Pallas kernels for 0%

commit v1 on v0

v1 whole, which is shorter than its diff:
```python
import functools
import math

import jax
import jax.numpy as jnp
import numpy as np
from jax import lax
from jax.experimental import pallas as pl
from jax.experimental.pallas import tpu as pltpu
from jax.sharding import PartitionSpec as P

MESH = pl.DeviceIdType.MESH
HEAD = 128
EPSILON = 1e-06
THETA = 1000000.0
BF16, F32 = jnp.bfloat16, jnp.float32
FACTOR = 1.0 / math.sqrt(HEAD)
ANY = pl.BlockSpec(memory_space=pl.ANY)
VM = pl.BlockSpec(memory_space=pltpu.VMEM)
DMA = pltpu.SemaphoreType.DMA


def fid(zl, y, k):
    return zl * 8 + y * 2 + k


class Net:
    def __init__(self):
        f, c = lax.axis_index("fsdp"), lax.axis_index("ctx")
        zl, y, k, zh, x = f // 8, (f // 2) % 4, f % 2, c // 4, c % 4
        self.zl, self.y, self.k, self.zh, self.x = zl, y, k, zh, x
        self.z = zh * 2 + zl
        self.f, self.c = f, c
        self.yp, self.ym = self.along("y", 1), self.along("y", 3)
        self.zp, self.zm = self.along("z", 1), self.along("z", 3)
        self.xp, self.xm = self.along("x", 1), self.along("x", 3)
        self.pair = (fid(1 - zl, y, k), c)
        self.sib = (fid(zl, y, 1 - k), c)
        self.peer_c = (1 - zh) * 4 + x
        self.peer = (f, self.peer_c)

    def at(self, dim):
        return {"y": self.y, "x": self.x, "z": self.z}[dim]

    def along(self, dim, off):
        there = (self.at(dim) + off) % 4
        if dim == "y":
            return (fid(self.zl, there, self.k), self.c)
        if dim == "x":
            return (self.f, self.zh * 4 + there)
        return (fid(there % 2, self.y, self.k), (there // 2) * 4 + self.x)

    def ctx(self, off):
        return (self.c + off) % 8


def barrier(devices):
    sem = pltpu.get_barrier_semaphore()
    for d in devices:
        pl.semaphore_signal(sem, inc=1, device_id=d, device_id_type=MESH)
    pl.semaphore_wait(sem, len(devices))


class Wire:
    def __init__(self, send, recv):
        self.send, self.recv, self.n, self.all = send, recv, 0, []

    def __call__(self, src, dst, device):
        i = self.n
        self.n += 1
        copy = pltpu.make_async_remote_copy(
            src_ref=src, dst_ref=dst, send_sem=self.send.at[i], recv_sem=self.recv.at[i],
            device_id=device, device_id_type=MESH)
        copy.start()
        self.all.append(copy)
        return copy

    def finish(self):
        for copy in self.all:
            copy.wait_send()


class Local:
    def __init__(self, sems):
        self.sems, self.n = sems, 0

    def __call__(self, src, dst):
        copy = pltpu.make_async_copy(src, dst, self.sems.at[self.n])
        self.n += 1
        copy.start()
        return copy


def sems(wires, local):
    return [DMA((wires,)), DMA((wires,)), DMA((local,))]


def talking(number, name, **more):
    return dict(
        compiler_params=pltpu.CompilerParams(
            collective_id=number, has_side_effects=True, vmem_limit_bytes=60 << 20),
        name=name, **more)
def quarters(rows):
    if rows % 64 == 0:
        q = rows // 4
        return (0, q, 2 * q, 3 * q, rows)
    return (0, 16, 32, 48, rows)


class WeightFlow:
    def __init__(self, net, wire, src, out, paired=False):
        self.net, self.wire, self.src, self.out = net, wire, src, out
        self.zp, self.zm = (net.pair, net.pair) if paired else (net.zp, net.zm)
        self.rows = src.shape[0]
        self.q = quarters(self.rows)
        self.c = {}

    def place(self, dz, dy, a=0, b=4):
        n = self.net
        zl = n.zl if dz == 0 else 1 - n.zl
        at = fid(zl, (n.y + dy + 4) % 4, n.k) * self.rows + self.q[a]
        return self.out.at[pl.ds(pl.multiple_of(at, 16), self.q[b] - self.q[a])]

    def own(self, a=0, b=4):
        return self.src.at[pl.ds(self.q[a], self.q[b] - self.q[a])]

    def pass_on(self, name, device, dz, dy, a=0, b=4):
        ref = self.place(dz, dy, a, b)
        self.c[name] = self.wire(ref, ref, device)

    def got(self, name):
        self.c[name].wait_recv()

    def stage(self, s):
        n, w, c = self.net, self.wire, self.c
        if s == 0:
            c["yp"] = w(self.own(), self.place(0, 0), n.yp)
            c["ym"] = w(self.own(), self.place(0, 0), n.ym)
            c["zp"] = w(self.own(0, 2), self.place(0, 0, 0, 2), self.zp)
            c["zm"] = w(self.own(2, 4), self.place(0, 0, 2, 4), self.zm)
            c["d"] = w(self.own(), self.place(0, 0), n.sib)
        elif s == 1:
            self.got("yp")
            self.pass_on("yp2", n.yp, 0, -1, 0, 2)
            self.pass_on("zp_m", self.zp, 0, -1, 0, 2)
            self.pass_on("zm_m", self.zm, 0, -1, 2, 4)
            self.pass_on("d_m", n.sib, 0, -1)
            self.got("ym")
            self.pass_on("ym2", n.ym, 0, 1, 2, 4)
            self.pass_on("zp_p", self.zp, 0, 1, 0, 2)
            self.pass_on("zm_p", self.zm, 0, 1, 2, 4)
            self.pass_on("d_p", n.sib, 0, 1)
            self.got("zp")
            self.pass_on("dz0", n.sib, 1, 0, 0, 2)
            self.got("zm")
            self.pass_on("dz1", n.sib, 1, 0, 2, 4)
        elif s == 2:
            self.got("yp2")
            self.pass_on("zp_2", self.zp, 0, 2, 0, 1)
            self.pass_on("d2a", n.sib, 0, 2, 0, 2)
            self.got("ym2")
            self.pass_on("zm_2", self.zm, 0, 2, 2, 3)
            self.pass_on("d2b", n.sib, 0, 2, 2, 4)
            self.got("zp_m")
            self.pass_on("yq", n.yp, 1, -1, 1, 2)
            self.pass_on("dzm0", n.sib, 1, -1, 0, 2)
            self.got("zm_p")
            self.pass_on("yr", n.ym, 1, 1, 3, 4)
            self.pass_on("dzp1", n.sib, 1, 1, 2, 4)
            self.got("zm_m")
            self.pass_on("dzm1", n.sib, 1, -1, 2, 4)
            self.got("zp_p")
            self.pass_on("dzp0", n.sib, 1, 1, 0, 2)
        elif s == 3:
            self.got("zp_2")
            self.got("yq")
            self.pass_on("dz20", n.sib, 1, 2, 0, 2)
            self.got("zm_2")
            self.got("yr")
            self.pass_on("dz21", n.sib, 1, 2, 2, 4)
        elif s == 4:
            for name in ("d", "d_m", "d_p", "dz0", "dz1", "d2a", "d2b", "dzm0", "dzp1", "dzm1", "dzp0", "dz20", "dz21"):
                self.got(name)


class RowFlow:
    def __init__(self, net, wire, src, out):
        self.net, self.wire, self.src, self.out = net, wire, src, out
        self.rows = src.shape[0]
        self.c = {}

    def place(self, ctx, a=0, b=2):
        lo, hi = a * self.rows // 2, b * self.rows // 2
        return self.out.at[pl.ds(pl.multiple_of(ctx * self.rows + lo, 16), hi - lo)]

    def pass_on(self, name, device, ctx, a=0, b=2):
        ref = self.place(ctx, a, b)
        self.c[name] = self.wire(ref, ref, device)

    def got(self, name):
        self.c[name].wait_recv()

    def stage(self, s):
        n, w, c = self.net, self.wire, self.c
        left, right = n.zh * 4 + (n.x + 3) % 4, n.zh * 4 + (n.x + 1) % 4
        left2, right2 = (1 - n.zh) * 4 + (n.x + 3) % 4, (1 - n.zh) * 4 + (n.x + 1) % 4
        if s == 0:
            c["pz"] = w(self.src, self.place(n.c), n.peer)
            c["xp"] = w(self.src, self.place(n.c), n.xp)
            c["xm"] = w(self.src, self.place(n.c), n.xm)
        elif s == 1:
            self.got("pz")
            self.pass_on("px", n.xp, n.peer_c)
            self.pass_on("pxm", n.xm, n.peer_c)
            self.got("xp")
            self.pass_on("xp2", n.xp, left, 0, 1)
            self.got("xm")
            self.pass_on("xm2", n.xm, right, 1, 2)
        elif s == 2:
            self.got("px")
            self.pass_on("px2", n.xp, left2, 0, 1)
            self.got("pxm")
            self.pass_on("pxm2", n.xm, right2, 1, 2)
        elif s == 3:
            for name in ("xp2", "xm2", "px2", "pxm2"):
                self.got(name)


def gather_kernel(nw, *refs):
    srcs, rows = refs[:nw], refs[nw]
    outs, rows_out = refs[nw + 1:2 * nw + 1], refs[2 * nw + 1]
    send, recv, local = refs[2 * nw + 2:]
    net, wire, here = Net(), Wire(send, recv), Local(local)
    barrier([net.yp, net.ym, net.zp, net.zm, net.sib, net.xp, net.xm, net.peer])
    flows = [WeightFlow(net, wire, s, o, i == 0) for i, (s, o) in enumerate(zip(srcs, outs))]
    seq = RowFlow(net, wire, rows, rows_out)
    flows[0].stage(0)
    seq.stage(0)
    flows[1].stage(0)
    kept = [here(fl.src, fl.place(0, 0)) for fl in flows]
    kept.append(here(rows, seq.place(net.c)))
    flows[0].stage(1)
    flows[2].stage(0)
    seq.stage(1)
    flows[0].stage(2)
    flows[1].stage(1)
    seq.stage(2)
    flows[0].stage(3)
    flows[0].stage(4)
    for s in range(2, nw + 3):
        if s + 1 < nw:
            flows[s + 1].stage(0)
        if s < nw:
            flows[s].stage(1)
        if s == 2:
            seq.stage(3)
        if s - 1 < nw:
            flows[s - 1].stage(2)
        if 1 <= s - 2 < nw:
            flows[s - 2].stage(3)
            flows[s - 2].stage(4)
    for h in kept:
        h.wait()
    wire.finish()


def gather(weights, rows):
    nw = len(weights)
    outs = [jax.ShapeDtypeStruct((16 * w.shape[0], w.shape[1]), w.dtype) for w in weights]
    outs.append(jax.ShapeDtypeStruct((8 * rows.shape[0], rows.shape[1]), rows.dtype))
    res = pl.pallas_call(
        functools.partial(gather_kernel, nw),
        out_shape=outs, in_specs=[ANY] * (nw + 1), out_specs=[ANY] * len(outs),
        scratch_shapes=sems(27 * nw + 9, nw + 1), **talking(0, "gather"),
    )(*weights, rows)
    return res[:nw], res[nw]


def spread_kernel(forward, src, dst, send, recv, local):
    net, wire, here = Net(), Wire(send, recv), Local(local)
    barrier([(net.f, net.ctx(o)) for o in range(1, 8)])
    rows, cols = (dst.shape[0], src.shape[1]) if forward else (src.shape[0], dst.shape[1])

    def by_row(ref, c):
        return ref.at[pl.ds(pl.multiple_of(c * rows, 16), rows)]

    def by_col(ref, c):
        return ref.at[:, pl.ds(pl.multiple_of(c * cols, 128), cols)]

    pick, put = (by_row, by_col) if forward else (by_col, by_row)
    copies = []
    for o in (4, 6, 2, 5, 7, 1, 3):
        there = net.ctx(o)
        copies.append(wire(pick(src, there), put(dst, net.c), (net.f, there)))
    own = here(pick(src, net.c), put(dst, net.c))
    for copy in copies:
        copy.wait_recv()
    own.wait()
    wire.finish()


def spread(forward, src, number):
    a, b = src.shape
    shape = (a // 8, b * 8) if forward else (a * 8, b // 8)
    return pl.pallas_call(
        functools.partial(spread_kernel, forward),
        out_shape=jax.ShapeDtypeStruct(shape, src.dtype), in_specs=[ANY], out_specs=ANY,
        scratch_shapes=sems(7, 1), **talking(number, "spread%d" % number),
    )(src)
def block(i, size):
    return pl.ds(pl.multiple_of(i * size, size), size)


def dot_t(left, right):
    return lax.dot_general(left, right, (((1,), (1,)), ((), ())), preferred_element_type=F32)


def t_dot(left, right):
    return lax.dot_general(left, right, (((0,), (0,)), ((), ())), preferred_element_type=F32)


def plain_dot(left, right):
    return jnp.dot(left, right, preferred_element_type=F32)


def unit(v):
    r = lax.rsqrt(jnp.mean(v * v, axis=-1, keepdims=True) + EPSILON)
    return v * r, r


ROWS = 256


def attn_forward(x, t, cos_in, sin_in, w, gains, q, k, v, lin, cs, sn, start, hf, heads, inv):
    length, width = x.shape[0], x.shape[1] - HEAD
    per = t.shape[0] // 16
    depth = per - 16
    total = jnp.zeros((16, t.shape[1]), F32)
    for f in range(16):
        w[f * depth:(f + 1) * depth, :] = t[f * per:f * per + depth, :]
        total = total + t[f * per + depth:(f + 1) * per, :].astype(F32)
    gains[...] = total
    attn_gain = jnp.concatenate([total[0:1], total[1:2]], axis=1)
    query_gain, key_gain = total[4:5, 0:HEAD], total[4:5, HEAD:2 * HEAD]

    def count(i, carry):
        doc = x[block(i, ROWS), width:].astype(F32)
        return (carry[0] + jnp.sum((doc < 0.5).astype(F32), axis=0, keepdims=True),
                carry[1] + jnp.sum((doc < 1.5).astype(F32), axis=0, keepdims=True))

    zero = jnp.zeros((1, HEAD), F32)
    first, second = lax.fori_loop(0, length // ROWS, count, (zero, zero))
    lanes = lax.broadcasted_iota(jnp.int32, (1, HEAD), 1) % (HEAD // 2)
    freqs = jnp.exp(lanes.astype(F32) * (-2.0 * math.log(THETA) / HEAD))
    c1, s1 = jnp.cos(first * freqs), jnp.sin(first * freqs)
    c2, s2 = jnp.cos(second * freqs), jnp.sin(second * freqs)
    sign = jnp.where(lax.broadcasted_iota(jnp.int32, (1, HEAD), 1) < HEAD // 2, -1.0, 1.0)

    def prepare(i, carry):
        rows = block(i, ROWS)
        doc = x[rows, width:].astype(F32)
        start[rows, :] = jnp.where(doc < 0.5, 0.0, jnp.where(doc < 1.5, first, second))
        cd = jnp.where(doc < 0.5, 1.0, jnp.where(doc < 1.5, c1, c2))
        sd = jnp.where(doc < 0.5, 0.0, jnp.where(doc < 1.5, s1, s2))
        ci, si = cos_in[rows, :], sin_in[rows, :]
        cosine = ci * cd + si * sd
        sine = (si * cd - ci * sd) * sign
        cs[rows, :] = cosine
        sn[rows, :] = sine
        normed = (unit(x[rows, :width].astype(F32))[0] * attn_gain).astype(BF16)
        out = plain_dot(normed, w[...])
        lin[rows, :] = out[:, :3 * HEAD]
        v[rows, :] = out[:, 3 * HEAD:].astype(BF16)
        for h in range(3):
            e = unit(out[:, h * HEAD:(h + 1) * HEAD])[0] * (query_gain if h < 2 else key_gain)
            e = (e * cosine + pltpu.roll(e, HEAD // 2, 1) * sine).astype(BF16)
            if h < 2:
                q[h, rows, :] = e
            else:
                k[rows, :] = e
        return carry

    lax.fori_loop(0, length // ROWS, prepare, 0)

    def queries(i, carry):
        rows = block(i, ROWS)
        here = q[:, rows, :].reshape(2 * ROWS, HEAD)
        begin = start[rows, :]

        def keys(j, state):
            acc, norm = state
            these = block(j, ROWS)
            p = jnp.exp(dot_t(here, k[these, :]) * FACTOR)
            p = jnp.where(allowed_at(i, j, begin), p.reshape(2, ROWS, ROWS), 0.0).reshape(2 * ROWS, ROWS)
            norm = norm + p[:, :HEAD] + p[:, HEAD:]
            return acc + plain_dot(p.astype(BF16), v[these, :]), norm

        zeros = jnp.zeros((2 * ROWS, HEAD), F32)
        acc, norm = lax.fori_loop(0, i + 1, keys, (zeros, zeros))
        over = jnp.broadcast_to(1.0 / jnp.sum(norm, axis=1, keepdims=True), (2 * ROWS, HEAD))
        acc = acc * over
        inv[:, rows, :] = over.reshape(2, ROWS, HEAD)
        for h in range(2):
            part = acc[h * ROWS:(h + 1) * ROWS]
            hf[rows, h * HEAD:(h + 1) * HEAD] = part
            heads[rows, h * HEAD:(h + 1) * HEAD] = part.astype(BF16)
        return carry

    lax.fori_loop(0, length // ROWS, queries, 0)


def allowed_at(i, j, begin):
    own = lax.broadcasted_iota(jnp.int32, (ROWS, ROWS), 0) + i * ROWS
    other = lax.broadcasted_iota(jnp.int32, (ROWS, ROWS), 1) + j * ROWS
    begin = jnp.concatenate([begin, begin], axis=1)
    return ((other.astype(F32) >= begin) & (other <= own))[None]


def attn_backward(x, w, gains, q, k, v, lin, cs, sn, start, hf, inv, dh, dw, dn, dg, dq, dk, dv, delta, dlin):
    length, width = x.shape[0], x.shape[1] - HEAD
    blocks = length // ROWS
    g = gains[...]
    attn_gain = jnp.concatenate([g[0:1], g[1:2]], axis=1)
    query_gain, key_gain = g[4:5, 0:HEAD], g[4:5, HEAD:2 * HEAD]

    def before(i, carry):
        rows = block(i, ROWS)
        for h in range(2):
            cols = slice(h * HEAD, (h + 1) * HEAD)
            s = jnp.sum(dh[rows, cols].astype(F32) * hf[rows, cols], axis=1, keepdims=True)
            delta[h, rows, :] = jnp.broadcast_to(s, (ROWS, HEAD))
            dq[h, rows, :] = jnp.zeros((ROWS, HEAD), F32)
        return carry

    lax.fori_loop(0, blocks, before, 0)

    def keys(j, carry):
        these = block(j, ROWS)
        kt, vt = k[these, :], v[these, :]

        def queries(i, state):
            d_key, d_value = state
            rows = block(i, ROWS)
            here = q[:, rows, :].reshape(2 * ROWS, HEAD)
            grad = jnp.concatenate([dh[rows, :HEAD], dh[rows, HEAD:]], axis=0)
            over = inv[:, rows, :].reshape(2 * ROWS, HEAD)
            off = delta[:, rows, :].reshape(2 * ROWS, HEAD)
            over = jnp.concatenate([over, over], axis=1)
            off = jnp.concatenate([off, off], axis=1)
            p = jnp.exp(dot_t(here, kt) * FACTOR) * over
            p = jnp.where(allowed_at(i, j, start[rows, :]), p.reshape(2, ROWS, ROWS), 0.0).reshape(2 * ROWS, ROWS)
            ds = (p * (dot_t(grad, vt) - off)).astype(BF16)
            dq[:, rows, :] = dq[:, rows, :] + plain_dot(ds, kt).reshape(2, ROWS, HEAD)
            return d_key + t_dot(ds, here), d_value + t_dot(p.astype(BF16), grad)

        zeros = jnp.zeros((ROWS, HEAD), F32)
        d_key, d_value = lax.fori_loop(j, blocks, queries, (zeros, zeros))
        dk[these, :] = d_key
        dv[these, :] = d_value
        return carry

    lax.fori_loop(0, blocks, keys, 0)

    def after(i, carry):
        d_attn, d_query, d_key = carry
        rows = block(i, ROWS)
        cosine, sine = cs[rows, :], sn[rows, :]
        for h in range(3):
            cols = slice(h * HEAD, (h + 1) * HEAD)
            d = (dq[h, rows, :] if h < 2 else dk[rows, :]) * FACTOR
            d = d * cosine - pltpu.roll(d, HEAD // 2, 1) * sine
            e, r = unit(lin[rows, cols])
            s = jnp.sum(d * e, axis=0, keepdims=True)
            d_query, d_key = (d_query + s, d_key) if h < 2 else (d_query, d_key + s)
            d = d * (query_gain if h < 2 else key_gain)
            d = r * (d - e * jnp.mean(d * e, axis=-1, keepdims=True))
            dlin[rows, cols] = d.astype(BF16)
        dlin[rows, 3 * HEAD:] = dv[rows, :].astype(BF16)
        part = dot_t(dlin[rows, :], w[...])
        e = unit(x[rows, :width].astype(F32))[0]
        d_attn = d_attn + jnp.sum(part * e, axis=0, keepdims=True)
        dn[rows, :] = part.astype(BF16)
        normed = (e * attn_gain).astype(BF16)

        part = t_dot(normed, dlin[rows, :])
        dw[...] = jnp.where(i == 0, part, dw[...] + part)
        return d_attn, d_query, d_key

    zero = jnp.zeros((1, HEAD), F32)
    dw[...] = jnp.zeros_like(dw)
    d_attn, d_query, d_key = lax.fori_loop(0, blocks, after, (jnp.zeros((1, width), F32), zero, zero))
    dg[0:1, :] = d_attn
    dg[1:2, :] = jnp.concatenate([d_query, d_key, jnp.zeros((1, width - 2 * HEAD), F32)], axis=1)


def shapes(*items):
    return [jax.ShapeDtypeStruct(s, d) for s, d in items]


def attend(x, t, cos_in, sin_in):
    length = x.shape[0]
    out = shapes(
        ((16 * (t.shape[0] // 16 - 16), t.shape[1]), BF16), ((16, t.shape[1]), F32),
        ((2, length, HEAD), BF16), ((length, HEAD), BF16), ((length, HEAD), BF16), ((length, 3 * HEAD), F32),
        ((length, HEAD), F32), ((length, HEAD), F32), ((length, HEAD), F32), ((length, 2 * HEAD), F32),
        ((length, 2 * HEAD), BF16), ((2, length, HEAD), F32))
    return pl.pallas_call(
        attn_forward, out_shape=out, in_specs=[VM] * 4, out_specs=[VM] * len(out),
        compiler_params=pltpu.CompilerParams(vmem_limit_bytes=56 << 20), name="attend")(x, t, cos_in, sin_in)


def attend_back(x, kept, dh):
    w, gains, q, k, v, lin, cs, sn, start, hf, _, inv = kept
    length, width = x.shape[0], x.shape[1] - HEAD
    out = shapes((w.shape, F32), ((length, width), BF16), ((8, width), F32))
    args = (x, w, gains, q, k, v, lin, cs, sn, start, hf, inv, dh)
    return pl.pallas_call(
        attn_backward, out_shape=out, in_specs=[VM] * len(args), out_specs=[VM] * len(out),
        scratch_shapes=[
            pltpu.VMEM((2, length, HEAD), F32), pltpu.VMEM((length, HEAD), F32), pltpu.VMEM((length, HEAD), F32),
            pltpu.VMEM((2, length, HEAD), F32), pltpu.VMEM((length, 4 * HEAD), BF16)],
        compiler_params=pltpu.CompilerParams(vmem_limit_bytes=60 << 20), name="attend_back")(*args)
def add_rows(out, parts, rows, step):
    def some(r, carry):
        here = pl.ds(pl.multiple_of(r * step, 16), step)
        total = parts[0](here).astype(F32)
        for part in parts[1:]:
            total = total + part(here).astype(F32)
        out(here, total.astype(BF16))
        return carry

    lax.fori_loop(0, rows // step, some, 0)


class SumFlow:
    def __init__(self, net, wire, here, src, first, order, mine, other, got, part, fin, out):
        self.net, self.wire, self.here, self.src, self.first, self.order = net, wire, here, src, first, order
        self.mine, self.other, self.got, self.part, self.fin, self.out = mine, other, got, part, fin, out
        self.rows, self.cols = mine.shape[2], mine.shape[3]
        self.w = self.cols // 8
        self.far = {}

    def cut(self, ref, dim, d, k=None):
        tail = ref.shape[-1]
        a = (slice(None), slice(None))
        cols = pl.ds(0, tail)
        if dim == "y":
            a = (slice(None), pl.ds(d, 1))
        elif dim == "x":
            cols = pl.ds(pl.multiple_of(d * (tail // 4), 128), tail // 4)
        else:
            a = (pl.ds(d % 2, 1), slice(None))
            cols = pl.ds(pl.multiple_of((d // 2) * (tail // 2), 128), tail // 2)
        if k is None:
            return ref.at[a[0], a[1], :, cols]
        return ref.at[a[0], a[1], k, pl.ds(self.first, self.rows), cols]

    def begin(self):
        n, dim = self.net, self.order[0]
        self.near, self.own = {}, {}
        for o in (2, 1, 3, 0):
            d = (n.at(dim) + o) % 4
            self.near[o] = self.wire(self.cut(self.src, dim, d, 1 - n.k), self.cut(self.other, dim, d), n.sib)
            self.own[o] = self.here(self.cut(self.src, dim, d, n.k), self.cut(self.mine, dim, d))

    def add(self, out, parts):
        a, b = out.shape[0], out.shape[1]
        step = 16
        for i in range(a):
            for j in range(b):
                def take(ref):
                    return lambda here: ref[i, j, here, :]

                def put(here, value):
                    out[i, j, here, :] = value
                add_rows(put, [take(p) for p in parts], self.rows, step)

    def chip(self, o):
        n, dim = self.net, self.order[0]
        d = (n.at(dim) + o) % 4
        self.near[o].wait_recv()
        self.own[o].wait()
        piece = self.cut(self.mine, dim, d)
        self.add(piece, [piece, self.cut(self.other, dim, d)])
        if o:
            self.far[o] = self.wire(piece, self.got[0].at[o - 1], n.along(dim, o))

    def phase(self, p):
        n, dim = self.net, self.order[p]
        held = self.mine if p == 0 else self.part[p - 1]
        for o in (1, 3, 2):
            self.far[o].wait_recv()
        result = self.part[p] if p < 2 else self.fin
        self.add(result, [self.cut(held, dim, n.at(dim))] + [self.got[p].at[o - 1] for o in (1, 2, 3)])
        if p < 2:
            after = self.order[p + 1]
            for o in (2, 1, 3):
                d = (n.at(after) + o) % 4
                self.far[o] = self.wire(self.cut(result, after, d), self.got[p + 1].at[o - 1], n.along(after, o))
        else:
            s = n.c if self.order == "zyx" else n.x * 2 + n.zh
            to = self.out.at[pl.ds(self.first, self.rows), pl.ds(pl.multiple_of(s * self.w, 128), self.w)]
            fin = self.fin.at[0, 0]
            self.last = [self.wire(fin, to, (n.f, n.ctx(o))) for o in (4, 6, 2, 5, 7, 1, 3)]
            self.kept = self.here(fin, to)

    def end(self):
        for copy in self.last:
            copy.wait_recv()
        self.kept.wait()


def sum_shapes(rows, cols, order):
    shape, out = [2, 4, rows, cols], []
    for dim in order:
        if dim == "y":
            shape[1] = 1
        elif dim == "x":
            shape[3] //= 4
        else:
            shape[0], shape[3] = 1, shape[3] // 2
        out.append(tuple(shape))
    return out


PLAN = ((0, 0, 64, "yxz"), (1, 0, 64, "xzy"), (2, 0, 192, "zyx"),
        (3, 0, 48, "yxz"), (3, 48, 48, "xzy"), (3, 96, 32, "zyx"))


def everyone(net):
    return ([net.sib] + [net.along(d, o) for d in "yxz" for o in (1, 2, 3)]
            + [(net.f, (1 - net.zh) * 4 + (net.x + o) % 4) for o in (1, 2, 3)])


def sum_scratch(plan, shapes_in):
    held = []
    for which, first, rows, order in plan:
        cols = shapes_in[which][-1]
        a, b, c = sum_shapes(rows, cols, order)
        full = (2, 4, rows, cols)
        held += [pltpu.VMEM(s, BF16) for s in (full, full, (3, *a), (3, *b), (3, *c), a, b, c)]
    return held


def make_flows(net, wire, here, plan, srcs, outs, held):
    flows = []
    for n, (which, first, rows, order) in enumerate(plan):
        mine, other, g0, g1, g2, p0, p1, fin = held[8 * n:8 * n + 8]
        flows.append(SumFlow(net, wire, here, srcs[which], first, order, mine, other, (g0, g1, g2), (p0, p1), fin, outs[which]))
    return flows


def sum_kernel(plan, count, *refs):
    srcs, outs = refs[:count], refs[count:2 * count]
    held, (send, recv, local) = refs[2 * count:-3], refs[-3:]
    net, wire, here = Net(), Wire(send, recv), Local(local)
    barrier(everyone(net))
    flows = make_flows(net, wire, here, plan, srcs, outs, held)
    for fl in flows:
        fl.begin()
    for o in (2, 1, 3, 0):
        for fl in flows:
            fl.chip(o)
    for p in range(3):
        for fl in flows:
            fl.phase(p)
    for fl in flows:
        fl.end()
    wire.finish()


def sum_all(grads, number):
    srcs = [g.reshape(2, 4, 2, g.shape[0] // 16, g.shape[1]) for g in grads]
    out = [jax.ShapeDtypeStruct((g.shape[0] // 16, g.shape[1]), BF16) for g in grads]
    wires, locals_ = 20 * len(PLAN), 5 * len(PLAN)
    return pl.pallas_call(
        functools.partial(sum_kernel, PLAN, len(grads)), out_shape=out,
        in_specs=[ANY] * len(grads), out_specs=[ANY] * len(grads),
        scratch_shapes=sum_scratch(PLAN, [g.shape for g in grads]) + sems(wires, locals_), **talking(number, "sum_all"))(*srcs)


def last_kernel(dw, dn, rows_out, dn_out, mine, other, got, fin, blocks, own, send, recv, local):
    net, wire, here = Net(), Wire(send, recv), Local(local)
    others = [(o, (net.f, net.ctx(o))) for o in (4, 6, 2, 5, 7, 1, 3)]
    cores = [(dz, dy, (fid((net.zl + dz) % 2, (net.y + dy) % 4, net.k), net.c)) for dz in (1, 0) for dy in (2, 1, 3, 0) if dz or dy]
    barrier([net.sib] + [d for _, d in others] + [d for _, _, d in cores])
    rows = own.shape[0]
    near = wire(dw.at[:, :, 1 - net.k], other, net.sib)
    kept = here(dw.at[:, :, net.k], mine)
    home = here(dn.at[pl.ds(pl.multiple_of(net.c * rows, 16), rows)], own)
    moved = [wire(dn.at[pl.ds(pl.multiple_of(net.ctx(o) * rows, 16), rows)], blocks.at[o - 1], d) for o, d in others]
    near.wait_recv()
    kept.wait()
    for a in range(2):
        for b in range(4):
            mine[a, b] = (mine[a, b].astype(F32) + other[a, b].astype(F32)).astype(BF16)
    far = [wire(mine.at[(net.zl + dz) % 2, (net.y + dy) % 4], got.at[dz * 4 + dy - 1], d) for dz, dy, d in cores]
    for copy in far:
        copy.wait_recv()
    total = mine[net.zl, net.y].astype(F32)
    for i in range(7):
        total = total + got[i].astype(F32)
    fin[...] = total.astype(BF16)
    spreads = [wire(fin, rows_out.at[net.c], d) for _, d in others]
    placed = here(fin, rows_out.at[net.c])
    for copy in moved:
        copy.wait_recv()
    home.wait()

    def some(r, carry):
        at = pl.ds(pl.multiple_of(r * 16, 16), 16)
        s = own[at, :].astype(F32)
        for i in range(7):
            s = s + blocks[i, at, :].astype(F32)
        dn_out[at, :] = s
        return carry

    lax.fori_loop(0, rows // 16, some, 0)
    for copy in spreads:
        copy.wait_recv()
    placed.wait()
    wire.finish()


def last_sums(dw, dn, number):
    rows, width = dn.shape[0] // 8, dn.shape[1]
    a, b = dw.shape[-2:]
    return pl.pallas_call(
        last_kernel, out_shape=shapes(((8, a, b), BF16), ((rows, width), F32)),
        in_specs=[ANY, ANY], out_specs=[ANY, VM],
        scratch_shapes=[
            pltpu.VMEM((2, 4, a, b), BF16), pltpu.VMEM((2, 4, a, b), BF16), pltpu.VMEM((7, a, b), BF16), pltpu.VMEM((a, b), BF16),
            pltpu.VMEM((7, rows, width), BF16), pltpu.VMEM((rows, width), BF16)] + sems(22, 3), **talking(number, "last_sums"))(dw, dn)
def root_mean_norm(rows, scaling):
    return rows * lax.rsqrt(jnp.mean(rows * rows, axis=-1, keepdims=True) + EPSILON) * scaling


def silu_product(gate, upward):
    return jax.nn.silu(gate) * upward


def mlp(residual, heads, grad_rows, full_output, full_gate, full_up, full_down, mlp_scale):
    hidden = residual + plain_dot(heads, full_output)
    mixed_f, mix_pull = jax.vjp(root_mean_norm, hidden, mlp_scale)
    mixed = mixed_f.astype(BF16)
    gate, upward = plain_dot(mixed, full_gate), plain_dot(mixed, full_up)
    active_f, active_pull = jax.vjp(silu_product, gate, upward)
    active = active_f.astype(BF16)
    outputs = (hidden + plain_dot(active, full_down)).astype(BF16)
    d_down = t_dot(active, grad_rows)
    d_gate, d_upward = active_pull(dot_t(grad_rows, full_down))
    gate_low, up_low = d_gate.astype(BF16), d_upward.astype(BF16)
    d_gate_w, d_up_w = t_dot(mixed, gate_low), t_dot(mixed, up_low)
    d_mixed = dot_t(gate_low, full_gate) + dot_t(up_low, full_up)
    d_hidden_norm, d_mlp_scale = mix_pull(d_mixed)
    d_hidden = grad_rows.astype(F32) + d_hidden_norm
    hidden_low = d_hidden.astype(BF16)
    d_output = t_dot(heads, hidden_low)
    d_heads = dot_t(hidden_low, full_output).astype(BF16)
    grads = [g.astype(BF16) for g in (d_gate_w, d_up_w, d_down, d_output)]
    return outputs, d_hidden, d_heads, grads, d_mlp_scale


def tables(length):
    freqs = THETA ** (-np.arange(HEAD // 2, dtype=np.float64) * 2.0 / HEAD)
    angles = np.arange(length, dtype=np.float64)[:, None] * np.concatenate([freqs, freqs])[None, :]
    return jnp.asarray(np.cos(angles), F32), jnp.asarray(np.sin(angles), F32)


def placed(values, f, size):
    return lax.dynamic_update_slice_in_dim(jnp.zeros((size,), BF16), values, f * values.shape[0], 0)


def body(inputs, doc_ids, query_proj, key_projection, value_projection, output_proj, gate_proj, up_proj, down_proj,
         attn_gain, mlp_gain, query_norm_gain, key_gain, out_grad):
    f, c = lax.axis_index("fsdp"), lax.axis_index("ctx")
    rows, width = inputs.shape[1:]
    depth = query_proj.shape[0]
    cols = 4 * HEAD
    own = jnp.concatenate([
        lax.dynamic_slice_in_dim(query_proj, c * 2 * HEAD, 2 * HEAD, 1),
        lax.dynamic_slice_in_dim(key_projection, c * HEAD, HEAD, 1),
        lax.dynamic_slice_in_dim(value_projection, c * HEAD, HEAD, 1)], axis=1)
    small = jnp.concatenate([
        placed(attn_gain, f, width), placed(mlp_gain, f, width), placed(query_norm_gain, f, HEAD), placed(key_gain, f, HEAD),
        jnp.zeros((16 * cols - 2 * width - 2 * HEAD,), BF16)]).reshape(16, cols)
    pack = jnp.concatenate([own, small], axis=0)
    sequence = jnp.concatenate([inputs[0], jnp.broadcast_to(doc_ids[0].astype(BF16)[:, None], (rows, HEAD))], axis=1)
    (t, full_output, full_gate, full_up, full_down), x = gather([pack, output_proj, gate_proj, up_proj, down_proj], sequence)
    kept = attend(x, t, *tables(x.shape[0]))
    gains, heads = kept[1], kept[10]
    own_heads = spread(True, heads, 1)
    residual = inputs[0].astype(F32)
    mlp_scale = gains[2:4].reshape(width)
    outputs, d_hidden, d_heads, grads, d_mlp_scale = mlp(
        residual, own_heads, out_grad[0], full_output, full_gate, full_up, full_down, mlp_scale)
    dh = spread(False, d_heads, 2)
    gate_g, up_g, down_g, output_g = sum_all(grads, 3)
    dw, dn, dg = attend_back(x, kept, dh)
    gain_rows = jnp.concatenate([
        dg[0].reshape(16, depth), d_mlp_scale.reshape(16, depth),
        dg[1, :HEAD].reshape(16, 8), dg[1, HEAD:2 * HEAD].reshape(16, 8)], axis=1)
    gain_rows = jnp.pad(gain_rows[:, None, :], ((0, 0), (0, 15), (0, cols - gain_rows.shape[1])))
    dw = jnp.concatenate([dw.reshape(16, depth, cols), gain_rows], axis=1).astype(BF16)
    back, d_normed = last_sums(dw.reshape(2, 4, 2, depth + 16, cols), dn, 4)
    _, norm_pull = jax.vjp(lambda r: root_mean_norm(r, gains[0:2].reshape(width)), residual)
    input_grad = d_hidden + norm_pull(d_normed)[0]
    back = back.astype(F32)
    query_g = jnp.moveaxis(back[:, :depth, :2 * HEAD], 0, 1).reshape(depth, -1)
    key_g = jnp.moveaxis(back[:, :depth, 2 * HEAD:3 * HEAD], 0, 1).reshape(depth, -1)
    value_g = jnp.moveaxis(back[:, :depth, 3 * HEAD:], 0, 1).reshape(depth, -1)
    small_g = jnp.sum(back[:, depth, :], axis=0)
    return (outputs[None], input_grad[None], query_g, key_g, value_g, output_g.astype(F32), gate_g.astype(F32),
            up_g.astype(F32), down_g.astype(F32), small_g[:depth], small_g[depth:2 * depth],
            small_g[2 * depth:2 * depth + 8], small_g[2 * depth + 8:2 * depth + 16])


def solution(mesh):
    seq, weight, gain = P("fsdp", "ctx", None), P("fsdp", None), P("fsdp")
    in_specs = (seq, P("fsdp", "ctx")) + (weight,) * 7 + (gain,) * 4 + (seq,)
    out_specs = (seq, seq) + (weight,) * 7 + (gain,) * 4
    return jax.shard_map(body, mesh=mesh, in_specs=in_specs, out_specs=out_specs, check_vma=False)
```

time: 997 us -> 389 us (0.39); the launches traced: 985 us -> 389 us
  waiting for transfers between devices: 640 us -> 0 us
  Pallas kernels: 0 us -> 321 us
  blocking collectives: 81.7 us -> 0 us
  other arithmetic: 75.9 us -> 18.8 us
  local copies, waits for them, and re-layouts: 65 us -> 12 us
  matrix products: 83.1 us -> 35.8 us
  between operations: 17.8 us -> 1 us
  loops' own time: 11.8 us -> 0 us
    reduce_scatter x5 -> x0, waiting for transfers between devices: 421 us -> none  [the longest x3 285 us: side_by_side(): result = lax.psum_scatter(both, axis, scatter_dimension=dim, tiled=True)]
    pallas_call x0 -> x7, Pallas kernels: none -> 321 us  [the longest x1 93.4 us: sum_all(): pl.pallas_call(functools.partial(sum_kernel, PLAN, len(grads)), out_shape...]
    all_gather x5 -> x0, waiting for transfers between devices: 191 us -> none  [the longest x3 152 us: sent_together(): lax.all_gather(both, axis, axis=dim, tiled=True)]
    unnamed x2 -> x0, blocking collectives: 61.4 us -> none
    dot_general x28 -> x12, matrix products: 83.1 us -> 35.8 us  [the longest x4 16.8 us: t_dot(): lax.dot_general(left, right, (((0,), (0,)), ((), ())), preferred_element_...]
    psum x1 -> x0, waiting for transfers between devices: 27.1 us -> none  [body(): lax.psum(as_sent(ordered), 'ctx')]
    psum x1 -> x0, blocking collectives: 20.3 us -> none  [body(): lax.psum(as_sent(ordered), 'ctx')]
    reduce_or x16 -> x0, other arithmetic: 17.7 us -> none  [the longest x8 11.6 us: back_block(): return lax.cond(jnp.any(allowed), back_compute, unchanged, carry_state)]
  transfers between devices with their start and end apart: 12 -> 0, of which waited for: 11 -> 0; matrix products, arithmetic and copies ran while one was open for 13% -> 0% of each run, Pallas kernels for 0% -> 0%
where the time goes in v1:
time: 389 us
  Pallas kernels  321 us (83%)
  matrix products  35.8 us (9%)
  other arithmetic  18.8 us (5%)
  local copies, waits for them, and re-layouts  12 us (3%)
    pallas_call x1, Pallas kernels, sum_all(): pl.pallas_call(functools.partial(sum_kernel, PLAN, len(grads)), out_shape...  93.4 us
    pallas_call x1, Pallas kernels, gather(): pl.pallas_call(functools.partial(gather_kernel, nw), out_shape=outs, in_s...  84.7 us
    pallas_call x1, Pallas kernels, last_sums(): pl.pallas_call(last_kernel, out_shape=shapes(((8, a, b), BF16), ((rows, w...  56.6 us
    pallas_call x1, Pallas kernels, attend_back(): pl.pallas_call(attn_backward, out_shape=out, in_specs=[VM] * len(args), o...  32.5 us
    pallas_call x2, Pallas kernels, spread(): pl.pallas_call(functools.partial(spread_kernel, forward), out_shape=jax.S...  30.8 us
    pallas_call x1, Pallas kernels, attend(): pl.pallas_call(attn_forward, out_shape=out, in_specs=[VM] * 4, out_specs=...  23.2 us
    dot_general x4, matrix products, t_dot(): lax.dot_general(left, right, (((0,), (0,)), ((), ())), preferred_element_...  16.8 us
    dot_general x4, matrix products, dot_t(): lax.dot_general(left, right, (((1,), (1,)), ((), ())), preferred_element_...  10.3 us

profile of v1, /device:TPU:1, one launch (start us, length us, event | category | flops | bytes accessed | tf_op | source)
XLA Modules:
  0.0 388.8 jit_solution(3531494791111979142)
XLA Ops:
  0.7 0.9 dynamic_update_slice.12
  1.6 0.9 dynamic_update_slice.13
  2.4 0.9 dynamic_update_slice.14
  7.1 1.8 pad_maximum_fusion.1.refs_5_
  8.9 84.7 %gather.1 = (bf16[1280,512]{1,0:T(8,128)(2,1)}, bf16[2048,1024]{1,0:T(8,128)(2,1)}, bf16[1024,3072]{1,0:T(8,128)(2,1)}, bf16[1024,3072]{1,0:T(8,128)(2,1)}, bf16...) custom-call(bf16[80,512]{1,0:T(8,128)(2,1)} %pad_maximum_fusion.2.refs_0_, bf16[128,1024]{1,0:T(8,128)(2,1)} %refs_1_.1, ...), custom_call_target="tpu_custom_call" | custom-call | tf_op jit(solution)/shard_map/gather/pallas_call | solution.py:271
  93.6 23.2 %attend.1 = (bf16[1024,512]{1,0:T(8,128)(2,1)}, f32[16,512]{1,0:T(8,128)}, bf16[2,1536,128]{2,1,0:T(8,128)(2,1)}, bf16[1536,128]{1,0:T(8,128)(2,1)}, bf16[1536,1...) custom-call(bf16[1536,1152]{1,0:T(8,128)(2,1)} %get-tuple-element.40, ...), custom_call_target="tpu_custom_call" | custom-call | tf_op jit(solution)/shard_map/attend/pallas_call | solution.py:507
  116.8 15.6 %spread1.1 = bf16[192,2048]{1,0:T(8,128)(2,1)} custom-call(bf16[1536,256]{1,0:T(8,128)(2,1)} %get-tuple-element.42.src), custom_call_target="tpu_custom_call" | custom-call | tf_op jit(solution)/shard_map/spread1/pallas_call | solution.py:305
  132.5 3.7 multiply_reduce_fusion.2
  137.1 1.4 fusion.19
  139.9 1.4 fusion.20
  141.8 3.2 multiply_convert_fusion
  145.0 2.2 fusion.5
  147.2 2.2 fusion.21
  149.4 2.4 multiply_reduce_fusion
  152.2 2.4 convolution_convert_fusion.4.src
  154.6 15.2 %spread2.1.dh = bf16[1536,256]{1,0:T(8,128)(2,1)} custom-call(bf16[192,2048]{1,0:T(8,128)(2,1)} %convolution_convert_fusion.4.src), custom_call_target="tpu_custom_call" | custom-call | tf_op jit(solution)/shard_map/spread2/pallas_call | solution.py:305
  169.8 32.5 %attend_back.1 = (f32[1024,512]{1,0:T(8,128)}, bf16[1536,1024]{1,0:T(8,128)(2,1)}, f32[8,1024]{1,0:T(8,128)}) custom-call(bf16[1536,1152]{1,0:T(8,128)(2,1)} %get-tuple-element.40.x, bf16[1024,512]{1,0:T(8,128)(2,1)} %get-tuple-element.48.w, f32[16,512]{1,0:T(8,128)} %get-tuple-element.44.gains, bf16[2,1536,128]{2,1,0:T(8,128)(2,1)} %get-tuple-element.49.q, ...), custom_call_target="tpu_custom_call" | custom-call | tf_op jit(solution)/shard_map/attend_back/pallas_call | solution.py:517
  203.6 1.7 convert.24
  205.4 1.2 pad_maximum_fusion.dw
  206.6 56.6 %last_sums.1 = (bf16[8,80,512]{2,1,0:T(8,128)(2,1)}, f32[192,1024]{1,0:T(8,128)}) custom-call(bf16[2,4,2,80,512]{4,3,2,1,0:T(8,128)(2,1)} %pad_maximum_fusion.dw, bf16[1536,1024]{1,0:T(8,128)(2,1)} %get-tuple-element.60.dn), custom_call_target="tpu_custom_call" | custom-call | tf_op jit(solution)/shard_map/last_sums/pallas_call | solution.py:728
  263.2 1.4 fusion.9
  264.7 2.2 fusion.8
  269.8 4.5 %convolution_convert_fusion.2 = bf16[1024,3072]{1,0:T(8,128)(2,1)} fusion(bf16[192,1024]{1,0:T(8,128)(2,1)S(1)} %multiply_convert_fusion.2, bf16[192,3072]{1,0:T(8,128)(2,1)S(1)} %copy-done.11), kind=kOutput, calls=%fused_computation.2 | convolution fusion | flops 1211105280 | bytes 7864320 | tf_op jit(solution)/shard_map/dot_general | solution.py:319
  274.4 4.5 %convolution_convert_fusion.1 = bf16[1024,3072]{1,0:T(8,128)(2,1)} fusion(bf16[192,1024]{1,0:T(8,128)(2,1)S(1)} %multiply_convert_fusion.2, bf16[192,3072]{1,0:T(8,128)(2,1)S(1)} %get-tuple-element.73), kind=kOutput, calls=%fused_computation.1 | convolution fusion | flops 1211105280 | bytes 7864320 | tf_op jit(solution)/shard_map/dot_general | solution.py:319
  278.8 4.5 %convolution_convert_fusion = bf16[3072,1024]{1,0:T(8,128)(2,1)} fusion(bf16[192,3072]{1,0:T(8,128)(2,1)S(1)} %copy-done.8, bf16[1,192,1024]{2,1,0:T(8,128)(2,1)S(1)} %copy-done.9), kind=kOutput, calls=%fused_computation | convolution fusion | flops 1211105280 | bytes 7864320 | tf_op jit(solution)/shard_map/dot_general | solution.py:319
  283.3 3.3 convolution_convert_fusion.3
  286.6 93.4 %sum_all.1 = (bf16[64,3072]{1,0:T(8,128)(2,1)}, bf16[64,3072]{1,0:T(8,128)(2,1)}, bf16[192,1024]{1,0:T(8,128)(2,1)}, bf16[128,1024]{1,0:T(8,128)(2,1)}) custom-call(bf16[2,4,2,64,3072]{4,3,2,1,0:T(8,128)(2,1)} %bitcast.71, bf16[2,4,2,64,3072]{4,3,2,1,0:T(8,128)(2,1)} %bitcast.72, bf16[2,4,2,192,1024]{4,3,2,1,0:T(8,128)(2,1)} %bitcast.73, ...), custom_call_target="tpu_custom_call" | custom-call | tf_op jit(solution)/shard_map/sum_all/pallas_call | solution.py:676
  380.0 1.8 convert_element_type.84
  381.9 1.9 convert_element_type.85
  383.8 1.9 convert_element_type.86
  385.7 1.0 convert_element_type.87
  386.7 0.9 slice_reduce_fusion
  (81 shorter events, 12.2 us)
Async XLA Ops:
  0.6 5.0 %copy-start = (bf16[64,2048]{1,0:T(8,128)(2,1)S(1)}, bf16[64,2048]{1,0:T(8,128)(2,1)}, u32[]{:S(2)}) copy-start(bf16[64,2048]{1,0:T(8,128)(2,1)} %param.18) | copy-start | bytes 786436
  93.6 38.8 %copy-start.5 = (bf16[1,192,1024]{2,1,0:T(8,128)(2,1)S(1)}, bf16[1,192,1024]{2,1,0:T(8,128)(2,1)}, u32[]{:S(2)}) copy-start(bf16[1,192,1024]{2,1,0:T(8,128)(2,1)} %param.16) | copy-start | bytes 1179652
  132.4 4.6 %copy-start.3 = (bf16[1024,3072]{1,0:T(8,128)(2,1)S(1)}, bf16[1024,3072]{1,0:T(8,128)(2,1)}, u32[]{:S(2)}) copy-start(bf16[1024,3072]{1,0:T(8,128)(2,1)} %get-tuple-element.45) | copy-start | bytes 18874372
  136.9 2.2 slice-start
  137.1 2.8 slice-start.1
  137.1 4.2 %slice-start.2 = ((s8[6291456]{0:T(1024)(128)(4,1)}), s8[4194304]{0:T(1024)(128)(4,1)S(1)}, s32[]{:S(2)}) async-start(s8[6291456]{0:T(1024)(128)(4,1)} %bitcast.86), calls=%async_computation.2 | async-start | bytes 8388608
  138.6 3.2 slice-start.3
  139.9 2.0 copy-start.9
  145.0 2.2 copy-start.7
  145.0 2.2 copy-start.10
  149.4 2.7 copy-start.2
  263.2 3.7 copy-start.12
  267.1 1.2 copy-start.6
  267.1 2.7 copy-start.11
  274.4 4.5 %copy-start.8 = (bf16[192,3072]{1,0:T(8,128)(2,1)S(1)}, bf16[192,3072]{1,0:T(8,128)(2,1)}, u32[]{:S(2)}) copy-start(bf16[192,3072]{1,0:T(8,128)(2,1)} %copy-done.7) | copy-start | bytes 3538948
  278.8 4.5 %copy-start.4 = (bf16[192,2048]{1,0:T(8,128)(2,1)S(1)}, bf16[192,2048]{1,0:T(8,128)(2,1)}, u32[]{:S(2)}) copy-start(bf16[192,2048]{1,0:T(8,128)(2,1)} %spread1.1) | copy-start | bytes 2359300
  286.6 102.1 %copy-start.1 = (bf16[64,2048]{1,0:T(8,128)(2,1)S(1)}, bf16[64,2048]{1,0:T(8,128)(2,1)}, u32[]{:S(2)}) copy-start(bf16[64,2048]{1,0:T(8,128)(2,1)} %param.18) | copy-start | bytes 786436
  380.0 5.7 %copy-start.13 = (bf16[192,1024]{1,0:T(8,128)(2,1)S(1)}, bf16[192,1024]{1,0:T(8,128)(2,1)}, u32[]{:S(2)}) copy-start(bf16[192,1024]{1,0:T(8,128)(2,1)} %get-tuple-element.66) | copy-start | bytes 1179652

commit v2 on v1

--- a/solution.py
+++ b/solution.py
@@ -61,9 +61,24 @@
     pl.semaphore_wait(sem, len(devices))
 
 
+class Copy:
+    def __init__(self, copy, made_by):
+        self.copy, self.made_by = copy, made_by
+        if not made_by.again:
+            copy.start()
+
+    def wait_recv(self):
+        if not self.made_by.again:
+            self.copy.wait_recv()
+
+    def wait(self):
+        if not self.made_by.again:
+            self.copy.wait()
+
+
 class Wire:
-    def __init__(self, send, recv):
-        self.send, self.recv, self.n, self.all = send, recv, 0, []
+    def __init__(self, send, recv, again=False):
+        self.send, self.recv, self.n, self.all, self.again = send, recv, 0, [], again
 
     def __call__(self, src, dst, device):
         i = self.n
@@ -71,9 +86,8 @@
         copy = pltpu.make_async_remote_copy(
             src_ref=src, dst_ref=dst, send_sem=self.send.at[i], recv_sem=self.recv.at[i],
             device_id=device, device_id_type=MESH)
-        copy.start()
         self.all.append(copy)
-        return copy
+        return Copy(copy, self)
 
     def finish(self):
         for copy in self.all:
@@ -81,14 +95,13 @@
 
 
 class Local:
-    def __init__(self, sems):
-        self.sems, self.n = sems, 0
+    def __init__(self, sems, again=False):
+        self.sems, self.n, self.again = sems, 0, again
 
     def __call__(self, src, dst):
-        copy = pltpu.make_async_copy(src, dst, self.sems.at[self.n])
+        i = self.n
         self.n += 1
-        copy.start()
-        return copy
+        return Copy(None if self.again else pltpu.make_async_copy(src, dst, self.sems.at[i]), self)
 
 
 def sems(wires, local):
@@ -98,7 +111,7 @@
 def talking(number, name, **more):
     return dict(
         compiler_params=pltpu.CompilerParams(
-            collective_id=number, has_side_effects=True, vmem_limit_bytes=60 << 20),
+            collective_id=number, has_side_effects=True, vmem_limit_bytes=63 << 20),
         name=name, **more)
 def quarters(rows):
     if rows % 64 == 0:
@@ -226,87 +239,140 @@
                 self.got(name)
 
 
-def gather_kernel(nw, *refs):
-    srcs, rows = refs[:nw], refs[nw]
-    outs, rows_out = refs[nw + 1:2 * nw + 1], refs[2 * nw + 1]
-    send, recv, local = refs[2 * nw + 2:]
+class Later:
+    def __init__(self, steps):
+        self.steps = list(steps)
+
+    def __call__(self):
+        if self.steps:
+            self.steps.pop(0)()
+
+    def rest(self):
+        while self.steps:
+            self()
+
+
+def stage(flow, *numbers):
+    def go():
+        for s in numbers:
+            flow.stage(s)
+    return go
+
+
+def together(*steps):
+    def go():
+        for s in steps:
+            s()
+    return go
+
+
+class Spread:
+    def __init__(self, net, wire, here, forward, src, dst):
+        rows, cols = (dst.shape[0], src.shape[1]) if forward else (src.shape[0], dst.shape[1])
+
+        def by_row(ref, c):
+            return ref.at[pl.ds(pl.multiple_of(c * rows, 16), rows)]
+
+        def by_col(ref, c):
+            return ref.at[:, pl.ds(pl.multiple_of(c * cols, 128), cols)]
+
+        pick, put = (by_row, by_col) if forward else (by_col, by_row)
+        self.copies = []
+        for o in (6, 2, 4, 5, 7, 1, 3):
+            there = net.ctx(o)
+            self.copies.append(wire(pick(src, there), put(dst, net.c), (net.f, there)))
+        self.own = here(pick(src, net.c), put(dst, net.c))
+
+    def end(self):
+        for copy in self.copies:
+            copy.wait_recv()
+        self.own.wait()
+
+
+def neighbours(net):
+    return ([net.sib] + [net.along(d, o) for d in "yz" for o in (1, 2, 3)] + [(net.f, net.ctx(o)) for o in (1, 2, 3, 5, 6, 7)])
+
+
+KEPT = 11
+
+
+def forward_kernel(nw, *refs):
+    srcs, rows, cos_in, sin_in = refs[:nw], refs[nw], refs[nw + 1], refs[nw + 2]
+    refs = refs[nw + 3:]
+    outs, rows_out, own_heads, kept_out = refs[:nw - 1], refs[nw - 1], refs[nw], refs[nw + 1:nw + 1 + KEPT]
+    refs = refs[nw + 1 + KEPT:]
+    x, t, cos_at, sin_at, heads = refs[:5]
+    kept = refs[5:5 + KEPT]
+    send, recv, local = refs[5 + KEPT:]
+    w, gains, q, k, v, lin, cs, sn, start, hf, inv = kept
     net, wire, here = Net(), Wire(send, recv), Local(local)
-    barrier([net.yp, net.ym, net.zp, net.zm, net.sib, net.xp, net.xm, net.peer])
-    flows = [WeightFlow(net, wire, s, o, i == 0) for i, (s, o) in enumerate(zip(srcs, outs))]
-    seq = RowFlow(net, wire, rows, rows_out)
-    flows[0].stage(0)
+    barrier(neighbours(net))
+    flows = [WeightFlow(net, wire, s, o, i == 0) for i, (s, o) in enumerate(zip(srcs, (t, *outs)))]
+    first, seq = flows[0], RowFlow(net, wire, rows, x)
+    first.stage(0)
     seq.stage(0)
     flows[1].stage(0)
-    kept = [here(fl.src, fl.place(0, 0)) for fl in flows]
-    kept.append(here(rows, seq.place(net.c)))
-    flows[0].stage(1)
+    tables_in = [here(cos_in, cos_at), here(sin_in, sin_at)]
+    placed_here = [here(fl.src, fl.place(0, 0)) for fl in flows]
+    placed_here.append(here(rows, seq.place(net.c)))
+    first.stage(1)
     flows[2].stage(0)
     seq.stage(1)
-    flows[0].stage(2)
+    first.stage(2)
     flows[1].stage(1)
     seq.stage(2)
-    flows[0].stage(3)
-    flows[0].stage(4)
-    for s in range(2, nw + 3):
-        if s + 1 < nw:
-            flows[s + 1].stage(0)
-        if s < nw:
-            flows[s].stage(1)
-        if s == 2:
-            seq.stage(3)
-        if s - 1 < nw:
-            flows[s - 1].stage(2)
-        if 1 <= s - 2 < nw:
-            flows[s - 2].stage(3)
-            flows[s - 2].stage(4)
-    for h in kept:
-        h.wait()
+    first.stage(3)
+    flows[3].stage(0)
+    first.stage(4)
+    flows[2].stage(1)
+    flows[1].stage(2)
+    seq.stage(3)
+    for c in tables_in + placed_here:
+        c.wait()
+    saved = [here(x, rows_out)]
+    tick = Later([
+        together(stage(flows[4], 0), stage(flows[1], 3)),
+        together(stage(flows[3], 1), stage(flows[2], 2)),
+        stage(flows[2], 3),
+        together(stage(flows[4], 1), stage(flows[3], 2)),
+        stage(flows[3], 3),
+        stage(flows[4], 2),
+    ])
+    attn_forward(tick, x, t, cos_at, sin_at, w, gains, q, k, v, lin, cs, sn, start, hf, heads, inv)
+    spread = Spread(net, wire, here, True, heads, own_heads)
+    saved += [here(a, b) for a, b in zip(kept, kept_out)]
+    tick.rest()
+    flows[4].stage(3)
+    for fl in flows[1:]:
+        fl.stage(4)
+    spread.end()
+    for c in saved:
+        c.wait()
     wire.finish()
 
 
-def gather(weights, rows):
+def shapes(*items):
+    return [jax.ShapeDtypeStruct(s, d) for s, d in items]
+
+
+def forward(weights, rows, cos_in, sin_in):
     nw = len(weights)
-    outs = [jax.ShapeDtypeStruct((16 * w.shape[0], w.shape[1]), w.dtype) for w in weights]
-    outs.append(jax.ShapeDtypeStruct((8 * rows.shape[0], rows.shape[1]), rows.dtype))
+    per, cols = weights[0].shape
+    length = 8 * rows.shape[0]
+    kept = shapes(
+        ((16 * (per - 16), cols), BF16), ((16, cols), F32), ((2, length, HEAD), BF16), ((length, HEAD), BF16),
+        ((length, HEAD), BF16), ((length, 3 * HEAD), F32), ((length, HEAD), F32), ((length, HEAD), F32),
+        ((length, HEAD), F32), ((length, 2 * HEAD), F32), ((2, length, HEAD), F32))
+    outs = [jax.ShapeDtypeStruct((16 * w.shape[0], w.shape[1]), w.dtype) for w in weights[1:]]
+    outs += shapes(((length, rows.shape[1]), BF16), ((rows.shape[0], 16 * HEAD), BF16)) + kept
+    scratch = [((length, rows.shape[1]), BF16), ((16 * per, cols), BF16), ((length, HEAD), F32), ((length, HEAD), F32), ((length, 2 * HEAD), BF16)]
     res = pl.pallas_call(
-        functools.partial(gather_kernel, nw),
-        out_shape=outs, in_specs=[ANY] * (nw + 1), out_specs=[ANY] * len(outs),
-        scratch_shapes=sems(27 * nw + 9, nw + 1), **talking(0, "gather"),
-    )(*weights, rows)
-    return res[:nw], res[nw]
-
-
-def spread_kernel(forward, src, dst, send, recv, local):
-    net, wire, here = Net(), Wire(send, recv), Local(local)
-    barrier([(net.f, net.ctx(o)) for o in range(1, 8)])
-    rows, cols = (dst.shape[0], src.shape[1]) if forward else (src.shape[0], dst.shape[1])
-
-    def by_row(ref, c):
-        return ref.at[pl.ds(pl.multiple_of(c * rows, 16), rows)]
-
-    def by_col(ref, c):
-        return ref.at[:, pl.ds(pl.multiple_of(c * cols, 128), cols)]
-
-    pick, put = (by_row, by_col) if forward else (by_col, by_row)
-    copies = []
-    for o in (4, 6, 2, 5, 7, 1, 3):
-        there = net.ctx(o)
-        copies.append(wire(pick(src, there), put(dst, net.c), (net.f, there)))
-    own = here(pick(src, net.c), put(dst, net.c))
-    for copy in copies:
-        copy.wait_recv()
-    own.wait()
-    wire.finish()
-
-
-def spread(forward, src, number):
-    a, b = src.shape
-    shape = (a // 8, b * 8) if forward else (a * 8, b // 8)
-    return pl.pallas_call(
-        functools.partial(spread_kernel, forward),
-        out_shape=jax.ShapeDtypeStruct(shape, src.dtype), in_specs=[ANY], out_specs=ANY,
-        scratch_shapes=sems(7, 1), **talking(number, "spread%d" % number),
-    )(src)
+        functools.partial(forward_kernel, nw),
+        out_shape=outs, in_specs=[ANY] * (nw + 3), out_specs=[ANY] * len(outs),
+        scratch_shapes=[pltpu.VMEM(s, d) for s, d in scratch] + [pltpu.VMEM(a.shape, a.dtype) for a in kept]
+        + sems(27 * nw + 9 + 7, nw + 3 + 1 + 1 + KEPT), **talking(0, "layer_forward"),
+    )(*weights, rows, cos_in, sin_in)
+    return res[:nw - 1], res[nw - 1], res[nw], res[nw + 1:]
 def block(i, size):
     return pl.ds(pl.multiple_of(i * size, size), size)
 
@@ -331,7 +397,7 @@
 ROWS = 256
 
 
-def attn_forward(x, t, cos_in, sin_in, w, gains, q, k, v, lin, cs, sn, start, hf, heads, inv):
+def attn_forward(tick, x, t, cos_in, sin_in, w, gains, q, k, v, lin, cs, sn, start, hf, heads, inv):
     length, width = x.shape[0], x.shape[1] - HEAD
     per = t.shape[0] // 16
     depth = per - 16
@@ -380,7 +446,9 @@
                 k[rows, :] = e
         return carry
 
-    lax.fori_loop(0, length // ROWS, prepare, 0)
+    for i in range(0, length // ROWS, 2):
+        lax.fori_loop(i, i + 2, prepare, 0)
+        tick()
 
     def queries(i, carry):
         rows = block(i, ROWS)
@@ -406,7 +474,9 @@
             heads[rows, h * HEAD:(h + 1) * HEAD] = part.astype(BF16)
         return carry
 
-    lax.fori_loop(0, length // ROWS, queries, 0)
+    for i, j in ((0, 3), (3, 4), (4, 5), (5, 6)):
+        lax.fori_loop(i, j, queries, 0)
+        tick()
 
 
 def allowed_at(i, j, begin):
@@ -416,12 +486,9 @@
     return ((other.astype(F32) >= begin) & (other <= own))[None]
 
 
-def attn_backward(x, w, gains, q, k, v, lin, cs, sn, start, hf, inv, dh, dw, dn, dg, dq, dk, dv, delta, dlin):
-    length, width = x.shape[0], x.shape[1] - HEAD
+def attn_backward(tick, gains, q, k, v, start, hf, inv, dh, dq, dk, dv, delta):
+    length = dh.shape[0]
     blocks = length // ROWS
-    g = gains[...]
-    attn_gain = jnp.concatenate([g[0:1], g[1:2]], axis=1)
-    query_gain, key_gain = g[4:5, 0:HEAD], g[4:5, HEAD:2 * HEAD]
 
     def before(i, carry):
         rows = block(i, ROWS)
@@ -459,11 +526,23 @@
         dv[these, :] = d_value
         return carry
 
-    lax.fori_loop(0, blocks, keys, 0)
+    for i, j in ((0, 1), (1, 2), (2, 4), (4, 6)):
+        lax.fori_loop(i, j, keys, 0)
+        tick()
+
+
+WIDE = 384
+
+
+def attn_backward_end(x, w, gains, lin, cs, sn, dq, dk, dv, dlin, dw, dn):
+    length, width = x.shape[0], x.shape[1] - HEAD
+    g = gains[...]
+    attn_gain = jnp.concatenate([g[0:1], g[1:2]], axis=1)
+    query_gain, key_gain = g[4:5, 0:HEAD], g[4:5, HEAD:2 * HEAD]
 
     def after(i, carry):
         d_attn, d_query, d_key = carry
-        rows = block(i, ROWS)
+        rows = block(i, WIDE)
         cosine, sine = cs[rows, :], sn[rows, :]
         for h in range(3):
             cols = slice(h * HEAD, (h + 1) * HEAD)
@@ -479,7 +558,7 @@
         part = dot_t(dlin[rows, :], w[...])
         e = unit(x[rows, :width].astype(F32))[0]
         d_attn = d_attn + jnp.sum(part * e, axis=0, keepdims=True)
-        dn[rows, :] = part.astype(BF16)
+        dn[i // 2, pl.ds((i % 2) * 2, 2)] = part.astype(BF16).reshape(2, WIDE // 2, width)
         normed = (e * attn_gain).astype(BF16)
 
         part = t_dot(normed, dlin[rows, :])
@@ -488,41 +567,19 @@
 
     zero = jnp.zeros((1, HEAD), F32)
     dw[...] = jnp.zeros_like(dw)
-    d_attn, d_query, d_key = lax.fori_loop(0, blocks, after, (jnp.zeros((1, width), F32), zero, zero))
-    dg[0:1, :] = d_attn
-    dg[1:2, :] = jnp.concatenate([d_query, d_key, jnp.zeros((1, width - 2 * HEAD), F32)], axis=1)
+    return lax.fori_loop(0, length // WIDE, after, (jnp.zeros((1, width), F32), zero, zero))
 
 
 def shapes(*items):
     return [jax.ShapeDtypeStruct(s, d) for s, d in items]
 
 
-def attend(x, t, cos_in, sin_in):
-    length = x.shape[0]
-    out = shapes(
-        ((16 * (t.shape[0] // 16 - 16), t.shape[1]), BF16), ((16, t.shape[1]), F32),
-        ((2, length, HEAD), BF16), ((length, HEAD), BF16), ((length, HEAD), BF16), ((length, 3 * HEAD), F32),
-        ((length, HEAD), F32), ((length, HEAD), F32), ((length, HEAD), F32), ((length, 2 * HEAD), F32),
-        ((length, 2 * HEAD), BF16), ((2, length, HEAD), F32))
-    return pl.pallas_call(
-        attn_forward, out_shape=out, in_specs=[VM] * 4, out_specs=[VM] * len(out),
-        compiler_params=pltpu.CompilerParams(vmem_limit_bytes=56 << 20), name="attend")(x, t, cos_in, sin_in)
-
-
-def attend_back(x, kept, dh):
-    w, gains, q, k, v, lin, cs, sn, start, hf, _, inv = kept
-    length, width = x.shape[0], x.shape[1] - HEAD
-    out = shapes((w.shape, F32), ((length, width), BF16), ((8, width), F32))
-    args = (x, w, gains, q, k, v, lin, cs, sn, start, hf, inv, dh)
-    return pl.pallas_call(
-        attn_backward, out_shape=out, in_specs=[VM] * len(args), out_specs=[VM] * len(out),
-        scratch_shapes=[
-            pltpu.VMEM((2, length, HEAD), F32), pltpu.VMEM((length, HEAD), F32), pltpu.VMEM((length, HEAD), F32),
-            pltpu.VMEM((2, length, HEAD), F32), pltpu.VMEM((length, 4 * HEAD), BF16)],
-        compiler_params=pltpu.CompilerParams(vmem_limit_bytes=60 << 20), name="attend_back")(*args)
 def add_rows(out, parts, rows, step):
     def some(r, carry):
         here = pl.ds(pl.multiple_of(r * step, 16), step)
+        if len(parts) == 2:
+            out(here, parts[0](here) + parts[1](here))
+            return carry
         total = parts[0](here).astype(F32)
         for part in parts[1:]:
             total = total + part(here).astype(F32)
@@ -532,11 +589,14 @@
     lax.fori_loop(0, rows // step, some, 0)
 
 
+FIRST = (2, 1, 3, 0)
+
+
 class SumFlow:
-    def __init__(self, net, wire, here, src, first, order, mine, other, got, part, fin, out):
+    def __init__(self, net, wire, here, src, first, order, slots, other, got, part, fin, out):
         self.net, self.wire, self.here, self.src, self.first, self.order = net, wire, here, src, first, order
-        self.mine, self.other, self.got, self.part, self.fin, self.out = mine, other, got, part, fin, out
-        self.rows, self.cols = mine.shape[2], mine.shape[3]
+        self.slots, self.other, self.got, self.part, self.fin, self.out = slots, other, got, part, fin, out
+        self.rows, self.cols = other.shape[2], other.shape[3]
         self.w = self.cols // 8
         self.far = {}
 
@@ -558,12 +618,20 @@
     def begin(self):
         n, dim = self.net, self.order[0]
         self.near, self.own = {}, {}
-        for o in (2, 1, 3, 0):
+        for o in FIRST:
             d = (n.at(dim) + o) % 4
             self.near[o] = self.wire(self.cut(self.src, dim, d, 1 - n.k), self.cut(self.other, dim, d), n.sib)
-            self.own[o] = self.here(self.cut(self.src, dim, d, n.k), self.cut(self.mine, dim, d))
+        self.bring(0)
+        self.bring(1)
+
+    def bring(self, i):
+        n, dim = self.net, self.order[0]
+        d = (n.at(dim) + FIRST[i]) % 4
+        self.own[FIRST[i]] = self.here(self.cut(self.src, dim, d, n.k), self.slots.at[i % 2])
 
     def add(self, out, parts):
+        if self.wire.again:
+            return
         a, b = out.shape[0], out.shape[1]
         step = 16
         for i in range(a):
@@ -580,14 +648,17 @@
         d = (n.at(dim) + o) % 4
         self.near[o].wait_recv()
         self.own[o].wait()
-        piece = self.cut(self.mine, dim, d)
-        self.add(piece, [piece, self.cut(self.other, dim, d)])
+        i = FIRST.index(o)
+        piece = self.cut(self.other, dim, d)
+        self.add(piece, [piece, self.slots.at[i % 2]])
+        if i + 2 < 4:
+            self.bring(i + 2)
         if o:
             self.far[o] = self.wire(piece, self.got[0].at[o - 1], n.along(dim, o))
 
     def phase(self, p):
         n, dim = self.net, self.order[p]
-        held = self.mine if p == 0 else self.part[p - 1]
+        held = self.other if p == 0 else self.part[p - 1]
         for o in (1, 3, 2):
             self.far[o].wait_recv()
         result = self.part[p] if p < 2 else self.fin
@@ -598,11 +669,21 @@
                 d = (n.at(after) + o) % 4
                 self.far[o] = self.wire(self.cut(result, after, d), self.got[p + 1].at[o - 1], n.along(after, o))
         else:
-            s = n.c if self.order == "zyx" else n.x * 2 + n.zh
-            to = self.out.at[pl.ds(self.first, self.rows), pl.ds(pl.multiple_of(s * self.w, 128), self.w)]
-            fin = self.fin.at[0, 0]
-            self.last = [self.wire(fin, to, (n.f, n.ctx(o))) for o in (4, 6, 2, 5, 7, 1, 3)]
+            fin, to = self.fin.at[0, 0], self.place(n.zh)
+            self.across = self.wire(fin, to, n.peer)
+            self.last = [self.wire(fin, to, n.along("x", o)) for o in (2, 1, 3)]
             self.kept = self.here(fin, to)
+
+    def place(self, zh):
+        n = self.net
+        s = zh * 4 + n.x if self.order == "zyx" else n.x * 2 + zh
+        return self.out.at[pl.ds(self.first, self.rows), pl.ds(pl.multiple_of(s * self.w, 128), self.w)]
+
+    def share(self):
+        n = self.net
+        self.across.wait_recv()
+        to = self.place(1 - n.zh)
+        self.last += [self.wire(to, to, n.along("x", o)) for o in (2, 1, 3)]
 
     def end(self):
         for copy in self.last:
@@ -623,13 +704,11 @@
     return out
 
 
-PLAN = ((0, 0, 64, "yxz"), (1, 0, 64, "xzy"), (2, 0, 192, "zyx"),
-        (3, 0, 48, "yxz"), (3, 48, 48, "xzy"), (3, 96, 32, "zyx"))
-
-
-def everyone(net):
-    return ([net.sib] + [net.along(d, o) for d in "yxz" for o in (1, 2, 3)]
-            + [(net.f, (1 - net.zh) * 4 + (net.x + o) % 4) for o in (1, 2, 3)])
+PLAN = ((0, 0, 64, "yxz"), (1, 0, 64, "yxz"), (2, 0, 192, "zyx"), (3, 0, 64, "xzy"), (3, 64, 64, "zyx"))
+
+
+def first_shapes(plan, shapes_in):
+    return [sum_shapes(rows, shapes_in[which][-1], order)[0] for which, _, rows, order in plan]
 
 
 def sum_scratch(plan, shapes_in):
@@ -637,100 +716,187 @@
     for which, first, rows, order in plan:
         cols = shapes_in[which][-1]
         a, b, c = sum_shapes(rows, cols, order)
-        full = (2, 4, rows, cols)
-        held += [pltpu.VMEM(s, BF16) for s in (full, full, (3, *a), (3, *b), (3, *c), a, b, c)]
+        held += [pltpu.VMEM(s, BF16) for s in ((2, 4, rows, cols), (3, *a), (3, *b), (3, *c), a, b, c)]
     return held
 
 
-def make_flows(net, wire, here, plan, srcs, outs, held):
+def make_flows(net, wire, here, plan, srcs, outs, held, slots):
     flows = []
     for n, (which, first, rows, order) in enumerate(plan):
-        mine, other, g0, g1, g2, p0, p1, fin = held[8 * n:8 * n + 8]
-        flows.append(SumFlow(net, wire, here, srcs[which], first, order, mine, other, (g0, g1, g2), (p0, p1), fin, outs[which]))
+        other, g0, g1, g2, p0, p1, fin = held[7 * n:7 * n + 7]
+        flows.append(SumFlow(net, wire, here, srcs[which], first, order, slots[n], other, (g0, g1, g2), (p0, p1), fin, outs[which]))
     return flows
 
 
-def sum_kernel(plan, count, *refs):
-    srcs, outs = refs[:count], refs[count:2 * count]
-    held, (send, recv, local) = refs[2 * count:-3], refs[-3:]
-    net, wire, here = Net(), Wire(send, recv), Local(local)
-    barrier(everyone(net))
-    flows = make_flows(net, wire, here, plan, srcs, outs, held)
+class Ends:
+    def __init__(self, net, wire, here, dwx, dn, rows_out, dn_out, other, got, fin, got_x, part, got_z):
+        self.net, self.wire, self.here, self.dwx, self.dn, self.rows_out, self.dn_out = net, wire, here, dwx, dn, rows_out, dn_out
+        self.other, self.got, self.fin, self.got_x, self.part, self.got_z = other, got, fin, got_x, part, got_z
+
+    def begin(self):
+        n = self.net
+        self.moved = {o: self.wire(self.dn.at[:, (n.x + o) % 4], self.got_x.at[o - 1], n.along("x", o)) for o in (2, 1, 3)}
+        self.near = self.wire(self.dwx.at[:, :, 1 - n.k], self.other, n.sib)
+
+    def chip(self):
+        n = self.net
+        self.near.wait_recv()
+        for a in range(2):
+            for b in range(4):
+                self.other[a, b] = self.other[a, b] + self.dwx[a, b, n.k]
+        self.far = []
+        for dz in (1, 0):
+            for dy in (2, 1, 3, 0):
+                if dz or dy:
+                    there = ((n.zl + dz) % 2, (n.y + dy) % 4)
+                    self.far.append(self.wire(self.other.at[there[0], there[1]], self.got.at[dz * 4 + dy - 1], (fid(there[0], there[1], n.k), n.c)))
+
+    def along_x(self):
+        n = self.net
+        for copy in self.moved.values():
+            copy.wait_recv()
+
+        for zh in range(2):
+            def take(o):
+                return (lambda here: self.dn[zh, n.x, here, :]) if o == 0 else (lambda here: self.got_x[o - 1, zh, here, :])
+
+            def put(here, value):
+                self.part[zh, here, :] = value
+            add_rows(put, [take(o) for o in range(4)], self.part.shape[1], 16)
+        self.over = self.wire(self.part.at[1 - n.zh], self.got_z, n.peer)
+
+    def share(self):
+        n = self.net
+        for copy in self.far:
+            copy.wait_recv()
+        total = self.other[n.zl, n.y].astype(F32)
+        for i in range(7):
+            total = total + self.got[i].astype(F32)
+        self.fin[...] = total.astype(BF16)
+        self.copies = [self.wire(self.fin, self.rows_out.at[n.c], (n.f, n.ctx(o))) for o in (6, 2, 4, 5, 7, 1, 3)]
+        self.kept = self.here(self.fin, self.rows_out.at[n.c])
+
+    def end(self):
+        n = self.net
+        self.over.wait_recv()
+
+        def some(r, carry):
+            at = pl.ds(pl.multiple_of(r * 16, 16), 16)
+            self.dn_out[at, :] = self.part[n.zh, at, :].astype(F32) + self.got_z[at, :].astype(F32)
+            return carry
+
+        lax.fori_loop(0, self.got_z.shape[0] // 16, some, 0)
+        for copy in self.copies:
+            copy.wait_recv()
+        self.kept.wait()
+
+
+def backward_kernel(ng, *refs):
+    srcs, x_in, d_heads, mlp_rows, kept_in = refs[:ng], refs[ng], refs[ng + 1], refs[ng + 2], refs[ng + 3:ng + 3 + KEPT]
+    refs = refs[ng + 3 + KEPT:]
+    outs, rows_out, dn_out = refs[:ng], refs[ng], refs[ng + 1]
+    refs = refs[ng + 2:]
+    kept, refs = refs[:KEPT], refs[KEPT:]
+    w, gains, q, k, v, lin, cs, sn, start, hf, inv = kept
+    dh, dq, dk, dv, delta, mlp_at, dwx, dn = refs[:8]
+    end_held, refs = refs[8:14], refs[14:]
+    held, (send, recv, local) = refs[:-3], refs[-3:]
+    net = Net()
+    length, width = x_in.shape[0], x_in.shape[1] - HEAD
+    depth = w.shape[0] // 16
+
+    def slotted(*slots):
+        wire, here = Wire(send, recv), Local(local)
+        barrier(neighbours(net))
+        spread = Spread(net, wire, here, False, d_heads, dh)
+        flows = make_flows(net, wire, here, PLAN, srcs, outs, held, slots)
+        for fl in flows:
+            fl.begin()
+        loads = [here(a, b) for a, b in zip(kept_in, kept)] + [here(mlp_rows, mlp_at)]
+        for fl in flows:
+            fl.chip(2)
+        for c in loads:
+            c.wait()
+        spread.end()
+
+        def chips(o):
+            def go():
+                for fl in flows:
+                    fl.chip(o)
+            return go
+
+        tick = Later([chips(1), chips(3), chips(0)])
+        attn_backward(tick, gains, q, k, v, start, hf, inv, dh, dq, dk, dv, delta)
+        tick.rest()
+
+    pl.run_scoped(slotted, *[pltpu.VMEM((2, *a), BF16) for a in first_shapes(PLAN, [s.shape for s in srcs])])
+    wire, here = Wire(send, recv, True), Local(local, True)
+    Spread(net, wire, here, False, d_heads, dh)
+    flows = make_flows(net, wire, here, PLAN, srcs, outs, held, held[1::7])
     for fl in flows:
         fl.begin()
+    for a, b in list(zip(kept_in, kept)) + [(mlp_rows, mlp_at)]:
+        here(a, b)
     for o in (2, 1, 3, 0):
         for fl in flows:
             fl.chip(o)
-    for p in range(3):
-        for fl in flows:
-            fl.phase(p)
+    wire.again = here.again = False
+    ends = Ends(net, wire, here, dwx, dn, rows_out, dn_out, *end_held)
+
+    def ending(x, dlin, dw):
+        fetch = pltpu.make_async_copy(x_in, x, local.at[local.shape[0] - 1])
+        fetch.start()
+        fetch.wait()
+        d_attn, d_query, d_key = attn_backward_end(x, w, gains, lin, cs, sn, dq, dk, dv, dlin, dw, dn)
+        cols = dw.shape[1]
+        lanes = jnp.concatenate([d_query, d_key, jnp.zeros((1, cols - 2 * HEAD), F32)], axis=1)
+        small = jnp.concatenate([d_attn[:, :cols], d_attn[:, cols:], jnp.zeros((2, cols), F32), lanes, jnp.zeros((11, cols), F32)], axis=0)
+        small = (small + mlp_at[...]).astype(BF16)
+        for f in range(16):
+            at = (f // 8, (f // 2) % 4, f % 2)
+            dwx[at[0], at[1], at[2], :depth, :] = dw[f * depth:(f + 1) * depth, :].astype(BF16)
+            dwx[at[0], at[1], at[2], depth:, :] = small
+
+    pl.run_scoped(ending, pltpu.VMEM((length, width + HEAD), BF16), pltpu.VMEM((length, 4 * HEAD), BF16), pltpu.VMEM((16 * depth, 4 * HEAD), F32))
+    ends.begin()
+    for fl in flows:
+        fl.phase(0)
+    ends.chip()
+    ends.along_x()
+    for fl in flows:
+        fl.phase(1)
+    ends.share()
+    for fl in flows:
+        fl.phase(2)
+    for fl in flows:
+        fl.share()
+    ends.end()
     for fl in flows:
         fl.end()
     wire.finish()
 
 
-def sum_all(grads, number):
+def backward(grads, x, d_heads, mlp_rows, kept):
     srcs = [g.reshape(2, 4, 2, g.shape[0] // 16, g.shape[1]) for g in grads]
+    length, width = x.shape[0], x.shape[1] - HEAD
+    rows, cols = length // 8, 4 * HEAD
+    depth = width // 16
     out = [jax.ShapeDtypeStruct((g.shape[0] // 16, g.shape[1]), BF16) for g in grads]
-    wires, locals_ = 20 * len(PLAN), 5 * len(PLAN)
-    return pl.pallas_call(
-        functools.partial(sum_kernel, PLAN, len(grads)), out_shape=out,
-        in_specs=[ANY] * len(grads), out_specs=[ANY] * len(grads),
-        scratch_shapes=sum_scratch(PLAN, [g.shape for g in grads]) + sems(wires, locals_), **talking(number, "sum_all"))(*srcs)
-
-
-def last_kernel(dw, dn, rows_out, dn_out, mine, other, got, fin, blocks, own, send, recv, local):
-    net, wire, here = Net(), Wire(send, recv), Local(local)
-    others = [(o, (net.f, net.ctx(o))) for o in (4, 6, 2, 5, 7, 1, 3)]
-    cores = [(dz, dy, (fid((net.zl + dz) % 2, (net.y + dy) % 4, net.k), net.c)) for dz in (1, 0) for dy in (2, 1, 3, 0) if dz or dy]
-    barrier([net.sib] + [d for _, d in others] + [d for _, _, d in cores])
-    rows = own.shape[0]
-    near = wire(dw.at[:, :, 1 - net.k], other, net.sib)
-    kept = here(dw.at[:, :, net.k], mine)
-    home = here(dn.at[pl.ds(pl.multiple_of(net.c * rows, 16), rows)], own)
-    moved = [wire(dn.at[pl.ds(pl.multiple_of(net.ctx(o) * rows, 16), rows)], blocks.at[o - 1], d) for o, d in others]
-    near.wait_recv()
-    kept.wait()
-    for a in range(2):
-        for b in range(4):
-            mine[a, b] = (mine[a, b].astype(F32) + other[a, b].astype(F32)).astype(BF16)
-    far = [wire(mine.at[(net.zl + dz) % 2, (net.y + dy) % 4], got.at[dz * 4 + dy - 1], d) for dz, dy, d in cores]
-    for copy in far:
-        copy.wait_recv()
-    total = mine[net.zl, net.y].astype(F32)
-    for i in range(7):
-        total = total + got[i].astype(F32)
-    fin[...] = total.astype(BF16)
-    spreads = [wire(fin, rows_out.at[net.c], d) for _, d in others]
-    placed = here(fin, rows_out.at[net.c])
-    for copy in moved:
-        copy.wait_recv()
-    home.wait()
-
-    def some(r, carry):
-        at = pl.ds(pl.multiple_of(r * 16, 16), 16)
-        s = own[at, :].astype(F32)
-        for i in range(7):
-            s = s + blocks[i, at, :].astype(F32)
-        dn_out[at, :] = s
-        return carry
-
-    lax.fori_loop(0, rows // 16, some, 0)
-    for copy in spreads:
-        copy.wait_recv()
-    placed.wait()
-    wire.finish()
-
-
-def last_sums(dw, dn, number):
-    rows, width = dn.shape[0] // 8, dn.shape[1]
-    a, b = dw.shape[-2:]
-    return pl.pallas_call(
-        last_kernel, out_shape=shapes(((8, a, b), BF16), ((rows, width), F32)),
-        in_specs=[ANY, ANY], out_specs=[ANY, VM],
-        scratch_shapes=[
-            pltpu.VMEM((2, 4, a, b), BF16), pltpu.VMEM((2, 4, a, b), BF16), pltpu.VMEM((7, a, b), BF16), pltpu.VMEM((a, b), BF16),
-            pltpu.VMEM((7, rows, width), BF16), pltpu.VMEM((rows, width), BF16)] + sems(22, 3), **talking(number, "last_sums"))(dw, dn)
+    out += shapes(((8, depth + 16, cols), BF16), ((rows, width), F32))
+    scratch = [(a.shape, a.dtype) for a in kept]
+    scratch += [((length, 2 * HEAD), BF16), ((2, length, HEAD), F32), ((length, HEAD), F32), ((length, HEAD), F32),
+                ((2, length, HEAD), F32), (mlp_rows.shape, F32), ((2, 4, 2, depth + 16, cols), BF16), ((2, 4, rows, width), BF16)]
+    scratch += [((2, 4, depth + 16, cols), BF16), ((7, depth + 16, cols), BF16), ((depth + 16, cols), BF16),
+                ((3, 2, rows, width), BF16), ((2, rows, width), BF16), ((rows, width), BF16)]
+    ng = len(grads)
+    wires = 20 * len(PLAN) + 7 + 3 + 1 + 7 + 1 + 7
+    local = 5 * len(PLAN) + 1 + KEPT + 1 + 1 + 1
+    res = pl.pallas_call(
+        functools.partial(backward_kernel, ng), out_shape=out,
+        in_specs=[ANY] * (ng + 3 + KEPT), out_specs=[ANY] * (ng + 1) + [VM],
+        scratch_shapes=[pltpu.VMEM(s, d) for s, d in scratch] + sum_scratch(PLAN, [s.shape for s in srcs]) + sems(wires, local),
+        **talking(1, "layer_backward"))(*srcs, x, d_heads, mlp_rows, *kept)
+    return res[:ng], res[ng], res[ng + 1]
 def root_mean_norm(rows, scaling):
     return rows * lax.rsqrt(jnp.mean(rows * rows, axis=-1, keepdims=True) + EPSILON) * scaling
 
@@ -786,33 +952,29 @@
         jnp.zeros((16 * cols - 2 * width - 2 * HEAD,), BF16)]).reshape(16, cols)
     pack = jnp.concatenate([own, small], axis=0)
     sequence = jnp.concatenate([inputs[0], jnp.broadcast_to(doc_ids[0].astype(BF16)[:, None], (rows, HEAD))], axis=1)
-    (t, full_output, full_gate, full_up, full_down), x = gather([pack, output_proj, gate_proj, up_proj, down_proj], sequence)
-    kept = attend(x, t, *tables(x.shape[0]))
-    gains, heads = kept[1], kept[10]
-    own_heads = spread(True, heads, 1)
+    (full_output, full_gate, full_up, full_down), x, own_heads, kept = forward(
+        [pack, output_proj, gate_proj, up_proj, down_proj], sequence, *tables(8 * rows))
+    gains = kept[1]
     residual = inputs[0].astype(F32)
     mlp_scale = gains[2:4].reshape(width)
     outputs, d_hidden, d_heads, grads, d_mlp_scale = mlp(
         residual, own_heads, out_grad[0], full_output, full_gate, full_up, full_down, mlp_scale)
-    dh = spread(False, d_heads, 2)
-    gate_g, up_g, down_g, output_g = sum_all(grads, 3)
-    dw, dn, dg = attend_back(x, kept, dh)
-    gain_rows = jnp.concatenate([
-        dg[0].reshape(16, depth), d_mlp_scale.reshape(16, depth),
-        dg[1, :HEAD].reshape(16, 8), dg[1, HEAD:2 * HEAD].reshape(16, 8)], axis=1)
-    gain_rows = jnp.pad(gain_rows[:, None, :], ((0, 0), (0, 15), (0, cols - gain_rows.shape[1])))
-    dw = jnp.concatenate([dw.reshape(16, depth, cols), gain_rows], axis=1).astype(BF16)
-    back, d_normed = last_sums(dw.reshape(2, 4, 2, depth + 16, cols), dn, 4)
+    mlp_rows = jnp.pad(d_mlp_scale.reshape(2, cols), ((2, 12), (0, 0)))
+    (gate_g, up_g, down_g, output_g), back, d_normed = backward(grads, x, d_heads, mlp_rows, kept)
     _, norm_pull = jax.vjp(lambda r: root_mean_norm(r, gains[0:2].reshape(width)), residual)
     input_grad = d_hidden + norm_pull(d_normed)[0]
     back = back.astype(F32)
     query_g = jnp.moveaxis(back[:, :depth, :2 * HEAD], 0, 1).reshape(depth, -1)
     key_g = jnp.moveaxis(back[:, :depth, 2 * HEAD:3 * HEAD], 0, 1).reshape(depth, -1)
     value_g = jnp.moveaxis(back[:, :depth, 3 * HEAD:], 0, 1).reshape(depth, -1)
-    small_g = jnp.sum(back[:, depth, :], axis=0)
+    small_g = jnp.sum(back[:, depth:, :], axis=0)
+
+    def mine(values, size):
+        return lax.dynamic_slice_in_dim(values, f * size, size)
+
     return (outputs[None], input_grad[None], query_g, key_g, value_g, output_g.astype(F32), gate_g.astype(F32),
-            up_g.astype(F32), down_g.astype(F32), small_g[:depth], small_g[depth:2 * depth],
-            small_g[2 * depth:2 * depth + 8], small_g[2 * depth + 8:2 * depth + 16])
+            up_g.astype(F32), down_g.astype(F32), mine(small_g[0:2].reshape(width), depth), mine(small_g[2:4].reshape(width), depth),
+            mine(small_g[4, :HEAD], HEAD // 16), mine(small_g[4, HEAD:2 * HEAD], HEAD // 16))
 
 
 def solution(mesh):

time: 389 us -> 315 us (0.81); the launches traced: 389 us -> 309 us
  Pallas kernels: 321 us -> 243 us
  other arithmetic: 18.8 us -> 12.6 us
    pallas_call x7 -> x2, Pallas kernels: 321 us -> 243 us  [the longest x1 135 us: backward(): pl.pallas_call(functools.partial(backward_kernel, ng), out_shape=out, in_...]
where the time goes in v2:
time: 315 us; the launch traced here: 309 us
  Pallas kernels  243 us (77%)
  matrix products  39.3 us (12%)
  local copies, waits for them, and re-layouts  12.7 us (4%)
  other arithmetic  12.6 us (4%)
    pallas_call x1, Pallas kernels, backward(): pl.pallas_call(functools.partial(backward_kernel, ng), out_shape=out, in_...  135 us
    pallas_call x1, Pallas kernels, forward(): pl.pallas_call(functools.partial(forward_kernel, nw), out_shape=outs, in_...  108 us
    dot_general x4, matrix products, t_dot(): lax.dot_general(left, right, (((0,), (0,)), ((), ())), preferred_element_...  16.8 us
    dot_general x4, matrix products, dot_t(): lax.dot_general(left, right, (((1,), (1,)), ((), ())), preferred_element_...  13.8 us
    dot_general x4, matrix products, plain_dot(): return jnp.dot(left, right, preferred_element_type=F32)  8.76 us

profile of v2, /device:TPU:1, one launch (start us, length us, event | category | flops | bytes accessed | tf_op | source)
XLA Modules:
  0.0 309.1 jit_solution(6190352051667725564)
XLA Ops:
  0.7 0.7 convert_reduce_fusion
  1.4 0.9 dynamic_update_slice.14
  2.3 0.8 dynamic_update_slice.15
  3.1 0.8 dynamic_update_slice.12
  4.0 0.8 dynamic_update_slice.13
  5.6 0.7 constant_dynamic-slice_fusion.3
  6.3 0.7 constant_dynamic-slice_fusion.2
  7.8 1.8 pad_maximum_fusion.refs_5_
  9.6 107.9 %layer_forward.1 = (bf16[2048,1024]{1,0:T(8,128)(2,1)}, bf16[1024,3072]{1,0:T(8,128)(2,1)}, bf16[1024,3072]{1,0:T(8,128)(2,1)}, bf16[3072,1024]{1,0:T(8,128)(2,1...) custom-call(bf16[80,512]{1,0:T(8,128)(2,1)} %pad_maximum_fusion.1.re, ...), custom_call_target="tpu_custom_call" | custom-call | tf_op jit(solution)/shard_map/layer_forward/pallas_call | solution.py:369
  117.5 0.8 slice_bitcast_fusion.5
  118.3 3.7 %multiply_reduce_fusion.2 = (f32[192]{0:T(256)S(1)}, f32[192,1024]{1,0:T(8,128)S(1)}) fusion(bf16[192,2048]{1,0:T(8,128)(2,1)} %get-tuple-element.36, bf16[2048,1024]{1,0:T(8,128)(2,1)} %get-tuple-element.37, bf16[1,192,1024]{2,1,0:T(8,128)(2,1)S(1)} %copy-done.4), kind=kOutput, calls=%fused_computation.32 | convolution fusion | flops 806092608 | bytes 6161152 | tf_op jit(solution)/shard_map/dot_general | solution.py:389
  122.6 1.4 fusion.21
  124.9 1.4 fusion.20
  126.9 3.1 %multiply_convert_fusion = (bf16[192,3072]{1,0:T(8,128)(2,1)S(1)}, bf16[192,3072]{1,0:T(8,128)(2,1)S(1)}, bf16[192,3072]{1,0:T(8,128)(2,1)S(1)}) fusion(f32[192,3072]{1,0:T(8,128)S(1)} %fusion.20, f32[192,3072]{1,0:T(8,128)S(1)} %fusion.21, bf16[3072,1024]{1,0:T(8,128)(2,1)S(1)} %bitcast.89, bf16[1,192,1024]{2,1,0:T(8,128)(2,1)S(1)} %copy-done.10), kind=kOutput, calls=%fused_computation.10 | convolution fusion | flops 1217396736 | bytes 14942208 | tf_op jit(solution)/shard_map/dot_general | solution.py:381
  130.1 2.2 fusion.5
  132.3 2.3 fusion.22
  134.6 3.3 %multiply_reduce_fusion = (f32[1024]{0:T(1024)S(1)}, f32[192]{0:T(256)S(1)}, f32[192,1024]{1,0:T(8,128)}) fusion(f32[192,1024]{1,0:T(8,128)S(1)} %get-tuple-element.77, f32[192]{0:T(256)S(1)} %fusion.15, f32[1024]{0:T(1024)S(1)} %bitcast.82, f32[192,1024]{1,0:T(8,128)S(1)} %fusion.22, bf16[192,3072]{1,0:T(8,128)(2,1)S(1)} %get-tuple-element.63, ...), kind=kOutput, calls=%fused_computation.29 | convolution fusion | flops 1209334528 | bytes 9840128 | tf_op jit(solution)/shard_map/dot_general | solution.py:381
  137.9 1.5 fusion.6
  139.4 5.1 %convolution_convert_fusion.4.refs_5_ = bf16[192,2048]{1,0:T(8,128)(2,1)} fusion(bf16[2048,1024]{1,0:T(8,128)(2,1)} %get-tuple-element.37, f32[192,1024]{1,0:T(8,128)S(1)} %fusion.6), kind=kOutput, calls=%fused_computation.6 | convolution fusion | flops 805896192 | bytes 5767168 | tf_op jit(solution)/shard_map/dot_general | solution.py:381
  145.1 3.3 %convolution_convert_fusion.3 = bf16[2048,1024]{1,0:T(8,128)(2,1)} fusion(bf16[192,2048]{1,0:T(8,128)(2,1)S(1)} %copy-done.5, f32[192,1024]{1,0:T(8,128)S(1)} %fusion.6), kind=kOutput, calls=%fused_computation.4 | convolution fusion | flops 807600128 | bytes 5767168 | tf_op jit(solution)/shard_map/dot_general | solution.py:385
  148.5 4.5 %convolution_convert_fusion = bf16[3072,1024]{1,0:T(8,128)(2,1)} fusion(bf16[192,3072]{1,0:T(8,128)(2,1)S(1)} %copy-done.9, bf16[1,192,1024]{2,1,0:T(8,128)(2,1)S(1)} %copy-done.11), kind=kOutput, calls=%fused_computation | convolution fusion | flops 1211105280 | bytes 7864320 | tf_op jit(solution)/shard_map/dot_general | solution.py:385
  153.0 4.5 %convolution_convert_fusion.1 = bf16[1024,3072]{1,0:T(8,128)(2,1)} fusion(bf16[192,1024]{1,0:T(8,128)(2,1)S(1)} %multiply_convert_fusion.2, bf16[192,3072]{1,0:T(8,128)(2,1)S(1)} %copy-done.7), kind=kOutput, calls=%fused_computation.1 | convolution fusion | flops 1211105280 | bytes 7864320 | tf_op jit(solution)/shard_map/dot_general | solution.py:385
  157.5 4.5 %convolution_convert_fusion.2 = bf16[1024,3072]{1,0:T(8,128)(2,1)} fusion(bf16[192,1024]{1,0:T(8,128)(2,1)S(1)} %multiply_convert_fusion.2, bf16[192,3072]{1,0:T(8,128)(2,1)S(1)} %copy-done.13), kind=kOutput, calls=%fused_computation.2 | convolution fusion | flops 1211105280 | bytes 7864320 | tf_op jit(solution)/shard_map/dot_general | solution.py:385
  161.9 135.3 %layer_backward.1 = (bf16[64,3072]{1,0:T(8,128)(2,1)}, bf16[64,3072]{1,0:T(8,128)(2,1)}, bf16[192,1024]{1,0:T(8,128)(2,1)}, bf16[128,1024]{1,0:T(8,128)(2,1)}, b...) custom-call(bf16[2,4,2,64,3072]{4,3,2,1,0:T(8,128)(2,1)} %bitcast.75, bf16[2,4,2,64,3072]{4,3,2,1,0:T(8,128)(2,1)} %bitcast.74, ...), custom_call_target="tpu_custom_call" | custom-call | tf_op jit(solution)/shard_map/layer_backward/pallas_call | solution.py:894
  297.3 1.4 fusion.9
  298.7 2.5 fusion.8
  301.2 0.8 convert_element_type.82
  304.2 0.8 copy.32
  305.0 0.8 copy_bitcast_fusion
  305.9 0.9 convert_element_type.83
  306.8 0.9 convert_element_type.84
  307.7 1.0 convert_element_type.85
  (81 shorter events, 6.3 us)
Async XLA Ops:
  0.6 6.4 %copy-start = (bf16[64,2048]{1,0:T(8,128)(2,1)S(1)}, bf16[64,2048]{1,0:T(8,128)(2,1)}, u32[]{:S(2)}) copy-start(bf16[64,2048]{1,0:T(8,128)(2,1)} %param.18) | copy-start | bytes 786436
  7.0 111.2 %copy-start.4 = (bf16[1,192,1024]{2,1,0:T(8,128)(2,1)S(1)}, bf16[1,192,1024]{2,1,0:T(8,128)(2,1)}, u32[]{:S(2)}) copy-start(bf16[1,192,1024]{2,1,0:T(8,128)(2,1)} %param.16) | copy-start | bytes 1179652
  118.3 4.3 %copy-start.2 = (bf16[1024,3072]{1,0:T(8,128)(2,1)S(1)}, bf16[1024,3072]{1,0:T(8,128)(2,1)}, u32[]{:S(2)}) copy-start(bf16[1024,3072]{1,0:T(8,128)(2,1)} %get-tuple-element.40) | copy-start | bytes 18874372
  122.0 2.3 slice-start
  122.5 2.3 slice-start.1
  122.6 3.8 %slice-start.2 = ((s8[6291456]{0:T(1024)(128)(4,1)}), s8[4194304]{0:T(1024)(128)(4,1)S(1)}, s32[]{:S(2)}) async-start(s8[6291456]{0:T(1024)(128)(4,1)} %bitcast.88), calls=%async_computation.2 | async-start | bytes 8388608
  124.9 1.5 copy-start.10
  124.9 2.1 slice-start.3
  130.1 2.2 copy-start.8
  130.1 2.2 copy-start.12
  130.1 4.5 %copy-start.6 = (bf16[192,3072]{1,0:T(8,128)(2,1)}, bf16[192,3072]{1,0:T(8,128)(2,1)S(1)}, u32[]{:S(2)}) copy-start(bf16[192,3072]{1,0:T(8,128)(2,1)S(1)} %get-tuple-element.63) | copy-start | bytes 3538948
  139.4 5.8 %copy-start.3 = (f32[192,1024]{1,0:T(8,128)}, f32[192,1024]{1,0:T(8,128)S(1)}, u32[]{:S(2)}) copy-start(f32[192,1024]{1,0:T(8,128)S(1)} %fusion.6) | copy-start | bytes 2359300
  139.4 5.7 %copy-start.5 = (bf16[192,2048]{1,0:T(8,128)(2,1)S(1)}, bf16[192,2048]{1,0:T(8,128)(2,1)}, u32[]{:S(2)}) copy-start(bf16[192,2048]{1,0:T(8,128)(2,1)} %get-tuple-element.36) | copy-start | bytes 2359300
  145.1 3.3 %copy-start.9 = (bf16[192,3072]{1,0:T(8,128)(2,1)S(1)}, bf16[192,3072]{1,0:T(8,128)(2,1)}, u32[]{:S(2)}) copy-start(bf16[192,3072]{1,0:T(8,128)(2,1)} %copy-done.8) | copy-start | bytes 3538948
  145.1 3.3 %copy-start.11 = (bf16[1,192,1024]{2,1,0:T(8,128)(2,1)S(1)}, bf16[1,192,1024]{2,1,0:T(8,128)(2,1)}, u32[]{:S(2)}) copy-start(bf16[1,192,1024]{2,1,0:T(8,128)(2,1)} %param.29) | copy-start | bytes 1179652
  148.5 4.5 %copy-start.7 = (bf16[192,3072]{1,0:T(8,128)(2,1)S(1)}, bf16[192,3072]{1,0:T(8,128)(2,1)}, u32[]{:S(2)}) copy-start(bf16[192,3072]{1,0:T(8,128)(2,1)} %copy-done.6) | copy-start | bytes 3538948
  153.0 4.5 %copy-start.13 = (bf16[192,3072]{1,0:T(8,128)(2,1)S(1)}, bf16[192,3072]{1,0:T(8,128)(2,1)}, u32[]{:S(2)}) copy-start(bf16[192,3072]{1,0:T(8,128)(2,1)} %copy-done.12) | copy-start | bytes 3538948
  297.2 4.0 %copy-start.18 = (bf16[128,1024]{1,0:T(8,128)(2,1)S(1)}, bf16[128,1024]{1,0:T(8,128)(2,1)}, u32[]{:S(2)}) copy-start(bf16[128,1024]{1,0:T(8,128)(2,1)} %get-tuple-element.55) | copy-start | bytes 786436
  297.3 4.8 %copy-start.14 = (bf16[8,80,512]{2,1,0:T(8,128)(2,1)S(1)}, bf16[8,80,512]{2,1,0:T(8,128)(2,1)}, u32[]{:S(2)}) copy-start(bf16[8,80,512]{2,1,0:T(8,128)(2,1)} %get-tuple-element.54) | copy-start | bytes 1966084
  302.2 3.6 %copy-start.17 = (bf16[64,3072]{1,0:T(8,128)(2,1)S(1)}, bf16[64,3072]{1,0:T(8,128)(2,1)}, u32[]{:S(2)}) copy-start(bf16[64,3072]{1,0:T(8,128)(2,1)} %get-tuple-element.56) | copy-start | bytes 1179652
  304.1 2.7 copy-start.16
  304.2 3.6 %copy-start.15 = (bf16[192,1024]{1,0:T(8,128)(2,1)S(1)}, bf16[192,1024]{1,0:T(8,128)(2,1)}, u32[]{:S(2)}) copy-start(bf16[192,1024]{1,0:T(8,128)(2,1)} %get-tuple-element.58) | copy-start | bytes 1179652
  304.2 4.5 %copy-start.1 = (bf16[64,2048]{1,0:T(8,128)(2,1)S(1)}, bf16[64,2048]{1,0:T(8,128)(2,1)}, u32[]{:S(2)}) copy-start(bf16[64,2048]{1,0:T(8,128)(2,1)} %param.18) | copy-start | bytes 786436

commit v3 on v2

--- a/solution.py
+++ b/solution.py
@@ -196,6 +196,72 @@
                 self.got(name)
 
 
+class SharedFlow(WeightFlow):
+    def quarter(self, dz, dy, hi, own=False):
+        n, q = self.net, self.rows // 4
+        zl = n.zl if dz == 0 else 1 - n.zl
+        at = (2 * hi + n.x % 2) * q
+        if own:
+            return self.src.at[pl.ds(pl.multiple_of(at, 16), q)]
+        return self.out.at[pl.ds(pl.multiple_of(fid(zl, (n.y + dy + 4) % 4, n.k) * self.rows + at, 16), q)]
+
+    def hand(self, name, device, dz, dy, hi):
+        ref = self.quarter(dz, dy, hi)
+        self.c[name] = self.wire(ref, ref, device)
+
+    def along_z(self, tag, dy):
+        self.hand("zp" + tag, self.zp, 0, dy, 0)
+        self.hand("zm" + tag, self.zm, 0, dy, 1)
+
+    def along_x(self, tag, dy):
+        self.got("zp" + tag)
+        self.hand("xp" + tag, self.net.xp, 1, dy, 0)
+        self.got("zm" + tag)
+        self.hand("xm" + tag, self.net.xm, 1, dy, 1)
+
+    def to_sibling(self, tag, dy):
+        self.got("xp" + tag)
+        self.got("xm" + tag)
+        self.pass_on("dz" + tag, self.net.sib, 1, dy)
+
+    def stage(self, s):
+        n, w, c = self.net, self.wire, self.c
+        if s == 0:
+            c["yp"] = w(self.own(), self.place(0, 0), n.yp)
+            c["ym"] = w(self.own(), self.place(0, 0), n.ym)
+            c["zp0"] = w(self.quarter(0, 0, 0, True), self.quarter(0, 0, 0), self.zp)
+            c["zm0"] = w(self.quarter(0, 0, 1, True), self.quarter(0, 0, 1), self.zm)
+            c["d"] = w(self.own(), self.place(0, 0), n.sib)
+        elif s == 1:
+            self.got("yp")
+            self.pass_on("yp2", n.yp, 0, -1, 0, 2)
+            self.along_z("m", -1)
+            self.pass_on("d_m", n.sib, 0, -1)
+            self.got("ym")
+            self.pass_on("ym2", n.ym, 0, 1, 2, 4)
+            self.along_z("p", 1)
+            self.pass_on("d_p", n.sib, 0, 1)
+            self.along_x("0", 0)
+        elif s == 2:
+            self.got("yp2")
+            self.hand("zp2", self.zp, 0, 2, 0)
+            self.pass_on("d2a", n.sib, 0, 2, 0, 2)
+            self.got("ym2")
+            self.hand("zm2", self.zm, 0, 2, 1)
+            self.pass_on("d2b", n.sib, 0, 2, 2, 4)
+            self.along_x("m", -1)
+            self.along_x("p", 1)
+            self.to_sibling("0", 0)
+        elif s == 3:
+            self.along_x("2", 2)
+            self.to_sibling("m", -1)
+            self.to_sibling("p", 1)
+        elif s == 4:
+            self.to_sibling("2", 2)
+            for name in ("d", "d_m", "d_p", "d2a", "d2b", "dz0", "dzm", "dzp", "dz2"):
+                self.got(name)
+
+
 class RowFlow:
     def __init__(self, net, wire, src, out):
         self.net, self.wire, self.src, self.out = net, wire, src, out
@@ -307,42 +373,47 @@
     w, gains, q, k, v, lin, cs, sn, start, hf, inv = kept
     net, wire, here = Net(), Wire(send, recv), Local(local)
     barrier(neighbours(net))
-    flows = [WeightFlow(net, wire, s, o, i == 0) for i, (s, o) in enumerate(zip(srcs, (t, *outs)))]
-    first, seq = flows[0], RowFlow(net, wire, rows, x)
+    first, out_f, gate_f, up_f, down_f = [
+        kind(net, wire, s, o, i == 0)
+        for i, (kind, s, o) in enumerate(zip((WeightFlow, WeightFlow, WeightFlow, SharedFlow, SharedFlow), srcs, (t, *outs)))]
+    flows = (first, out_f, gate_f, up_f, down_f)
+    seq = RowFlow(net, wire, rows, x)
     first.stage(0)
     seq.stage(0)
-    flows[1].stage(0)
+    out_f.stage(0)
+    gate_f.stage(0)
     tables_in = [here(cos_in, cos_at), here(sin_in, sin_at)]
     placed_here = [here(fl.src, fl.place(0, 0)) for fl in flows]
     placed_here.append(here(rows, seq.place(net.c)))
     first.stage(1)
-    flows[2].stage(0)
+    out_f.stage(1)
+    up_f.stage(0)
+    first.stage(2)
     seq.stage(1)
-    first.stage(2)
-    flows[1].stage(1)
+    gate_f.stage(1)
+    down_f.stage(0)
+    first.stage(3)
+    out_f.stage(2)
     seq.stage(2)
-    first.stage(3)
-    flows[3].stage(0)
+    up_f.stage(1)
     first.stage(4)
-    flows[2].stage(1)
-    flows[1].stage(2)
+    gate_f.stage(2)
     seq.stage(3)
     for c in tables_in + placed_here:
         c.wait()
     saved = [here(x, rows_out)]
     tick = Later([
-        together(stage(flows[4], 0), stage(flows[1], 3)),
-        together(stage(flows[3], 1), stage(flows[2], 2)),
-        stage(flows[2], 3),
-        together(stage(flows[4], 1), stage(flows[3], 2)),
-        stage(flows[3], 3),
-        stage(flows[4], 2),
+        together(stage(down_f, 1), stage(out_f, 3)),
+        stage(up_f, 2),
+        stage(gate_f, 3),
+        stage(down_f, 2),
+        stage(up_f, 3),
+        stage(down_f, 3),
     ])
     attn_forward(tick, x, t, cos_at, sin_at, w, gains, q, k, v, lin, cs, sn, start, hf, heads, inv)
     spread = Spread(net, wire, here, True, heads, own_heads)
     saved += [here(a, b) for a, b in zip(kept, kept_out)]
     tick.rest()
-    flows[4].stage(3)
     for fl in flows[1:]:
         fl.stage(4)
     spread.end()
@@ -370,7 +441,7 @@
         functools.partial(forward_kernel, nw),
         out_shape=outs, in_specs=[ANY] * (nw + 3), out_specs=[ANY] * len(outs),
         scratch_shapes=[pltpu.VMEM(s, d) for s, d in scratch] + [pltpu.VMEM(a.shape, a.dtype) for a in kept]
-        + sems(27 * nw + 9 + 7, nw + 3 + 1 + 1 + KEPT), **talking(0, "layer_forward"),
+        + sems(29 * nw + 9 + 7, nw + 3 + 1 + 1 + KEPT), **talking(0, "layer_forward"),
     )(*weights, rows, cos_in, sin_in)
     return res[:nw - 1], res[nw - 1], res[nw], res[nw + 1:]
 def block(i, size):
@@ -593,12 +664,12 @@
 
 
 class SumFlow:
-    def __init__(self, net, wire, here, src, first, order, slots, other, got, part, fin, out):
+    def __init__(self, net, wire, here, src, first, order, slots, other, relay, got, part, fin, out):
         self.net, self.wire, self.here, self.src, self.first, self.order = net, wire, here, src, first, order
-        self.slots, self.other, self.got, self.part, self.fin, self.out = slots, other, got, part, fin, out
+        self.slots, self.other, self.relay, self.got, self.part, self.fin, self.out = slots, other, relay, got, part, fin, out
         self.rows, self.cols = other.shape[2], other.shape[3]
         self.w = self.cols // 8
-        self.far = {}
+        self.far, self.via = {}, {}
 
     def cut(self, ref, dim, d, k=None):
         tail = ref.shape[-1]
@@ -616,18 +687,16 @@
         return ref.at[a[0], a[1], k, pl.ds(self.first, self.rows), cols]
 
     def begin(self):
-        n, dim = self.net, self.order[0]
         self.near, self.own = {}, {}
-        for o in FIRST:
-            d = (n.at(dim) + o) % 4
-            self.near[o] = self.wire(self.cut(self.src, dim, d, 1 - n.k), self.cut(self.other, dim, d), n.sib)
         self.bring(0)
         self.bring(1)
 
     def bring(self, i):
         n, dim = self.net, self.order[0]
-        d = (n.at(dim) + FIRST[i]) % 4
-        self.own[FIRST[i]] = self.here(self.cut(self.src, dim, d, n.k), self.slots.at[i % 2])
+        o = FIRST[i]
+        d = (n.at(dim) + o) % 4
+        self.near[o] = self.wire(self.cut(self.src, dim, d, 1 - n.k), self.cut(self.other, dim, d), n.sib)
+        self.own[o] = self.here(self.cut(self.src, dim, d, n.k), self.slots.at[i % 2])
 
     def add(self, out, parts):
         if self.wire.again:
@@ -641,7 +710,7 @@
 
                 def put(here, value):
                     out[i, j, here, :] = value
-                add_rows(put, [take(p) for p in parts], self.rows, step)
+                add_rows(put, [take(p) for p in parts], out.shape[2], step)
 
     def chip(self, o):
         n, dim = self.net, self.order[0]
@@ -653,16 +722,24 @@
         self.add(piece, [piece, self.slots.at[i % 2]])
         if i + 2 < 4:
             self.bring(i + 2)
-        if o:
-            self.far[o] = self.wire(piece, self.got[0].at[o - 1], n.along(dim, o))
+        half = self.rows // 2
+        if o == 2:
+            for which, to in ((0, 1), (1, 3)):
+                self.via[to] = self.wire(piece.at[:, :, pl.ds(which * half, half)], self.relay.at[which], n.along(dim, to))
+        elif o:
+            which = 0 if o == 1 else 1
+            self.via[o].wait_recv()
+            part = piece.at[:, :, pl.ds(which * half, half)]
+            self.add(part, [part, self.relay.at[which]])
+            self.far[o] = self.wire(piece, self.got[0].at[which], n.along(dim, o))
 
     def phase(self, p):
         n, dim = self.net, self.order[p]
         held = self.other if p == 0 else self.part[p - 1]
-        for o in (1, 3, 2):
+        for o in (1, 3, 2) if p else (1, 3):
             self.far[o].wait_recv()
         result = self.part[p] if p < 2 else self.fin
-        self.add(result, [self.cut(held, dim, n.at(dim))] + [self.got[p].at[o - 1] for o in (1, 2, 3)])
+        self.add(result, [self.cut(held, dim, n.at(dim))] + [self.got[p].at[i] for i in range(3 if p else 2)])
         if p < 2:
             after = self.order[p + 1]
             for o in (2, 1, 3):
@@ -676,7 +753,7 @@
 
     def place(self, zh):
         n = self.net
-        s = zh * 4 + n.x if self.order == "zyx" else n.x * 2 + zh
+        s = zh * 4 + n.x if self.order.index("z") < self.order.index("x") else n.x * 2 + zh
         return self.out.at[pl.ds(self.first, self.rows), pl.ds(pl.multiple_of(s * self.w, 128), self.w)]
 
     def share(self):
@@ -704,7 +781,7 @@
     return out
 
 
-PLAN = ((0, 0, 64, "yxz"), (1, 0, 64, "yxz"), (2, 0, 192, "zyx"), (3, 0, 64, "xzy"), (3, 64, 64, "zyx"))
+PLAN = ((0, 0, 64, "yxz"), (1, 0, 64, "xzy"), (2, 0, 192, "zyx"), (3, 0, 64, "yzx"), (3, 64, 64, "yxz"))
 
 
 def first_shapes(plan, shapes_in):
@@ -716,26 +793,31 @@
     for which, first, rows, order in plan:
         cols = shapes_in[which][-1]
         a, b, c = sum_shapes(rows, cols, order)
-        held += [pltpu.VMEM(s, BF16) for s in ((2, 4, rows, cols), (3, *a), (3, *b), (3, *c), a, b, c)]
+        half = (a[0], a[1], a[2] // 2, a[3])
+        held += [pltpu.VMEM(s, BF16) for s in ((2, 4, rows, cols), (2, *half), (2, *a), (3, *b), (3, *c), a, b, c)]
     return held
 
 
 def make_flows(net, wire, here, plan, srcs, outs, held, slots):
     flows = []
     for n, (which, first, rows, order) in enumerate(plan):
-        other, g0, g1, g2, p0, p1, fin = held[7 * n:7 * n + 7]
-        flows.append(SumFlow(net, wire, here, srcs[which], first, order, slots[n], other, (g0, g1, g2), (p0, p1), fin, outs[which]))
+        other, relay, g0, g1, g2, p0, p1, fin = held[8 * n:8 * n + 8]
+        flows.append(SumFlow(net, wire, here, srcs[which], first, order, slots[n], other, relay, (g0, g1, g2), (p0, p1), fin, outs[which]))
     return flows
 
 
 class Ends:
-    def __init__(self, net, wire, here, dwx, dn, rows_out, dn_out, other, got, fin, got_x, part, got_z):
+    def __init__(self, net, wire, here, dwx, dn, rows_out, dn_out, other, got, fin, got_xa, part_a, got_za, got_zb, part_b, got_xb):
         self.net, self.wire, self.here, self.dwx, self.dn, self.rows_out, self.dn_out = net, wire, here, dwx, dn, rows_out, dn_out
-        self.other, self.got, self.fin, self.got_x, self.part, self.got_z = other, got, fin, got_x, part, got_z
+        self.other, self.got, self.fin = other, got, fin
+        self.got_xa, self.part_a, self.got_za, self.got_zb, self.part_b, self.got_xb = got_xa, part_a, got_za, got_zb, part_b, got_xb
+        self.half = part_a.shape[-1]
+        self.rows = part_a.shape[1]
 
     def begin(self):
-        n = self.net
-        self.moved = {o: self.wire(self.dn.at[:, (n.x + o) % 4], self.got_x.at[o - 1], n.along("x", o)) for o in (2, 1, 3)}
+        n, h = self.net, self.half
+        self.over_b = self.wire(self.dn.at[1 - n.zh, :, :, pl.ds(h, h)], self.got_zb, n.peer)
+        self.moved_a = [self.wire(self.dn.at[:, (n.x + o) % 4, :, pl.ds(0, h)], self.got_xa.at[o - 1], n.along("x", o)) for o in (2, 1, 3)]
         self.near = self.wire(self.dwx.at[:, :, 1 - n.k], self.other, n.sib)
 
     def chip(self):
@@ -751,19 +833,27 @@
                     there = ((n.zl + dz) % 2, (n.y + dy) % 4)
                     self.far.append(self.wire(self.other.at[there[0], there[1]], self.got.at[dz * 4 + dy - 1], (fid(there[0], there[1], n.k), n.c)))
 
+    def along_z(self):
+        n, h = self.net, self.half
+        self.over_b.wait_recv()
+        for x in range(4):
+            def put(here, value):
+                self.part_b[x, here, :] = value
+            add_rows(put, [lambda here: self.dn[n.zh, x, here, h:], lambda here: self.got_zb[x, here, :]], self.rows, 16)
+        self.moved_b = [self.wire(self.part_b.at[(n.x + o) % 4], self.got_xb.at[o - 1], n.along("x", o)) for o in (2, 1, 3)]
+
     def along_x(self):
-        n = self.net
-        for copy in self.moved.values():
+        n, h = self.net, self.half
+        for copy in self.moved_a:
             copy.wait_recv()
-
         for zh in range(2):
             def take(o):
-                return (lambda here: self.dn[zh, n.x, here, :]) if o == 0 else (lambda here: self.got_x[o - 1, zh, here, :])
+                return (lambda here: self.dn[zh, n.x, here, :h]) if o == 0 else (lambda here: self.got_xa[o - 1, zh, here, :])
 
             def put(here, value):
-                self.part[zh, here, :] = value
-            add_rows(put, [take(o) for o in range(4)], self.part.shape[1], 16)
-        self.over = self.wire(self.part.at[1 - n.zh], self.got_z, n.peer)
+                self.part_a[zh, here, :] = value
+            add_rows(put, [take(o) for o in range(4)], self.rows, 16)
+        self.over_a = self.wire(self.part_a.at[1 - n.zh], self.got_za, n.peer)
 
     def share(self):
         n = self.net
@@ -777,15 +867,21 @@
         self.kept = self.here(self.fin, self.rows_out.at[n.c])
 
     def end(self):
-        n = self.net
-        self.over.wait_recv()
+        n, h = self.net, self.half
+        self.over_a.wait_recv()
+        for copy in self.moved_b:
+            copy.wait_recv()
 
         def some(r, carry):
             at = pl.ds(pl.multiple_of(r * 16, 16), 16)
-            self.dn_out[at, :] = self.part[n.zh, at, :].astype(F32) + self.got_z[at, :].astype(F32)
+            self.dn_out[at, :h] = self.part_a[n.zh, at, :].astype(F32) + self.got_za[at, :].astype(F32)
+            total = self.part_b[n.x, at, :].astype(F32)
+            for o in range(3):
+                total = total + self.got_xb[o, at, :].astype(F32)
+            self.dn_out[at, h:] = total
             return carry
 
-        lax.fori_loop(0, self.got_z.shape[0] // 16, some, 0)
+        lax.fori_loop(0, self.rows // 16, some, 0)
         for copy in self.copies:
             copy.wait_recv()
         self.kept.wait()
@@ -799,25 +895,18 @@
     kept, refs = refs[:KEPT], refs[KEPT:]
     w, gains, q, k, v, lin, cs, sn, start, hf, inv = kept
     dh, dq, dk, dv, delta, mlp_at, dwx, dn = refs[:8]
-    end_held, refs = refs[8:14], refs[14:]
+    end_held, refs = refs[8:17], refs[17:]
     held, (send, recv, local) = refs[:-3], refs[-3:]
     net = Net()
     length, width = x_in.shape[0], x_in.shape[1] - HEAD
     depth = w.shape[0] // 16
 
-    def slotted(*slots):
-        wire, here = Wire(send, recv), Local(local)
-        barrier(neighbours(net))
+    def opening(wire, here, slots):
         spread = Spread(net, wire, here, False, d_heads, dh)
         flows = make_flows(net, wire, here, PLAN, srcs, outs, held, slots)
         for fl in flows:
             fl.begin()
         loads = [here(a, b) for a, b in zip(kept_in, kept)] + [here(mlp_rows, mlp_at)]
-        for fl in flows:
-            fl.chip(2)
-        for c in loads:
-            c.wait()
-        spread.end()
 
         def chips(o):
             def go():
@@ -825,21 +914,22 @@
                     fl.chip(o)
             return go
 
-        tick = Later([chips(1), chips(3), chips(0)])
+        chips(2)()
+        return spread, loads, Later([chips(1), chips(3), chips(0)]), flows
+
+    def slotted(*slots):
+        barrier(neighbours(net))
+        spread, loads, tick, _ = opening(Wire(send, recv), Local(local), slots)
+        for c in loads:
+            c.wait()
+        spread.end()
         attn_backward(tick, gains, q, k, v, start, hf, inv, dh, dq, dk, dv, delta)
         tick.rest()
 
     pl.run_scoped(slotted, *[pltpu.VMEM((2, *a), BF16) for a in first_shapes(PLAN, [s.shape for s in srcs])])
     wire, here = Wire(send, recv, True), Local(local, True)
-    Spread(net, wire, here, False, d_heads, dh)
-    flows = make_flows(net, wire, here, PLAN, srcs, outs, held, held[1::7])
-    for fl in flows:
-        fl.begin()
-    for a, b in list(zip(kept_in, kept)) + [(mlp_rows, mlp_at)]:
-        here(a, b)
-    for o in (2, 1, 3, 0):
-        for fl in flows:
-            fl.chip(o)
+    _, _, tick, flows = opening(wire, here, held[2::8])
+    tick.rest()
     wire.again = here.again = False
     ends = Ends(net, wire, here, dwx, dn, rows_out, dn_out, *end_held)
 
@@ -857,19 +947,24 @@
             dwx[at[0], at[1], at[2], :depth, :] = dw[f * depth:(f + 1) * depth, :].astype(BF16)
             dwx[at[0], at[1], at[2], depth:, :] = small
 
+    def phase(p):
+        for fl in flows:
+            fl.phase(p)
+
+    def share():
+        for fl in flows:
+            fl.share()
+
     pl.run_scoped(ending, pltpu.VMEM((length, width + HEAD), BF16), pltpu.VMEM((length, 4 * HEAD), BF16), pltpu.VMEM((16 * depth, 4 * HEAD), F32))
     ends.begin()
-    for fl in flows:
-        fl.phase(0)
+    phase(0)
+    phase(1)
     ends.chip()
+    ends.along_z()
     ends.along_x()
-    for fl in flows:
-        fl.phase(1)
+    phase(2)
     ends.share()
-    for fl in flows:
-        fl.phase(2)
-    for fl in flows:
-        fl.share()
+    share()
     ends.end()
     for fl in flows:
         fl.end()
@@ -880,16 +975,17 @@
     srcs = [g.reshape(2, 4, 2, g.shape[0] // 16, g.shape[1]) for g in grads]
     length, width = x.shape[0], x.shape[1] - HEAD
     rows, cols = length // 8, 4 * HEAD
-    depth = width // 16
+    depth, half = width // 16, width // 2
     out = [jax.ShapeDtypeStruct((g.shape[0] // 16, g.shape[1]), BF16) for g in grads]
     out += shapes(((8, depth + 16, cols), BF16), ((rows, width), F32))
     scratch = [(a.shape, a.dtype) for a in kept]
     scratch += [((length, 2 * HEAD), BF16), ((2, length, HEAD), F32), ((length, HEAD), F32), ((length, HEAD), F32),
                 ((2, length, HEAD), F32), (mlp_rows.shape, F32), ((2, 4, 2, depth + 16, cols), BF16), ((2, 4, rows, width), BF16)]
     scratch += [((2, 4, depth + 16, cols), BF16), ((7, depth + 16, cols), BF16), ((depth + 16, cols), BF16),
-                ((3, 2, rows, width), BF16), ((2, rows, width), BF16), ((rows, width), BF16)]
+                ((3, 2, rows, half), BF16), ((2, rows, half), BF16), ((rows, half), BF16),
+                ((4, rows, half), BF16), ((4, rows, half), BF16), ((3, rows, half), BF16)]
     ng = len(grads)
-    wires = 20 * len(PLAN) + 7 + 3 + 1 + 7 + 1 + 7
+    wires = 21 * len(PLAN) + 7 + 3 + 1 + 3 + 1 + 7 + 1 + 7
     local = 5 * len(PLAN) + 1 + KEPT + 1 + 1 + 1
     res = pl.pallas_call(
         functools.partial(backward_kernel, ng), out_shape=out,
@@ -897,34 +993,72 @@
         scratch_shapes=[pltpu.VMEM(s, d) for s, d in scratch] + sum_scratch(PLAN, [s.shape for s in srcs]) + sems(wires, local),
         **talking(1, "layer_backward"))(*srcs, x, d_heads, mlp_rows, *kept)
     return res[:ng], res[ng], res[ng + 1]
+CHUNK = 384
+
+
+def mlp_kernel(steps, x, heads, g, gains, wo, wg, wu, wd, out, d_hidden, d_heads, rows_out, dg, du, dd, do, hidden, mixed, mixed_t, acc, d_mixed):
+    step = pl.program_id(0)
+    width = x.shape[1]
+    gain = jnp.concatenate([gains[2:3], gains[3:4]], axis=1)
+
+    @pl.when(step == 0)
+    def _():
+        h = x[...].astype(F32) + plain_dot(heads[...], wo[...])
+        hidden[...] = h
+        m = unit(h)[0] * gain
+        mixed[...] = m.astype(BF16)
+        mixed_t[...] = m.T.astype(BF16)
+        acc[...] = h
+        d_mixed[...] = jnp.zeros_like(d_mixed)
+
+    m, grad = mixed[...], g[...]
+    gate, upward = plain_dot(m, wg[...]), plain_dot(m, wu[...])
+    s = jax.nn.sigmoid(gate)
+    act = gate * s
+    active = (act * upward).astype(BF16)
+    acc[...] += plain_dot(active, wd[...])
+    d_active = dot_t(grad, wd[...])
+    dd[...] = t_dot(active, grad).astype(BF16)
+    d_up = (d_active * act).astype(BF16)
+    d_gate = (d_active * upward * (s + act * (1.0 - s))).astype(BF16)
+    dg[...] = plain_dot(mixed_t[...], d_gate).astype(BF16)
+    du[...] = plain_dot(mixed_t[...], d_up).astype(BF16)
+    d_mixed[...] += dot_t(d_gate, wg[...]) + dot_t(d_up, wu[...])
+
+    @pl.when(step == steps - 1)
+    def _():
+        out[...] = acc[...].astype(BF16)
+        e, r = unit(hidden[...])
+        d = d_mixed[...]
+        d_gain = jnp.sum(d * e, axis=0, keepdims=True)
+        d = d * gain
+        d = g[...].astype(F32) + r * (d - e * jnp.mean(d * e, axis=-1, keepdims=True))
+        d_hidden[...] = d
+        low = d.astype(BF16)
+        d_heads[...] = dot_t(low, wo[...]).astype(BF16)
+        do[...] = t_dot(heads[...], low).astype(BF16)
+        half = width // 2
+        rows_out[...] = jnp.concatenate([jnp.zeros((2, half), F32), d_gain[:, :half], d_gain[:, half:], jnp.zeros((12, half), F32)], axis=0)
+
+
+def mlp(x, heads, g, gains, wo, wg, wu, wd):
+    rows, width = x.shape
+    steps = wg.shape[1] // CHUNK
+    whole = lambda a: pl.BlockSpec(a.shape, lambda i: (0,) * len(a.shape), pipeline_mode=pl.Buffered(1))
+    fixed = lambda *s: pl.BlockSpec(s, lambda i: (0, 0))
+    by_col = pl.BlockSpec((width, CHUNK), lambda i: (0, i))
+    by_row = pl.BlockSpec((CHUNK, width), lambda i: (i, 0))
+    out = shapes(((rows, width), BF16), ((rows, width), F32), (heads.shape, BF16), ((16, width // 2), F32),
+                 (wg.shape, BF16), (wu.shape, BF16), (wd.shape, BF16), (wo.shape, BF16))
+    return pl.pallas_call(
+        functools.partial(mlp_kernel, steps), out_shape=out, grid=(steps,),
+        in_specs=[whole(x), whole(heads), whole(g), whole(gains), whole(wo), by_col, by_col, by_row],
+        out_specs=[fixed(rows, width), fixed(rows, width), fixed(*heads.shape), fixed(16, width // 2), by_col, by_col, by_row, fixed(*wo.shape)],
+        scratch_shapes=[pltpu.VMEM((rows, width), F32), pltpu.VMEM((rows, width), BF16), pltpu.VMEM((width, rows), BF16),
+                        pltpu.VMEM((rows, width), F32), pltpu.VMEM((rows, width), F32)],
+        compiler_params=pltpu.CompilerParams(vmem_limit_bytes=56 << 20), name="mlp")(x, heads, g, gains, wo, wg, wu, wd)
 def root_mean_norm(rows, scaling):
     return rows * lax.rsqrt(jnp.mean(rows * rows, axis=-1, keepdims=True) + EPSILON) * scaling
-
-
-def silu_product(gate, upward):
-    return jax.nn.silu(gate) * upward
-
-
-def mlp(residual, heads, grad_rows, full_output, full_gate, full_up, full_down, mlp_scale):
-    hidden = residual + plain_dot(heads, full_output)
-    mixed_f, mix_pull = jax.vjp(root_mean_norm, hidden, mlp_scale)
-    mixed = mixed_f.astype(BF16)
-    gate, upward = plain_dot(mixed, full_gate), plain_dot(mixed, full_up)
-    active_f, active_pull = jax.vjp(silu_product, gate, upward)
-    active = active_f.astype(BF16)
-    outputs = (hidden + plain_dot(active, full_down)).astype(BF16)
-    d_down = t_dot(active, grad_rows)
-    d_gate, d_upward = active_pull(dot_t(grad_rows, full_down))
-    gate_low, up_low = d_gate.astype(BF16), d_upward.astype(BF16)
-    d_gate_w, d_up_w = t_dot(mixed, gate_low), t_dot(mixed, up_low)
-    d_mixed = dot_t(gate_low, full_gate) + dot_t(up_low, full_up)
-    d_hidden_norm, d_mlp_scale = mix_pull(d_mixed)
-    d_hidden = grad_rows.astype(F32) + d_hidden_norm
-    hidden_low = d_hidden.astype(BF16)
-    d_output = t_dot(heads, hidden_low)
-    d_heads = dot_t(hidden_low, full_output).astype(BF16)
-    grads = [g.astype(BF16) for g in (d_gate_w, d_up_w, d_down, d_output)]
-    return outputs, d_hidden, d_heads, grads, d_mlp_scale
 
 
 def tables(length):
@@ -933,8 +1067,8 @@
     return jnp.asarray(np.cos(angles), F32), jnp.asarray(np.sin(angles), F32)
 
 
-def placed(values, f, size):
-    return lax.dynamic_update_slice_in_dim(jnp.zeros((size,), BF16), values, f * values.shape[0], 0)
+def placed(values, f):
+    return jnp.where(jnp.arange(16)[:, None] == f, values[None, :], jnp.zeros((), BF16)).reshape(-1)
 
 
 def body(inputs, doc_ids, query_proj, key_projection, value_projection, output_proj, gate_proj, up_proj, down_proj,
@@ -948,7 +1082,7 @@
         lax.dynamic_slice_in_dim(key_projection, c * HEAD, HEAD, 1),
         lax.dynamic_slice_in_dim(value_projection, c * HEAD, HEAD, 1)], axis=1)
     small = jnp.concatenate([
-        placed(attn_gain, f, width), placed(mlp_gain, f, width), placed(query_norm_gain, f, HEAD), placed(key_gain, f, HEAD),
+        placed(attn_gain, f), placed(mlp_gain, f), placed(query_norm_gain, f), placed(key_gain, f),
         jnp.zeros((16 * cols - 2 * width - 2 * HEAD,), BF16)]).reshape(16, cols)
     pack = jnp.concatenate([own, small], axis=0)
     sequence = jnp.concatenate([inputs[0], jnp.broadcast_to(doc_ids[0].astype(BF16)[:, None], (rows, HEAD))], axis=1)
@@ -956,10 +1090,8 @@
         [pack, output_proj, gate_proj, up_proj, down_proj], sequence, *tables(8 * rows))
     gains = kept[1]
     residual = inputs[0].astype(F32)
-    mlp_scale = gains[2:4].reshape(width)
-    outputs, d_hidden, d_heads, grads, d_mlp_scale = mlp(
-        residual, own_heads, out_grad[0], full_output, full_gate, full_up, full_down, mlp_scale)
-    mlp_rows = jnp.pad(d_mlp_scale.reshape(2, cols), ((2, 12), (0, 0)))
+    outputs, d_hidden, d_heads, mlp_rows, *grads = mlp(
+        inputs[0], own_heads, out_grad[0], gains, full_output, full_gate, full_up, full_down)
     (gate_g, up_g, down_g, output_g), back, d_normed = backward(grads, x, d_heads, mlp_rows, kept)
     _, norm_pull = jax.vjp(lambda r: root_mean_norm(r, gains[0:2].reshape(width)), residual)
     input_grad = d_hidden + norm_pull(d_normed)[0]

time: 315 us -> 254 us (0.81); the launches traced: 309 us -> 254 us
  matrix products: 39.3 us -> 0 us
  Pallas kernels: 243 us -> 234 us
  local copies, waits for them, and re-layouts: 12.7 us -> 7.49 us
    dot_general x12 -> x0, matrix products: 39.3 us -> none  [the longest x4 16.8 us: t_dot(): lax.dot_general(left, right, (((0,), (0,)), ((), ())), preferred_element_...]
    pallas_call x0 -> x1, Pallas kernels: none -> 31 us  [mlp(): pl.pallas_call(functools.partial(mlp_kernel, steps), out_shape=out, grid=...]
    pallas_call x1, Pallas kernels: 108 us -> 84.5 us  [forward(): pl.pallas_call(functools.partial(forward_kernel, nw), out_shape=outs, in_...]
    pallas_call x1, Pallas kernels: 135 us -> 119 us  [backward(): pl.pallas_call(functools.partial(backward_kernel, ng), out_shape=out, in_...]
    dynamic_update_slice x4 -> x0, local copies, waits for them, and re-layouts: 3.37 us -> none  [placed(): lax.dynamic_update_slice_in_dim(jnp.zeros((size,), BF16), values, f * val...]
where the time goes in v3:
time: 254 us
  Pallas kernels  234 us (92%)
  other arithmetic  11.1 us (4%)
  local copies, waits for them, and re-layouts  7.49 us (3%)
    pallas_call x1, Pallas kernels, backward(): pl.pallas_call(functools.partial(backward_kernel, ng), out_shape=out, in_...  119 us
    pallas_call x1, Pallas kernels, forward(): pl.pallas_call(functools.partial(forward_kernel, nw), out_shape=outs, in_...  84.5 us
    pallas_call x1, Pallas kernels, mlp(): pl.pallas_call(functools.partial(mlp_kernel, steps), out_shape=out, grid=...  31 us

profile of v3, /device:TPU:1, one launch (start us, length us, event | category | flops | bytes accessed | tf_op | source)
XLA Modules:
  0.0 253.5 jit_solution(7751913318373630013)
XLA Ops:
  0.7 0.8 broadcast_select_fusion.2
  1.5 0.1 select_n.48
  1.6 0.1 select_n.50
  1.7 0.7 broadcast_select_fusion
  2.4 0.1 select_n.52
  2.5 0.2 dynamic-update-slice.2
  2.7 0.1 select_n.54
  2.8 0.2 dynamic-update-slice.3
  3.1 0.3 dynamic-update-slice.4
  3.4 0.7 constant_dynamic-slice_fusion.2
  4.2 0.6 pad_maximum_fusion.1.refs_0_
  4.8 0.7 convert_reduce_fusion
  5.5 0.1 broadcast_in_dim.94
  5.6 1.8 pad_maximum_fusion.refs_5_
  7.4 84.5 %layer_forward.1 = (bf16[2048,1024]{1,0:T(8,128)(2,1)}, bf16[1024,3072]{1,0:T(8,128)(2,1)}, bf16[1024,3072]{1,0:T(8,128)(2,1)}, bf16[3072,1024]{1,0:T(8,128)(2,1...) custom-call(bf16[80,512]{1,0:T(8,128)(2,1)} %pad_maximum_fusion.1.re, ...), custom_call_target="tpu_custom_call" | custom-call | tf_op jit(solution)/shard_map/layer_forward/pallas_call | solution.py:440
  91.9 31.0 %mlp.1 = (bf16[192,1024]{1,0:T(8,128)(2,1)}, f32[192,1024]{1,0:T(8,128)}, bf16[192,2048]{1,0:T(8,128)(2,1)}, f32[16,512]{1,0:T(8,128)}, bf16[1024,3072]{1,0:T(8,...) custom-call(bf16[192,1024]{1,0:T(8,128)(2,1)} %bitcast.45, ...), custom_call_target="tpu_custom_call" | custom-call | tf_op jit(solution)/shard_map/mlp/pallas_call | solution.py:1053
  122.9 118.6 %layer_backward.1 = (bf16[64,3072]{1,0:T(8,128)(2,1)}, bf16[64,3072]{1,0:T(8,128)(2,1)}, bf16[192,1024]{1,0:T(8,128)(2,1)}, bf16[128,1024]{1,0:T(8,128)(2,1)}, b...) custom-call(bf16[2,4,2,64,3072]{4,3,2,1,0:T(8,128)(2,1)} %bitcast.41, bf16[2,4,2,64,3072]{4,3,2,1,0:T(8,128)(2,1)} %bitcast.42, ...), custom_call_target="tpu_custom_call" | custom-call | tf_op jit(solution)/shard_map/layer_backward/pallas_call | solution.py:990
  241.6 1.4 convert_element_type.31
  243.1 0.8 copy.32
  243.9 0.7 copy.40
  244.7 0.7 copy.41
  245.4 0.6 dynamic_slice.28
  246.0 0.6 dynamic_slice.29
  246.6 0.6 fusion.5
  247.2 0.6 fusion.6
  247.8 0.7 slice_bitcast_fusion.5
  248.5 0.2 fusion
  248.8 1.1 fusion.3
  249.9 0.9 convert_element_type.33
  250.8 0.9 convert_element_type.34
  251.7 1.0 convert_element_type.35
  252.7 0.8 convert_element_type.32
  (33 shorter events, 0.2 us)
Async XLA Ops:
  0.6 3.5 %copy-start = (bf16[64,2048]{1,0:T(8,128)(2,1)S(1)}, bf16[64,2048]{1,0:T(8,128)(2,1)}, u32[]{:S(2)}) copy-start(bf16[64,2048]{1,0:T(8,128)(2,1)} %param.18) | copy-start | bytes 786436
  241.6 6.9 %copy-start.2 = (bf16[1,192,1024]{2,1,0:T(8,128)(2,1)S(1)}, bf16[1,192,1024]{2,1,0:T(8,128)(2,1)}, u32[]{:S(2)}) copy-start(bf16[1,192,1024]{2,1,0:T(8,128)(2,1)} %param.16) | copy-start | bytes 1179652
  241.6 6.9 %copy-start.3 = (f32[192,1024]{1,0:T(8,128)S(1)}, f32[192,1024]{1,0:T(8,128)}, u32[]{:S(2)}) copy-start(f32[192,1024]{1,0:T(8,128)} %get-tuple-element.69) | copy-start | bytes 2359300
  241.6 7.2 %copy-start.4 = (f32[192,1024]{1,0:T(8,128)S(1)}, f32[192,1024]{1,0:T(8,128)}, u32[]{:S(2)}) copy-start(f32[192,1024]{1,0:T(8,128)} %get-tuple-element.51) | copy-start | bytes 2359300
  243.0 6.9 %copy-start.7 = (bf16[64,3072]{1,0:T(8,128)(2,1)S(1)}, bf16[64,3072]{1,0:T(8,128)(2,1)}, u32[]{:S(2)}) copy-start(bf16[64,3072]{1,0:T(8,128)(2,1)} %get-tuple-element.72) | copy-start | bytes 1179652
  243.0 7.8 %copy-start.6 = (bf16[64,3072]{1,0:T(8,128)(2,1)S(1)}, bf16[64,3072]{1,0:T(8,128)(2,1)}, u32[]{:S(2)}) copy-start(bf16[64,3072]{1,0:T(8,128)(2,1)} %get-tuple-element.73) | copy-start | bytes 1179652
  243.9 7.8 %copy-start.5 = (bf16[192,1024]{1,0:T(8,128)(2,1)S(1)}, bf16[192,1024]{1,0:T(8,128)(2,1)}, u32[]{:S(2)}) copy-start(bf16[192,1024]{1,0:T(8,128)(2,1)} %get-tuple-element.74) | copy-start | bytes 1179652
  245.4 8.2 %copy-start.1 = (bf16[64,2048]{1,0:T(8,128)(2,1)S(1)}, bf16[64,2048]{1,0:T(8,128)(2,1)}, u32[]{:S(2)}) copy-start(bf16[64,2048]{1,0:T(8,128)(2,1)} %param.18) | copy-start | bytes 786436
  246.6 6.1 %copy-start.8 = (bf16[128,1024]{1,0:T(8,128)(2,1)S(1)}, bf16[128,1024]{1,0:T(8,128)(2,1)}, u32[]{:S(2)}) copy-start(bf16[128,1024]{1,0:T(8,128)(2,1)} %get-tuple-element.71) | copy-start | bytes 786436

commit v4 on v3

--- a/solution.py
+++ b/solution.py
@@ -993,7 +993,7 @@
         scratch_shapes=[pltpu.VMEM(s, d) for s, d in scratch] + sum_scratch(PLAN, [s.shape for s in srcs]) + sems(wires, local),
         **talking(1, "layer_backward"))(*srcs, x, d_heads, mlp_rows, *kept)
     return res[:ng], res[ng], res[ng + 1]
-CHUNK = 384
+CHUNK = 512
 
 
 def mlp_kernel(steps, x, heads, g, gains, wo, wg, wu, wd, out, d_hidden, d_heads, rows_out, dg, du, dd, do, hidden, mixed, mixed_t, acc, d_mixed):
@@ -1095,11 +1095,12 @@
     (gate_g, up_g, down_g, output_g), back, d_normed = backward(grads, x, d_heads, mlp_rows, kept)
     _, norm_pull = jax.vjp(lambda r: root_mean_norm(r, gains[0:2].reshape(width)), residual)
     input_grad = d_hidden + norm_pull(d_normed)[0]
-    back = back.astype(F32)
-    query_g = jnp.moveaxis(back[:, :depth, :2 * HEAD], 0, 1).reshape(depth, -1)
-    key_g = jnp.moveaxis(back[:, :depth, 2 * HEAD:3 * HEAD], 0, 1).reshape(depth, -1)
-    value_g = jnp.moveaxis(back[:, :depth, 3 * HEAD:], 0, 1).reshape(depth, -1)
-    small_g = jnp.sum(back[:, depth:, :], axis=0)
+
+    def side_by_side(lo, hi):
+        return jnp.concatenate([back[i, :depth, lo:hi] for i in range(8)], axis=1).astype(F32)
+
+    query_g, key_g, value_g = side_by_side(0, 2 * HEAD), side_by_side(2 * HEAD, 3 * HEAD), side_by_side(3 * HEAD, 4 * HEAD)
+    small_g = jnp.sum(back[:, depth:, :].astype(F32), axis=0)
 
     def mine(values, size):
         return lax.dynamic_slice_in_dim(values, f * size, size)

time: 254 us -> 267 us (1.051)
  local copies, waits for them, and re-layouts: 7.49 us -> 17.3 us
  other arithmetic: 11.1 us -> 15.4 us
    unnamed x29 -> x37, local copies, waits for them, and re-layouts: 1.37 us -> 11.9 us
where the time goes in v4:
time: 267 us; the launch traced here: 266 us
  Pallas kernels  232 us (87%)
  local copies, waits for them, and re-layouts  17.3 us (6%)
  other arithmetic  15.4 us (6%)
    pallas_call x1, Pallas kernels, backward(): pl.pallas_call(functools.partial(backward_kernel, ng), out_shape=out, in_...  119 us
    pallas_call x1, Pallas kernels, forward(): pl.pallas_call(functools.partial(forward_kernel, nw), out_shape=outs, in_...  84.5 us
    pallas_call x1, Pallas kernels, mlp(): pl.pallas_call(functools.partial(mlp_kernel, steps), out_shape=out, grid=...  29.3 us
    unnamed x37, local copies, waits for them, and re-layouts  11.9 us

profile of v4, /device:TPU:1, one launch (start us, length us, event | category | flops | bytes accessed | tf_op | source)
XLA Modules:
  0.0 265.9 jit_solution(14838026831516743648)
XLA Ops:
  0.7 0.8 broadcast_select_fusion.2
  1.7 0.7 broadcast_select_fusion
  3.4 0.7 constant_dynamic-slice_fusion.2
  5.6 1.8 pad_maximum_fusion.refs_5_
  7.4 84.5 %layer_forward.1 = (bf16[2048,1024]{1,0:T(8,128)(2,1)}, bf16[1024,3072]{1,0:T(8,128)(2,1)}, bf16[1024,3072]{1,0:T(8,128)(2,1)}, bf16[3072,1024]{1,0:T(8,128)(2,1...) custom-call(bf16[80,512]{1,0:T(8,128)(2,1)} %pad_maximum_fusion.1.re, ...), custom_call_target="tpu_custom_call" | custom-call | tf_op jit(solution)/shard_map/layer_forward/pallas_call | solution.py:440
  91.9 29.3 %mlp.1 = (bf16[192,1024]{1,0:T(8,128)(2,1)}, f32[192,1024]{1,0:T(8,128)}, bf16[192,2048]{1,0:T(8,128)(2,1)}, f32[16,512]{1,0:T(8,128)}, bf16[1024,3072]{1,0:T(8,...) custom-call(bf16[192,1024]{1,0:T(8,128)(2,1)} %bitcast.77, ...), custom_call_target="tpu_custom_call" | custom-call | tf_op jit(solution)/shard_map/mlp/pallas_call | solution.py:1053
  121.2 118.6 %layer_backward.1 = (bf16[64,3072]{1,0:T(8,128)(2,1)}, bf16[64,3072]{1,0:T(8,128)(2,1)}, bf16[192,1024]{1,0:T(8,128)(2,1)}, bf16[128,1024]{1,0:T(8,128)(2,1)}, b...) custom-call(bf16[2,4,2,64,3072]{4,3,2,1,0:T(8,128)(2,1)} %bitcast.73, bf16[2,4,2,64,3072]{4,3,2,1,0:T(8,128)(2,1)} %bitcast.74, ...), custom_call_target="tpu_custom_call" | custom-call | tf_op jit(solution)/shard_map/layer_backward/pallas_call | solution.py:990
  239.9 0.8 constant_dynamic-update-slice_fusion.24
  240.8 0.7 constant_dynamic-update-slice_fusion.23
  241.5 0.7 constant_dynamic-update-slice_fusion.22
  242.3 0.7 constant_dynamic-update-slice_fusion.21
  243.0 0.7 constant_dynamic-update-slice_fusion.20
  243.8 0.7 constant_dynamic-update-slice_fusion.19
  244.5 0.7 constant_dynamic-update-slice_fusion.18
  245.3 0.7 constant_dynamic-update-slice_fusion.17
  246.0 0.7 convert_element_type.41
  247.4 0.8 constant_dynamic-update-slice_fusion.8
  248.2 0.8 constant_dynamic-update-slice_fusion.7
  249.0 0.8 constant_dynamic-update-slice_fusion.6
  249.7 0.8 constant_dynamic-update-slice_fusion.5
  250.5 0.8 constant_dynamic-update-slice_fusion.4
  251.2 0.8 constant_dynamic-update-slice_fusion.3
  252.0 0.8 constant_dynamic-update-slice_fusion.2
  252.8 0.8 constant_dynamic-update-slice_fusion.1
  253.5 0.8 convert_element_type.40
  255.1 1.4 fusion
  256.5 2.5 fusion.3
  259.0 0.9 convert_element_type.44
  259.9 0.9 convert_element_type.45
  260.8 1.0 convert_element_type.46
  261.8 0.8 convert_element_type.43
  262.6 0.9 convert_reduce_fusion
  (42 shorter events, 6.5 us)
Async XLA Ops:
  0.6 3.5 %copy-start = (bf16[64,2048]{1,0:T(8,128)(2,1)S(1)}, bf16[64,2048]{1,0:T(8,128)(2,1)}, u32[]{:S(2)}) copy-start(bf16[64,2048]{1,0:T(8,128)(2,1)} %param.18) | copy-start | bytes 786436
  121.2 133.9 %copy-start.2 = (bf16[1,192,1024]{2,1,0:T(8,128)(2,1)S(1)}, bf16[1,192,1024]{2,1,0:T(8,128)(2,1)}, u32[]{:S(2)}) copy-start(bf16[1,192,1024]{2,1,0:T(8,128)(2,1)} %param.16) | copy-start | bytes 1179652
  121.2 144.7 %copy-start.1 = (bf16[64,2048]{1,0:T(8,128)(2,1)S(1)}, bf16[64,2048]{1,0:T(8,128)(2,1)}, u32[]{:S(2)}) copy-start(bf16[64,2048]{1,0:T(8,128)(2,1)} %param.18) | copy-start | bytes 786436
  239.9 19.1 %copy-start.5 = (bf16[64,3072]{1,0:T(8,128)(2,1)S(1)}, bf16[64,3072]{1,0:T(8,128)(2,1)}, u32[]{:S(2)}) copy-start(bf16[64,3072]{1,0:T(8,128)(2,1)} %get-tuple-element.72) | copy-start | bytes 1179652
  239.9 20.0 %copy-start.4 = (bf16[64,3072]{1,0:T(8,128)(2,1)S(1)}, bf16[64,3072]{1,0:T(8,128)(2,1)}, u32[]{:S(2)}) copy-start(bf16[64,3072]{1,0:T(8,128)(2,1)} %get-tuple-element.73) | copy-start | bytes 1179652
  239.9 20.9 %copy-start.3 = (bf16[192,1024]{1,0:T(8,128)(2,1)S(1)}, bf16[192,1024]{1,0:T(8,128)(2,1)}, u32[]{:S(2)}) copy-start(bf16[192,1024]{1,0:T(8,128)(2,1)} %get-tuple-element.74) | copy-start | bytes 1179652
  239.9 21.9 %copy-start.6 = (bf16[128,1024]{1,0:T(8,128)(2,1)S(1)}, bf16[128,1024]{1,0:T(8,128)(2,1)}, u32[]{:S(2)}) copy-start(bf16[128,1024]{1,0:T(8,128)(2,1)} %get-tuple-element.71) | copy-start | bytes 786436

commit v5 on v3

--- a/solution.py
+++ b/solution.py
@@ -993,7 +993,7 @@
         scratch_shapes=[pltpu.VMEM(s, d) for s, d in scratch] + sum_scratch(PLAN, [s.shape for s in srcs]) + sems(wires, local),
         **talking(1, "layer_backward"))(*srcs, x, d_heads, mlp_rows, *kept)
     return res[:ng], res[ng], res[ng + 1]
-CHUNK = 384
+CHUNK = 512
 
 
 def mlp_kernel(steps, x, heads, g, gains, wo, wg, wu, wd, out, d_hidden, d_heads, rows_out, dg, du, dd, do, hidden, mixed, mixed_t, acc, d_mixed):

time: 254 us -> 252 us (level)
  no operation moved by 1% of the time
where the time goes in v5:
time: 252 us
  Pallas kernels  232 us (92%)
  other arithmetic  11.1 us (4%)
  local copies, waits for them, and re-layouts  7.49 us (3%)
    pallas_call x1, Pallas kernels, backward(): pl.pallas_call(functools.partial(backward_kernel, ng), out_shape=out, in_...  119 us
    pallas_call x1, Pallas kernels, forward(): pl.pallas_call(functools.partial(forward_kernel, nw), out_shape=outs, in_...  84.5 us
    pallas_call x1, Pallas kernels, mlp(): pl.pallas_call(functools.partial(mlp_kernel, steps), out_shape=out, grid=...  29.3 us

profile of v5, /device:TPU:1, one launch (start us, length us, event | category | flops | bytes accessed | tf_op | source)
XLA Modules:
  0.0 251.8 jit_solution(5972492666761660324)
XLA Ops:
  0.7 0.8 broadcast_select_fusion.2
  1.5 0.1 select_n.48
  1.6 0.1 select_n.50
  1.7 0.7 broadcast_select_fusion
  2.4 0.1 select_n.52
  2.5 0.2 dynamic-update-slice.2
  2.7 0.1 select_n.54
  2.8 0.2 dynamic-update-slice.3
  3.1 0.3 dynamic-update-slice.4
  3.4 0.7 constant_dynamic-slice_fusion.2
  4.2 0.6 pad_maximum_fusion.1.refs_0_
  4.8 0.7 convert_reduce_fusion
  5.5 0.1 broadcast_in_dim.94
  5.6 1.8 pad_maximum_fusion.refs_5_
  7.4 84.5 %layer_forward.1 = (bf16[2048,1024]{1,0:T(8,128)(2,1)}, bf16[1024,3072]{1,0:T(8,128)(2,1)}, bf16[1024,3072]{1,0:T(8,128)(2,1)}, bf16[3072,1024]{1,0:T(8,128)(2,1...) custom-call(bf16[80,512]{1,0:T(8,128)(2,1)} %pad_maximum_fusion.1.re, ...), custom_call_target="tpu_custom_call" | custom-call | tf_op jit(solution)/shard_map/layer_forward/pallas_call | solution.py:440
  91.9 29.3 %mlp.1 = (bf16[192,1024]{1,0:T(8,128)(2,1)}, f32[192,1024]{1,0:T(8,128)}, bf16[192,2048]{1,0:T(8,128)(2,1)}, f32[16,512]{1,0:T(8,128)}, bf16[1024,3072]{1,0:T(8,...) custom-call(bf16[192,1024]{1,0:T(8,128)(2,1)} %bitcast.45, ...), custom_call_target="tpu_custom_call" | custom-call | tf_op jit(solution)/shard_map/mlp/pallas_call | solution.py:1053
  121.2 118.6 %layer_backward.1 = (bf16[64,3072]{1,0:T(8,128)(2,1)}, bf16[64,3072]{1,0:T(8,128)(2,1)}, bf16[192,1024]{1,0:T(8,128)(2,1)}, bf16[128,1024]{1,0:T(8,128)(2,1)}, b...) custom-call(bf16[2,4,2,64,3072]{4,3,2,1,0:T(8,128)(2,1)} %bitcast.41, bf16[2,4,2,64,3072]{4,3,2,1,0:T(8,128)(2,1)} %bitcast.42, ...), custom_call_target="tpu_custom_call" | custom-call | tf_op jit(solution)/shard_map/layer_backward/pallas_call | solution.py:990
  239.9 1.4 convert_element_type.31
  241.3 0.8 copy.32
  242.2 0.7 copy.40
  242.9 0.7 copy.41
  243.7 0.6 dynamic_slice.28
  244.3 0.6 dynamic_slice.29
  244.9 0.6 fusion.5
  245.5 0.6 fusion.6
  246.0 0.7 slice_bitcast_fusion.5
  246.8 0.2 fusion
  247.0 1.1 fusion.3
  248.1 0.9 convert_element_type.33
  249.1 0.9 convert_element_type.34
  250.0 1.0 convert_element_type.35
  251.0 0.8 convert_element_type.32
  (33 shorter events, 0.2 us)
Async XLA Ops:
  0.6 3.5 %copy-start = (bf16[64,2048]{1,0:T(8,128)(2,1)S(1)}, bf16[64,2048]{1,0:T(8,128)(2,1)}, u32[]{:S(2)}) copy-start(bf16[64,2048]{1,0:T(8,128)(2,1)} %param.18) | copy-start | bytes 786436
  239.8 6.9 %copy-start.2 = (bf16[1,192,1024]{2,1,0:T(8,128)(2,1)S(1)}, bf16[1,192,1024]{2,1,0:T(8,128)(2,1)}, u32[]{:S(2)}) copy-start(bf16[1,192,1024]{2,1,0:T(8,128)(2,1)} %param.16) | copy-start | bytes 1179652
  239.8 6.9 %copy-start.3 = (f32[192,1024]{1,0:T(8,128)S(1)}, f32[192,1024]{1,0:T(8,128)}, u32[]{:S(2)}) copy-start(f32[192,1024]{1,0:T(8,128)} %get-tuple-element.69) | copy-start | bytes 2359300
  239.9 7.2 %copy-start.4 = (f32[192,1024]{1,0:T(8,128)S(1)}, f32[192,1024]{1,0:T(8,128)}, u32[]{:S(2)}) copy-start(f32[192,1024]{1,0:T(8,128)} %get-tuple-element.51) | copy-start | bytes 2359300
  241.3 6.9 %copy-start.7 = (bf16[64,3072]{1,0:T(8,128)(2,1)S(1)}, bf16[64,3072]{1,0:T(8,128)(2,1)}, u32[]{:S(2)}) copy-start(bf16[64,3072]{1,0:T(8,128)(2,1)} %get-tuple-element.72) | copy-start | bytes 1179652
  241.3 7.8 %copy-start.6 = (bf16[64,3072]{1,0:T(8,128)(2,1)S(1)}, bf16[64,3072]{1,0:T(8,128)(2,1)}, u32[]{:S(2)}) copy-start(bf16[64,3072]{1,0:T(8,128)(2,1)} %get-tuple-element.73) | copy-start | bytes 1179652
  242.2 7.8 %copy-start.5 = (bf16[192,1024]{1,0:T(8,128)(2,1)S(1)}, bf16[192,1024]{1,0:T(8,128)(2,1)}, u32[]{:S(2)}) copy-start(bf16[192,1024]{1,0:T(8,128)(2,1)} %get-tuple-element.74) | copy-start | bytes 1179652
  243.6 8.2 %copy-start.1 = (bf16[64,2048]{1,0:T(8,128)(2,1)S(1)}, bf16[64,2048]{1,0:T(8,128)(2,1)}, u32[]{:S(2)}) copy-start(bf16[64,2048]{1,0:T(8,128)(2,1)} %param.18) | copy-start | bytes 786436
  244.9 6.1 %copy-start.8 = (bf16[128,1024]{1,0:T(8,128)(2,1)S(1)}, bf16[128,1024]{1,0:T(8,128)(2,1)}, u32[]{:S(2)}) copy-start(bf16[128,1024]{1,0:T(8,128)(2,1)} %get-tuple-element.71) | copy-start | bytes 786436
